TPU v7x, 256 devices: a whole 4x4x8 slice. The times are simulated.
256 devices in a mesh: layer: 2 (over core), cam: 32 (over z, x), pair: 4 (over y).
Axes of the slice: x: 4, y: 4, z: 8, core: 2. Of those that a mesh axis runs over, the one named last changes fastest.
Arguments:
- jac_blocks: bfloat16 [8192, 4, 27, 128], P(('layer', 'cam', 'pair')), may hold values from -0.071777344 to 0.071777344
- point_blocks: bfloat16 [8192, 6, 128], P(('layer', 'cam', 'pair')), may hold values from -3.6 to 8, as said below
- visibility: int32 [8192, 4, 128], P(('layer', 'cam', 'pair')), may hold values from 0 to 47, as said below
- obs_count: int32 [8192, 128], P(('layer', 'cam', 'pair')), may hold values from 2 to 4
- tile_count: int32 [8192], P(('layer', 'cam', 'pair')), may hold values from 64 to 128
- route: int32 [8192, 1], P(('layer', 'cam', 'pair')), may hold values from 0 to 31; in each aligned block of 32 rows (0 to 31, 32 to 63, ...) at most 2 rows name the same one
- camera_blocks: float32 [32, 9, 9, 48], P('cam'), may hold values from -6 to 6
Outputs:
- schur: float32 [32, 432, 432], P('cam', ('layer', 'pair'))
Inputs may be any that keep to these rules, and one draw needn't show every extreme that they name: `visibility`: the 4 cameras of one point's list are distinct. `route`: of the 32 tiles of one device at most 2 name one camera group, and some device sends exactly 2 tiles to some group. `point_blocks`: each block is symmetric and diagonally dominant: every off-diagonal entry is at most 0.45 times the root of the product of its two diagonal entries, which lie in 1 to 8.
All inputs are finite; a program needn't handle non-finite values.
Results may differ from a plain program's by a relative error of at most 0.0003.
Values may be sent and summed in bfloat16 or wider, within the bound.
No kernel may reach another device: no remote copies, remote signals or barrier semaphores. Data moves between devices by JAX's collectives and lax.ppermute only.
A program may use at most 64 MiB of HBM per device.

v0:
```python
import math

import jax
import jax.numpy as jnp
from jax import lax
from jax.sharding import PartitionSpec as P


def point_inverse(blocks):
    values = blocks.astype(jnp.float32)
    entry_xx = values[..., 0, :]
    entry_yy = values[..., 1, :]
    entry_zz = values[..., 2, :]
    entry_xy = values[..., 3, :]
    entry_xz = values[..., 4, :]
    entry_yz = values[..., 5, :]
    cofac_xx = entry_yy * entry_zz - entry_yz * entry_yz
    cofac_yy = entry_xx * entry_zz - entry_xz * entry_xz
    cofac_zz = entry_xx * entry_yy - entry_xy * entry_xy
    cofac_xy = entry_xz * entry_yz - entry_xy * entry_zz
    cofac_xz = entry_xy * entry_yz - entry_xz * entry_yy
    cofac_yz = entry_xy * entry_xz - entry_xx * entry_yz
    determinant = entry_xx * cofac_xx + entry_xy * cofac_xy + entry_xz * cofac_xz
    inv_det = 1.0 / determinant
    return (
        (cofac_xx * inv_det, cofac_xy * inv_det, cofac_xz * inv_det),
        (cofac_xy * inv_det, cofac_yy * inv_det, cofac_yz * inv_det),
        (cofac_xz * inv_det, cofac_yz * inv_det, cofac_zz * inv_det),
    )


def reduce_blocks(jacobian, blocks):
    inverse = point_inverse(blocks)
    lead_shape = jacobian.shape[:-2]
    tile_width = jacobian.shape[-1]
    factors = jacobian.astype(jnp.float32).reshape(lead_shape + (9, 3, tile_width))
    columns = []
    for out_col in range(3):
        running = factors[..., :, 0, :] * inverse[0][out_col][..., None, None, :]
        for in_row in range(1, 3):
            running = (
                running + factors[..., :, in_row, :] * inverse[in_row][out_col][..., None, None, :]
            )
        columns.append(running)
    stacked = jnp.stack(columns, axis=-2)
    return stacked.reshape(lead_shape + (27, tile_width)).astype(jnp.bfloat16)


def spread(factors, marks, camera_ids):
    batch_tiles, slot_total, _, _, tile_width = factors.shape
    one_hot = (marks[:, :, None, :] == camera_ids[None, None, :, None]).astype(jnp.float32)
    running = (
        factors[:, 0].astype(jnp.float32)[:, :, None, :, :] * one_hot[:, 0][:, None, :, None, :]
    )
    for slot_index in range(1, slot_total):
        running = (
            running
            + factors[:, slot_index].astype(jnp.float32)[:, :, None, :, :]
            * one_hot[:, slot_index][:, None, :, None, :]
        )
    cameras = camera_ids.shape[0]
    arranged = running.astype(jnp.bfloat16).transpose(1, 2, 0, 3, 4)
    return arranged.reshape(9 * cameras, batch_tiles * 3 * tile_width)


def local(jac_blocks, point_blocks, visibility, obs_count, tile_count, route, camera_blocks):
    tile_total = jac_blocks.shape[0]
    slot_total = jac_blocks.shape[1]
    tile_width = jac_blocks.shape[3]
    groups = lax.axis_size("cam")
    capacity = 2 * tile_total // groups
    cameras = camera_blocks.shape[3]
    slot_iota = lax.broadcasted_iota(jnp.int32, (tile_total, slot_total, tile_width), 1)
    point_iota = lax.broadcasted_iota(jnp.int32, (tile_total, slot_total, tile_width), 2)
    is_live = (slot_iota < obs_count[:, None, :]) & (point_iota < tile_count[:, None, None])
    marked = jnp.where(is_live, visibility, -1)
    target = route[:, 0]
    choose = (target[:, None] == jnp.arange(groups, dtype=jnp.int32)[None, :]).astype(jnp.int32)
    before = jnp.cumsum(choose, axis=0) - choose
    position = target * capacity + jnp.sum(before * choose, axis=1)
    slot_match = position[None, :] == jnp.arange(groups * capacity, dtype=jnp.int32)[:, None]
    source = jnp.sum(
        jnp.where(slot_match, jnp.arange(tile_total, dtype=jnp.int32)[None, :], 0), axis=1
    )
    filled = jnp.any(slot_match, axis=1)

    def arrange(values):
        return jnp.take(values, source, axis=0).reshape((groups, capacity) + values.shape[1:])

    send_marks = jnp.where(filled[:, None, None], jnp.take(marked, source, axis=0), -1)
    send_marks = send_marks.reshape((groups, capacity, slot_total, tile_width))
    reduced = reduce_blocks(jac_blocks, point_blocks)
    got_reduced, got_jac, got_marks = (
        lax.all_to_all(arrange(reduced), "cam", split_axis=0, concat_axis=0, tiled=True),
        lax.all_to_all(arrange(jac_blocks), "cam", split_axis=0, concat_axis=0, tiled=True),
        lax.all_to_all(send_marks, "cam", split_axis=0, concat_axis=0, tiled=True),
    )
    received = groups * capacity
    flat_reduced = got_reduced.reshape((received, slot_total, 9, 3, tile_width))
    flat_jac = got_jac.reshape((received, slot_total, 9, 3, tile_width))
    flat_marks = got_marks.reshape((received, slot_total, tile_width))
    batch_tiles = math.gcd(received, max(1, 512 // tile_width))
    turn_count = received // batch_tiles
    camera_ids = jnp.arange(cameras, dtype=jnp.int32)

    def add_block(step_index, running):
        first_row = step_index * batch_tiles
        marks_part = lax.dynamic_slice_in_dim(flat_marks, first_row, batch_tiles, 0)
        left_side = spread(
            lax.dynamic_slice_in_dim(flat_reduced, first_row, batch_tiles, 0),
            marks_part,
            camera_ids,
        )
        right_side = spread(
            lax.dynamic_slice_in_dim(flat_jac, first_row, batch_tiles, 0), marks_part, camera_ids
        )
        return running + lax.dot_general(
            left_side, right_side, (((1,), (1,)), ((), ())), preferred_element_type=jnp.float32
        )

    partial_value = lax.fori_loop(
        0, turn_count, add_block, jnp.zeros((9 * cameras, 9 * cameras), jnp.float32)
    )
    halves = lax.psum_scatter(partial_value, "layer", scatter_dimension=0, tiled=True)
    shares = lax.psum_scatter(halves, "pair", scatter_dimension=0, tiled=True)
    share_rows = shares.shape[0]
    offset = (lax.axis_index("layer") * lax.axis_size("pair") + lax.axis_index("pair")) * share_rows
    unit_matrix = jnp.eye(cameras, dtype=jnp.float32)
    dense_hessian = (
        camera_blocks[0].transpose(0, 2, 1)[:, :, :, None] * unit_matrix[None, :, None, :]
    )
    dense_hessian = dense_hessian.reshape(9 * cameras, 9 * cameras)
    own_rows = lax.dynamic_slice_in_dim(dense_hessian, offset, share_rows, 0)
    return (own_rows - shares)[None]


def solution(mesh):
    placed = (
        P(("layer", "cam", "pair"), None, None, None),
        P(("layer", "cam", "pair"), None, None),
        P(("layer", "cam", "pair"), None, None),
        P(("layer", "cam", "pair"), None),
        P(("layer", "cam", "pair")),
        P(("layer", "cam", "pair"), None),
        P("cam", None, None, None),
    )
    return jax.shard_map(
        local,
        mesh=mesh,
        in_specs=placed,
        out_specs=P("cam", ("layer", "pair"), None),
        check_vma=False,
    )
```

profile of v0, /device:TPU:1, one launch (start us, length us, event | category | flops | bytes accessed | tf_op | source)
XLA Modules:
  0.0 423.0 jit_solution(1516540068311033685)
XLA Ops:
  11.8 12.0 %all-to-all-start.1 = ((s32[32,2,4,128]{3,1,2,0:T(2,128)}), s32[32,2,4,128]{3,1,2,0:T(2,128)}, u32[]{:S(2)}, u32[]{:S(2)}) async-start(s32[32,2,4,128]{3,1,2,0:T(2,128)} %copy.59), calls=%async_computation.1 | async-start | bytes 262144 | tf_op jit(solution)/shard_map/all_to_all | solution.py:96
  34.3 4.4 %broadcast_select_fusion = (bf16[64,4,27,128]{3,1,2,0:T(4,128)(2,1)}, bf16[64,4,27,128]{3,1,2,0:T(4,128)(2,1)S(1)}) fusion(bf16[64,4,27,128]{3,1,2,0:T(4,128)(2,1)S(1)} %gather_fusion.2, pred[64]{0:T(512)(128)(4,1)S(1)} %compare_and_fusion.1, bf16[64,4,27,128]{3,1,2,0:T(4,128)(2,1)} %gather_fusion.1), kind=kLoop, calls=%fused_computation.39 | loop fusion | flops 1769472 | bytes 7077952 | tf_op jit(solution)/shard_map/jit(_take)/select_n | solution.py:88
  41.3 9.3 %all-to-all-start = ((bf16[32,2,4,27,128]{4,1,3,2,0:T(2,128)(2,1)}), bf16[32,2,4,27,128]{4,1,3,2,0:T(2,128)(2,1)S(1)}, u32[]{:S(2)}, u32[]{:S(2)}) async-start(bf16[32,2,4,27,128]{4,1,3,2,0:T(2,128)(2,1)} %copy.56), calls=%async_computation | async-start | bytes 3538944 | tf_op jit(solution)/shard_map/all_to_all | solution.py:94
  53.2 38.4 %all-to-all-done = bf16[32,2,4,27,128]{4,1,3,2,0:T(2,128)(2,1)S(1)} async-done(((bf16[32,2,4,27,128]{4,1,3,2,0:T(2,128)(2,1)}), bf16[32,2,4,27,128]{4,1,3,2,0:T(2,128)(2,1)S(1)}, u32[]{:S(2)}, u32[]{:S(2)}) %all-to-all-start) | async-done | bytes 1769504 | tf_op jit(solution)/shard_map/all_to_all | solution.py:94
  91.5 6.8 %all-to-all-start.2 = ((bf16[32,2,4,27,128]{4,1,3,2,0:T(2,128)(2,1)}), bf16[32,2,4,27,128]{4,1,3,2,0:T(2,128)(2,1)S(1)}, u32[]{:S(2)}, u32[]{:S(2)}) async-start(bf16[32,2,4,27,128]{4,1,3,2,0:T(2,128)(2,1)} %copy.62), calls=%async_computation.2 | async-start | bytes 3538944 | tf_op jit(solution)/shard_map/all_to_all | solution.py:95
  103.4 34.5 %all-to-all-done.2 = bf16[32,2,4,27,128]{4,1,3,2,0:T(2,128)(2,1)S(1)} async-done(((bf16[32,2,4,27,128]{4,1,3,2,0:T(2,128)(2,1)}), bf16[32,2,4,27,128]{4,1,3,2,0:T(2,128)(2,1)S(1)}, u32[]{:S(2)}, u32[]{:S(2)}) %all-to-all-start.2) | async-done | bytes 1769504 | tf_op jit(solution)/shard_map/all_to_all | solution.py:95
  139.9 236.7 %while.14 = (s32[]{:T(128)}, f32[432,432]{1,0:T(8,128)}, bf16[64,4,9,3,128]{4,0,3,2,1:T(8,128)(2,1)}, s32[64,4,128]{2,0,1:T(8,128)}, bf16[64,4,9,3,128]{4,0,3,2,...) while((s32[]{:T(128)}, f32[432,432]{1,0:T(8,128)}, ...), condition=%wide.region_5.7_spmd.clone, body=%wide.region_4.6_spmd.clone.sunk | while | flops 584606208 | bytes 34720056 | solution.py:121
  142.3 4.4 %add_convert_fusion.6 = (bf16[9,48,4,3,128]{4,3,2,1,0:T(4,128)(2,1)S(1)}, bf16[9,48,4,3,128]{4,3,2,1,0:T(4,128)(2,1)S(1)}) fusion(f32[9,4,3,128]{3,2,1,0:T(4,128)S(1)} %convert_bitcast_fusion.16, f32[9,4,3,128]{3,2,1,0:T(4,128)S(1)} %convert_bitcast_fusion.17, f32[9,4,3,128]{3,2,1,0:T(4,128)S(1)} %convert_bitcast_fusion.18, ...), kind=kLoop, calls=%fused_computation.4.clone.1 | loop fusion | flops 10616832 | bytes 3489792 | tf_op jit(solution)/shard_map/while/body/eval_jaxpr/convert_element_type | solution.py:62
  156.9 4.4 %add_convert_fusion.6 = (bf16[9,48,4,3,128]{4,3,2,1,0:T(4,128)(2,1)S(1)}, bf16[9,48,4,3,128]{4,3,2,1,0:T(4,128)(2,1)S(1)}) fusion(f32[9,4,3,128]{3,2,1,0:T(4,128)S(1)} %convert_bitcast_fusion.16, f32[9,4,3,128]{3,2,1,0:T(4,128)S(1)} %convert_bitcast_fusion.17, f32[9,4,3,128]{3,2,1,0:T(4,128)S(1)} %convert_bitcast_fusion.18, ...), kind=kLoop, calls=%fused_computation.4.clone.1 | loop fusion | flops 10616832 | bytes 3489792 | tf_op jit(solution)/shard_map/while/body/eval_jaxpr/convert_element_type | solution.py:62
  171.7 4.4 %add_convert_fusion.6 = (bf16[9,48,4,3,128]{4,3,2,1,0:T(4,128)(2,1)S(1)}, bf16[9,48,4,3,128]{4,3,2,1,0:T(4,128)(2,1)S(1)}) fusion(f32[9,4,3,128]{3,2,1,0:T(4,128)S(1)} %convert_bitcast_fusion.16, f32[9,4,3,128]{3,2,1,0:T(4,128)S(1)} %convert_bitcast_fusion.17, f32[9,4,3,128]{3,2,1,0:T(4,128)S(1)} %convert_bitcast_fusion.18, ...), kind=kLoop, calls=%fused_computation.4.clone.1 | loop fusion | flops 10616832 | bytes 3489792 | tf_op jit(solution)/shard_map/while/body/eval_jaxpr/convert_element_type | solution.py:62
  186.5 4.4 %add_convert_fusion.6 = (bf16[9,48,4,3,128]{4,3,2,1,0:T(4,128)(2,1)S(1)}, bf16[9,48,4,3,128]{4,3,2,1,0:T(4,128)(2,1)S(1)}) fusion(f32[9,4,3,128]{3,2,1,0:T(4,128)S(1)} %convert_bitcast_fusion.16, f32[9,4,3,128]{3,2,1,0:T(4,128)S(1)} %convert_bitcast_fusion.17, f32[9,4,3,128]{3,2,1,0:T(4,128)S(1)} %convert_bitcast_fusion.18, ...), kind=kLoop, calls=%fused_computation.4.clone.1 | loop fusion | flops 10616832 | bytes 3489792 | tf_op jit(solution)/shard_map/while/body/eval_jaxpr/convert_element_type | solution.py:62
  201.3 4.4 %add_convert_fusion.6 = (bf16[9,48,4,3,128]{4,3,2,1,0:T(4,128)(2,1)S(1)}, bf16[9,48,4,3,128]{4,3,2,1,0:T(4,128)(2,1)S(1)}) fusion(f32[9,4,3,128]{3,2,1,0:T(4,128)S(1)} %convert_bitcast_fusion.16, f32[9,4,3,128]{3,2,1,0:T(4,128)S(1)} %convert_bitcast_fusion.17, f32[9,4,3,128]{3,2,1,0:T(4,128)S(1)} %convert_bitcast_fusion.18, ...), kind=kLoop, calls=%fused_computation.4.clone.1 | loop fusion | flops 10616832 | bytes 3489792 | tf_op jit(solution)/shard_map/while/body/eval_jaxpr/convert_element_type | solution.py:62
  216.1 4.4 %add_convert_fusion.6 = (bf16[9,48,4,3,128]{4,3,2,1,0:T(4,128)(2,1)S(1)}, bf16[9,48,4,3,128]{4,3,2,1,0:T(4,128)(2,1)S(1)}) fusion(f32[9,4,3,128]{3,2,1,0:T(4,128)S(1)} %convert_bitcast_fusion.16, f32[9,4,3,128]{3,2,1,0:T(4,128)S(1)} %convert_bitcast_fusion.17, f32[9,4,3,128]{3,2,1,0:T(4,128)S(1)} %convert_bitcast_fusion.18, ...), kind=kLoop, calls=%fused_computation.4.clone.1 | loop fusion | flops 10616832 | bytes 3489792 | tf_op jit(solution)/shard_map/while/body/eval_jaxpr/convert_element_type | solution.py:62
  230.9 4.4 %add_convert_fusion.6 = (bf16[9,48,4,3,128]{4,3,2,1,0:T(4,128)(2,1)S(1)}, bf16[9,48,4,3,128]{4,3,2,1,0:T(4,128)(2,1)S(1)}) fusion(f32[9,4,3,128]{3,2,1,0:T(4,128)S(1)} %convert_bitcast_fusion.16, f32[9,4,3,128]{3,2,1,0:T(4,128)S(1)} %convert_bitcast_fusion.17, f32[9,4,3,128]{3,2,1,0:T(4,128)S(1)} %convert_bitcast_fusion.18, ...), kind=kLoop, calls=%fused_computation.4.clone.1 | loop fusion | flops 10616832 | bytes 3489792 | tf_op jit(solution)/shard_map/while/body/eval_jaxpr/convert_element_type | solution.py:62
  245.7 4.4 %add_convert_fusion.6 = (bf16[9,48,4,3,128]{4,3,2,1,0:T(4,128)(2,1)S(1)}, bf16[9,48,4,3,128]{4,3,2,1,0:T(4,128)(2,1)S(1)}) fusion(f32[9,4,3,128]{3,2,1,0:T(4,128)S(1)} %convert_bitcast_fusion.16, f32[9,4,3,128]{3,2,1,0:T(4,128)S(1)} %convert_bitcast_fusion.17, f32[9,4,3,128]{3,2,1,0:T(4,128)S(1)} %convert_bitcast_fusion.18, ...), kind=kLoop, calls=%fused_computation.4.clone.1 | loop fusion | flops 10616832 | bytes 3489792 | tf_op jit(solution)/shard_map/while/body/eval_jaxpr/convert_element_type | solution.py:62
  260.5 4.4 %add_convert_fusion.6 = (bf16[9,48,4,3,128]{4,3,2,1,0:T(4,128)(2,1)S(1)}, bf16[9,48,4,3,128]{4,3,2,1,0:T(4,128)(2,1)S(1)}) fusion(f32[9,4,3,128]{3,2,1,0:T(4,128)S(1)} %convert_bitcast_fusion.16, f32[9,4,3,128]{3,2,1,0:T(4,128)S(1)} %convert_bitcast_fusion.17, f32[9,4,3,128]{3,2,1,0:T(4,128)S(1)} %convert_bitcast_fusion.18, ...), kind=kLoop, calls=%fused_computation.4.clone.1 | loop fusion | flops 10616832 | bytes 3489792 | tf_op jit(solution)/shard_map/while/body/eval_jaxpr/convert_element_type | solution.py:62
  275.3 4.4 %add_convert_fusion.6 = (bf16[9,48,4,3,128]{4,3,2,1,0:T(4,128)(2,1)S(1)}, bf16[9,48,4,3,128]{4,3,2,1,0:T(4,128)(2,1)S(1)}) fusion(f32[9,4,3,128]{3,2,1,0:T(4,128)S(1)} %convert_bitcast_fusion.16, f32[9,4,3,128]{3,2,1,0:T(4,128)S(1)} %convert_bitcast_fusion.17, f32[9,4,3,128]{3,2,1,0:T(4,128)S(1)} %convert_bitcast_fusion.18, ...), kind=kLoop, calls=%fused_computation.4.clone.1 | loop fusion | flops 10616832 | bytes 3489792 | tf_op jit(solution)/shard_map/while/body/eval_jaxpr/convert_element_type | solution.py:62
  290.1 4.4 %add_convert_fusion.6 = (bf16[9,48,4,3,128]{4,3,2,1,0:T(4,128)(2,1)S(1)}, bf16[9,48,4,3,128]{4,3,2,1,0:T(4,128)(2,1)S(1)}) fusion(f32[9,4,3,128]{3,2,1,0:T(4,128)S(1)} %convert_bitcast_fusion.16, f32[9,4,3,128]{3,2,1,0:T(4,128)S(1)} %convert_bitcast_fusion.17, f32[9,4,3,128]{3,2,1,0:T(4,128)S(1)} %convert_bitcast_fusion.18, ...), kind=kLoop, calls=%fused_computation.4.clone.1 | loop fusion | flops 10616832 | bytes 3489792 | tf_op jit(solution)/shard_map/while/body/eval_jaxpr/convert_element_type | solution.py:62
  319.7 4.4 %add_convert_fusion.6 = (bf16[9,48,4,3,128]{4,3,2,1,0:T(4,128)(2,1)S(1)}, bf16[9,48,4,3,128]{4,3,2,1,0:T(4,128)(2,1)S(1)}) fusion(f32[9,4,3,128]{3,2,1,0:T(4,128)S(1)} %convert_bitcast_fusion.16, f32[9,4,3,128]{3,2,1,0:T(4,128)S(1)} %convert_bitcast_fusion.17, f32[9,4,3,128]{3,2,1,0:T(4,128)S(1)} %convert_bitcast_fusion.18, ...), kind=kLoop, calls=%fused_computation.4.clone.1 | loop fusion | flops 10616832 | bytes 3489792 | tf_op jit(solution)/shard_map/while/body/eval_jaxpr/convert_element_type | solution.py:62
  334.5 4.4 %add_convert_fusion.6 = (bf16[9,48,4,3,128]{4,3,2,1,0:T(4,128)(2,1)S(1)}, bf16[9,48,4,3,128]{4,3,2,1,0:T(4,128)(2,1)S(1)}) fusion(f32[9,4,3,128]{3,2,1,0:T(4,128)S(1)} %convert_bitcast_fusion.16, f32[9,4,3,128]{3,2,1,0:T(4,128)S(1)} %convert_bitcast_fusion.17, f32[9,4,3,128]{3,2,1,0:T(4,128)S(1)} %convert_bitcast_fusion.18, ...), kind=kLoop, calls=%fused_computation.4.clone.1 | loop fusion | flops 10616832 | bytes 3489792 | tf_op jit(solution)/shard_map/while/body/eval_jaxpr/convert_element_type | solution.py:62
  349.3 4.4 %add_convert_fusion.6 = (bf16[9,48,4,3,128]{4,3,2,1,0:T(4,128)(2,1)S(1)}, bf16[9,48,4,3,128]{4,3,2,1,0:T(4,128)(2,1)S(1)}) fusion(f32[9,4,3,128]{3,2,1,0:T(4,128)S(1)} %convert_bitcast_fusion.16, f32[9,4,3,128]{3,2,1,0:T(4,128)S(1)} %convert_bitcast_fusion.17, f32[9,4,3,128]{3,2,1,0:T(4,128)S(1)} %convert_bitcast_fusion.18, ...), kind=kLoop, calls=%fused_computation.4.clone.1 | loop fusion | flops 10616832 | bytes 3489792 | tf_op jit(solution)/shard_map/while/body/eval_jaxpr/convert_element_type | solution.py:62
  364.1 4.4 %add_convert_fusion.6 = (bf16[9,48,4,3,128]{4,3,2,1,0:T(4,128)(2,1)S(1)}, bf16[9,48,4,3,128]{4,3,2,1,0:T(4,128)(2,1)S(1)}) fusion(f32[9,4,3,128]{3,2,1,0:T(4,128)S(1)} %convert_bitcast_fusion.16, f32[9,4,3,128]{3,2,1,0:T(4,128)S(1)} %convert_bitcast_fusion.17, f32[9,4,3,128]{3,2,1,0:T(4,128)S(1)} %convert_bitcast_fusion.18, ...), kind=kLoop, calls=%fused_computation.4.clone.1 | loop fusion | flops 10616832 | bytes 3489792 | tf_op jit(solution)/shard_map/while/body/eval_jaxpr/convert_element_type | solution.py:62
  378.9 13.7 %reduce-scatter.4.cloned.1.call-done = f32[216,432]{1,0:T(8,128)} async-done(((f32[432,432]{1,0:T(8,128)}), f32[216,432]{1,0:T(8,128)}) %reduce-scatter.4.cloned.1.call-update) | async-done | bytes 373264 | tf_op jit(solution)/shard_map/reduce_scatter | solution.py:124
  392.6 11.9 %fusion.2 = f32[56,432]{1,0:T(8,128)S(1)} fusion(f32[216,432]{1,0:T(8,128)} %reduce-scatter.4.cloned.1.call-done), kind=kCustom, calls=%all-reduce-scatter | all-reduce-scatter fusion | flops 96769 | bytes 471040
  (390 shorter events, 210.6 us)
Async XLA Ops:
  6.5 18.2 %copy-start.1 = (bf16[32,4,27,128]{3,1,2,0:T(4,128)(2,1)S(1)}, bf16[32,4,27,128]{3,1,2,0:T(4,128)(2,1)}, u32[]{:S(2)}) copy-start(bf16[32,4,27,128]{3,1,2,0:T(4,128)(2,1)} %param.11) | copy-start | bytes 2654212
  11.8 29.5 %all-to-all-start.1 = ((s32[32,2,4,128]{3,1,2,0:T(2,128)}), s32[32,2,4,128]{3,1,2,0:T(2,128)}, u32[]{:S(2)}, u32[]{:S(2)}) async-start(s32[32,2,4,128]{3,1,2,0:T(2,128)} %copy.59), calls=%async_computation.1 | async-start | bytes 262144 | tf_op jit(solution)/shard_map/all_to_all | solution.py:96
  41.3 9.3 %copy-start.2 = (bf16[64,4,27,128]{3,1,2,0:T(4,128)(2,1)S(1)}, bf16[64,4,27,128]{3,1,2,0:T(4,128)(2,1)}, u32[]{:S(2)}) copy-start(bf16[64,4,27,128]{3,1,2,0:T(4,128)(2,1)} %get-tuple-element.201) | copy-start | bytes 5308420
  41.3 50.2 %all-to-all-start = ((bf16[32,2,4,27,128]{4,1,3,2,0:T(2,128)(2,1)}), bf16[32,2,4,27,128]{4,1,3,2,0:T(2,128)(2,1)S(1)}, u32[]{:S(2)}, u32[]{:S(2)}) async-start(bf16[32,2,4,27,128]{4,1,3,2,0:T(2,128)(2,1)} %copy.56), calls=%async_computation | async-start | bytes 3538944 | tf_op jit(solution)/shard_map/all_to_all | solution.py:94
  91.5 46.4 %all-to-all-start.2 = ((bf16[32,2,4,27,128]{4,1,3,2,0:T(2,128)(2,1)}), bf16[32,2,4,27,128]{4,1,3,2,0:T(2,128)(2,1)S(1)}, u32[]{:S(2)}, u32[]{:S(2)}) async-start(bf16[32,2,4,27,128]{4,1,3,2,0:T(2,128)(2,1)} %copy.62), calls=%async_computation.2 | async-start | bytes 3538944 | tf_op jit(solution)/shard_map/all_to_all | solution.py:95
  98.3 294.3 %reduce-scatter.4.cloned.1.call-start = ((), (), s32[]{:S(2)}) async-start(), calls=%async_computation.4 | async-start | bytes 1327104 | tf_op jit(solution)/shard_map/reduce_scatter | solution.py:124
  151.3 3.3 copy-start.4
  165.9 3.5 copy-start.4
  180.7 3.5 copy-start.4
  195.5 3.5 copy-start.4
  210.3 3.5 copy-start.4
  225.1 3.5 copy-start.4
  239.9 3.5 copy-start.4
  254.7 3.5 copy-start.4
  269.5 3.5 copy-start.4
  284.3 3.5 copy-start.4
  299.1 3.5 copy-start.4
  313.9 3.5 copy-start.4
  328.7 3.5 copy-start.4
  343.5 3.5 copy-start.4
  358.3 3.5 copy-start.4
  373.1 3.5 copy-start.4
  404.5 3.4 copy-start.5
  405.2 8.3 %collective-permute-start = (f32[6,432]{1,0:T(8,128)}, f32[6,432]{1,0:T(8,128)S(1)}, u32[]{:S(2)}, u32[]{:S(2)}) collective-permute-start(f32[6,432]{1,0:T(8,128)} %slice.161), channel_id=1, source_target_pairs={{0,1},{1,2},{2,3},{4,5},{5,6},{6,7},{8,9},{9,10},{10,11},{12,13},{... | collective-permute-start | bytes 31112
  (32 other events, 73.7 us)
Sparse Core Ops, SparseCore 0:
  376.8 15.7 reduce-scatter.3
where the time goes:
time: 427 us; the launch traced here: 423 us
  local copies, waits for them, and re-layouts  132 us (31%)
  other arithmetic  89.9 us (21%)
  waiting for transfers between devices  86.7 us (20%)
  matrix products  55.7 us (13%)
  starting transfers between devices  31 us (7%)
  between operations  14.3 us (3%)
  blocking collectives  11.9 us (3%)
    convert_element_type x32, local copies, waits for them, and re-layouts, spread(): arranged = running.astype(jnp.bfloat16).transpose(1, 2, 0, 3, 4)  73.4 us
    convert_element_type x16, other arithmetic, spread(): arranged = running.astype(jnp.bfloat16).transpose(1, 2, 0, 3, 4)  69.9 us
    dot_general x16, matrix products, add_block(): lax.dot_general(left_side, right_side, (((1,), (1,)), ((), ())), preferre...  55.7 us
    all_to_all x1, waiting for transfers between devices, local(): lax.all_to_all(arrange(reduced), 'cam', split_axis=0, concat_axis=0, tile...  38.4 us
    all_to_all x1, waiting for transfers between devices, local(): lax.all_to_all(arrange(jac_blocks), 'cam', split_axis=0, concat_axis=0, t...  34.5 us
    slice x16, local copies, waits for them, and re-layouts, spread(): factors[:, 0].astype(jnp.float32)[:, :, None, :, :]  20.5 us
    reduce_scatter x1, waiting for transfers between devices, local(): lax.psum_scatter(partial_value, 'layer', scatter_dimension=0, tiled=True)  13.7 us
    all_to_all x1, starting transfers between devices, local(): lax.all_to_all(send_marks, 'cam', split_axis=0, concat_axis=0, tiled=True)  12 us
  transfers between devices with their start and end apart: 5, of which 3 were waited for; matrix products, arithmetic and copies ran while one was open for 8% of the time, Pallas kernels for 0%

commit v1 on v0

v1 whole, which is shorter than its diff:
```python
import functools

import jax
import jax.numpy as jnp
from jax import lax
from jax.experimental import pallas as pl
from jax.experimental.pallas import tpu as pltpu
from jax.sharding import PartitionSpec as P

GROUPS_OF_ROWS = 30


def pack_kernel(route_ref, count_ref, jac_ref, block_ref, vis_ref, obs_ref, out_ref, block_scratch, fill_ref):
    tiles = jac_ref.shape[0]
    groups = out_ref.shape[0]
    width = jac_ref.shape[3]
    block_scratch[...] = block_ref[...].astype(jnp.float32)
    dead = jnp.full((4, width), -1.0, jnp.bfloat16)

    def clear(group, carry):
        fill_ref[group] = 0
        out_ref[group, 0, 27] = dead
        out_ref[group, 1, 27] = dead
        return carry

    lax.fori_loop(0, groups, clear, 0, unroll=8)
    slot_iota = lax.broadcasted_iota(jnp.int32, (4, width), 0)
    point_iota = lax.broadcasted_iota(jnp.int32, (4, width), 1)

    def place(tile, carry):
        group = route_ref[tile]
        slot = fill_ref[group]
        fill_ref[group] = slot + 1
        obs = jnp.broadcast_to(obs_ref[pl.ds(tile, 1), :], (4, width))
        live = (slot_iota < obs) & (point_iota < count_ref[tile])
        marks = jnp.where(live, vis_ref[tile], -1).astype(jnp.float32).astype(jnp.bfloat16)
        rows = [block_scratch[c, pl.ds(tile, 1), :] for c in range(6)]
        zero = jnp.zeros_like(rows[0])
        out_ref[group, slot, pl.ds(0, 27)] = jac_ref[tile]
        out_ref[group, slot, 27] = marks
        out_ref[group, slot, 28] = jnp.concatenate(rows[:4], axis=0).astype(jnp.bfloat16)
        out_ref[group, slot, 29] = jnp.concatenate(rows[4:] + [zero, zero], axis=0).astype(jnp.bfloat16)
        return carry

    lax.fori_loop(0, tiles, place, 0, unroll=4)


def pack(jac, blocks, vis, obs, counts, dest, groups):
    width = jac.shape[3]
    smem = pl.BlockSpec(memory_space=pltpu.SMEM)
    vmem = pl.BlockSpec(memory_space=pltpu.VMEM)
    return pl.pallas_call(
        pack_kernel,
        out_shape=jax.ShapeDtypeStruct((groups, 2, GROUPS_OF_ROWS, 4, width), jnp.bfloat16),
        in_specs=[smem, smem, vmem, vmem, vmem, vmem],
        out_specs=vmem,
        scratch_shapes=[pltpu.VMEM(blocks.shape, jnp.float32), pltpu.SMEM((groups,), jnp.int32)],
        compiler_params=pltpu.CompilerParams(vmem_limit_bytes=24 * 1024 * 1024),
        cost_estimate=pl.CostEstimate(flops=1000000, bytes_accessed=3000000, transcendentals=0),
        name="pack",
    )(dest, counts, jac, blocks, vis, obs)


def inverse_rows(first, second):
    xx, yy, zz, xy = (first[c : c + 1] for c in range(4))
    xz, yz = (second[c : c + 1] for c in range(2))
    cxx = yy * zz - yz * yz
    cyy = xx * zz - xz * xz
    czz = xx * yy - xy * xy
    cxy = xz * yz - xy * zz
    cxz = xy * yz - xz * yy
    cyz = xy * xz - xx * yz
    inv_det = 1.0 / (xx * cxx + xy * cxy + xz * cxz)
    ixx, iyy, izz, ixy, ixz, iyz = (c * inv_det for c in (cxx, cyy, czz, cxy, cxz, cyz))
    return ((ixx, ixy, ixz), (ixy, iyy, iyz), (ixz, iyz, izz))


def expand_slot(got_ref, source, slot, rows_ref, left_ref, right_ref, column, cameras):
    width = got_ref.shape[4]
    first = got_ref[source, slot, 28].astype(jnp.float32)
    second = got_ref[source, slot, 29].astype(jnp.float32)
    inverse = inverse_rows(first, second)
    wide = [[jnp.broadcast_to(entry, (4, width)) for entry in line] for line in inverse]
    for r in range(9):
        factors = [got_ref[source, slot, 3 * r + m].astype(jnp.float32) for m in range(3)]
        for k in range(3):
            value = factors[0] * wide[0][k] + factors[1] * wide[1][k] + factors[2] * wide[2][k]
            rows_ref[3 * r + k, 0:4] = value.astype(jnp.bfloat16).astype(jnp.float32)
            rows_ref[3 * r + k, 4:8] = factors[k]
    rows_ref[27, 0:4] = got_ref[source, slot, 27].astype(jnp.float32)
    blocks = cameras // 16
    iota = lax.broadcasted_iota(jnp.int32, (16, width), 0).astype(jnp.float32)
    masks = []
    for i in range(4):
        mark = jnp.broadcast_to(rows_ref[27, i : i + 1], (16, width)).astype(jnp.bfloat16)
        masks.append([mark == (iota + 16.0 * b).astype(jnp.bfloat16) for b in range(blocks)])
    zero = jnp.zeros((16, width), jnp.bfloat16)
    for r in range(9):
        for k in range(3):
            for side, out in ((0, left_ref), (4, right_ref)):
                sums = [zero] * blocks
                for i in range(4):
                    row = jnp.broadcast_to(rows_ref[3 * r + k, side + i : side + i + 1], (16, width))
                    row = row.astype(jnp.bfloat16)
                    sums = [jnp.where(masks[i][b], row, sums[b]) for b in range(blocks)]
                for b in range(blocks):
                    out[pl.ds(r * cameras + 16 * b, 16), pl.ds(column + k * width, width)] = sums[b]


def schur_kernel(cameras, got_ref, out_ref, total, rows_ref, left_ref, right_ref):
    sources = got_ref.shape[0]
    width = got_ref.shape[4]
    total[...] = jnp.zeros_like(total)

    def expand(source, buffer):
        for slot in range(2):
            expand_slot(
                got_ref, source, slot, rows_ref.at[slot], left_ref.at[buffer], right_ref.at[buffer],
                slot * 3 * width, cameras,
            )

    def multiply(buffer):
        total[...] += lax.dot_general(
            left_ref[buffer], right_ref[buffer], (((1,), (1,)), ((), ())), preferred_element_type=jnp.float32
        )

    expand(0, 0)

    def step(turn, carry):
        expand(2 * turn + 1, 1)
        multiply(0)
        expand(jnp.minimum(2 * turn + 2, sources - 1), 0)
        multiply(1)
        return carry

    lax.fori_loop(0, sources // 2, step, 0)
    share = out_ref.shape[1]
    for part in range(out_ref.shape[0]):
        out_ref[part] = total[pl.ds(part * share, share), :]


def schur_partial(got, cameras, shares):
    width = got.shape[4]
    side = 9 * cameras
    vmem = pl.BlockSpec(memory_space=pltpu.VMEM)
    return pl.pallas_call(
        functools.partial(schur_kernel, cameras),
        out_shape=jax.ShapeDtypeStruct((shares, side // shares, side), jnp.float32),
        in_specs=[vmem],
        out_specs=vmem,
        scratch_shapes=[
            pltpu.VMEM((side, side), jnp.float32),
            pltpu.VMEM((2, 28, 8, width), jnp.float32),
            pltpu.VMEM((2, side, 6 * width), jnp.bfloat16),
            pltpu.VMEM((2, side, 6 * width), jnp.bfloat16),
        ],
        compiler_params=pltpu.CompilerParams(vmem_limit_bytes=32 * 1024 * 1024),
        cost_estimate=pl.CostEstimate(flops=10000000000, bytes_accessed=3000000, transcendentals=0),
        name="schur_partial",
    )(got)


def local(jac_blocks, point_blocks, visibility, obs_count, tile_count, route, camera_blocks):
    groups = lax.axis_size("cam")
    cameras = camera_blocks.shape[3]
    side = 9 * cameras
    shares = lax.axis_size("layer") * lax.axis_size("pair")
    packed = pack(
        jac_blocks.transpose(0, 2, 1, 3), point_blocks.transpose(1, 0, 2), visibility, obs_count, tile_count,
        route[:, 0], groups,
    )
    got = lax.all_to_all(packed, "cam", split_axis=0, concat_axis=0, tiled=True)
    partial_value = schur_partial(got, cameras, shares)
    pieces = lax.all_to_all(partial_value, ("layer", "pair"), split_axis=0, concat_axis=0, tiled=True)
    share = lax.axis_index("layer") * lax.axis_size("pair") + lax.axis_index("pair")
    share_rows = side // shares
    row = share * share_rows + lax.broadcasted_iota(jnp.int32, (share_rows, side), 0)
    column = lax.broadcasted_iota(jnp.int32, (share_rows, side), 1)
    lines = camera_blocks[0].reshape(9, side)
    first = share * share_rows // cameras
    own = jnp.zeros((share_rows, side), jnp.float32)
    for step in range(-(-share_rows // cameras) + 1):
        line = lax.dynamic_slice_in_dim(lines, jnp.minimum(first + step, 8), 1, 0)
        own = jnp.where(row // cameras == first + step, line, own)
    own = jnp.where(row % cameras == column % cameras, own, 0.0)
    return (own - jnp.sum(pieces, axis=0))[None]


def solution(mesh):
    placed = (
        P(("layer", "cam", "pair"), None, None, None),
        P(("layer", "cam", "pair"), None, None),
        P(("layer", "cam", "pair"), None, None),
        P(("layer", "cam", "pair"), None),
        P(("layer", "cam", "pair")),
        P(("layer", "cam", "pair"), None),
        P("cam", None, None, None),
    )
    return jax.shard_map(
        local,
        mesh=mesh,
        in_specs=placed,
        out_specs=P("cam", ("layer", "pair"), None),
        check_vma=False,
    )
```

time: 427 us -> 113 us (0.26)
  local copies, waits for them, and re-layouts: 132 us -> 4.94 us
  other arithmetic: 89.9 us -> 1.6 us
  matrix products: 55.7 us -> 0 us
  Pallas kernels: 0 us -> 28.1 us
  waiting for transfers between devices: 86.7 us -> 59.1 us
  between operations: 14.3 us -> 0.13 us
  starting transfers between devices: 31 us -> 19 us
  blocking collectives: 11.9 us -> 0 us
    convert_element_type x32 -> x0, local copies, waits for them, and re-layouts: 73.4 us -> none  [spread(): arranged = running.astype(jnp.bfloat16).transpose(1, 2, 0, 3, 4)]
    convert_element_type x35 -> x0, other arithmetic: 73.3 us -> none  [the longest x16 69.9 us: spread(): arranged = running.astype(jnp.bfloat16).transpose(1, 2, 0, 3, 4)]
    dot_general x16 -> x0, matrix products: 55.7 us -> none  [add_block(): lax.dot_general(left_side, right_side, (((1,), (1,)), ((), ())), preferre...]
    pallas_call x0 -> x2, Pallas kernels: none -> 28.1 us  [the longest x1 26 us: schur_partial(): pl.pallas_call(functools.partial(schur_kernel, cameras), out_shape=jax.Sh...]
    slice x16 -> x0, local copies, waits for them, and re-layouts: 20.5 us -> none  [spread(): factors[:, 0].astype(jnp.float32)[:, :, None, :, :]]
    all_to_all x3 -> x2, waiting for transfers between devices: 72.9 us -> 59.1 us  [the longest x1 45.6 us: local(): got = lax.all_to_all(packed, 'cam', split_axis=0, concat_axis=0, tiled=True)]
    reduce_scatter x1 -> x0, waiting for transfers between devices: 13.7 us -> none  [local(): lax.psum_scatter(partial_value, 'layer', scatter_dimension=0, tiled=True)]
    unnamed x1 -> x0, blocking collectives: 11.9 us -> none
  transfers between devices with their start and end apart: 5 -> 2, of which waited for: 3 -> 2; matrix products, arithmetic and copies ran while one was open for 8% -> 0% of each run, Pallas kernels for 0% -> 0%
where the time goes in v1:
time: 113 us
  waiting for transfers between devices  59.1 us (52%)
  Pallas kernels  28.1 us (25%)
  starting transfers between devices  19 us (17%)
  local copies, waits for them, and re-layouts  4.94 us (4%)
  other arithmetic  1.6 us (1%)
    all_to_all x1, waiting for transfers between devices, local(): got = lax.all_to_all(packed, 'cam', split_axis=0, concat_axis=0, tiled=True)  45.6 us
    pallas_call x1, Pallas kernels, schur_partial(): pl.pallas_call(functools.partial(schur_kernel, cameras), out_shape=jax.Sh...  26 us
    all_to_all x1, waiting for transfers between devices, local(): lax.all_to_all(partial_value, ('layer', 'pair'), split_axis=0, concat_axi...  13.5 us
    all_to_all x1, starting transfers between devices, local(): got = lax.all_to_all(packed, 'cam', split_axis=0, concat_axis=0, tiled=True)  12 us
    all_to_all x1, starting transfers between devices, local(): lax.all_to_all(partial_value, ('layer', 'pair'), split_axis=0, concat_axi...  6.97 us
    unnamed x14, local copies, waits for them, and re-layouts  4.83 us
  transfers between devices with their start and end apart: 2, of which 2 were waited for; matrix products, arithmetic and copies ran while one was open for 0% of the time, Pallas kernels for 0%

profile of v1, /device:TPU:1, one launch (start us, length us, event | category | flops | bytes accessed | tf_op | source)
XLA Modules:
  0.0 112.8 jit_solution(538349752052528524)
XLA Ops:
  0.0 0.0 copy-start
  0.0 1.2 %copy-done = bf16[32,4,27,128]{3,1,2,0:T(4,128)(2,1)S(1)} copy-done((bf16[32,4,27,128]{3,1,2,0:T(4,128)(2,1)S(1)}, bf16[32,4,27,128]{3,1,2,0:T(4,128)(2,1)}, u32[]{:S(2)}) %copy-start) | copy-done | bytes 884760
  1.2 0.0 copy-start.1
  1.2 0.8 copy-done.1
  2.0 0.0 copy-start.2
  2.0 0.8 copy-done.2
  2.8 0.0 copy-start.3
  2.8 0.7 copy-done.3
  3.5 0.0 copy-start.4
  3.5 0.7 copy-done.4
  4.2 0.0 copy-start.5
  4.2 0.7 copy-done.5
  4.8 2.1 %pack.1 = bf16[32,2,30,4,128]{4,3,2,1,0:T(4,128)(2,1)} custom-call(s32[32]{0:T(128)S(1)} %bitcast.8, s32[32]{0:T(128)S(1)} %copy-done.5, bf16[32,27,4,128]{3,2,1,0:T(4,128)(2,1)S(1)} %bitcast.6, bf16[6,32,128]{2,1,0:T(8,128)(2,1)S(1)} %bitcast.7, s32[32,4,128]{2,1,0:T(4,128)S(1)} %copy-done.1, s32[32,128]{1,0:T(8,128)S(1)} %copy-done.3), custom_call_target="tpu_custom_call" | custom-call | flops 1000000 | bytes 3000000 | tf_op jit(solution)/shard_map/pack/pallas_call | solution.py:52
  6.9 0.0 copy-start.6
  7.0 12.0 %all-to-all-start = ((bf16[32,2,30,4,128]{4,3,2,1,0:T(4,128)(2,1)}), bf16[32,2,30,4,128]{4,3,2,1,0:T(4,128)(2,1)S(1)}, u32[]{:S(2)}, u32[]{:S(2)}) async-start(bf16[32,2,30,4,128]{4,3,2,1,0:T(4,128)(2,1)} %pack.1), calls=%async_computation | async-start | bytes 3932160 | tf_op jit(solution)/shard_map/all_to_all | solution.py:172
  19.0 0.0 copy-done.6
  19.0 0.1 reduce
  19.1 0.1 reshape_squeeze.3
  19.2 45.6 %all-to-all-done.got_ref = bf16[32,2,30,4,128]{4,3,2,1,0:T(4,128)(2,1)S(1)} async-done(((bf16[32,2,30,4,128]{4,3,2,1,0:T(4,128)(2,1)}), bf16[32,2,30,4,128]{4,3,2,1,0:T(4,128)(2,1)S(1)}, u32[]{:S(2)}, u32[]{:S(2)}) %all-to-all-start) | async-done | bytes 1966112 | tf_op jit(solution)/shard_map/all_to_all | solution.py:172
  64.8 26.0 %schur_partial.1 = f32[8,54,432]{2,1,0:T(8,128)} custom-call(bf16[32,2,30,4,128]{4,3,2,1,0:T(4,128)(2,1)S(1)} %all-to-all-done.got_ref), custom_call_target="tpu_custom_call" | custom-call | flops 10000000000 | bytes 3000000 | tf_op jit(solution)/shard_map/schur_partial/pallas_call | solution.py:146
  90.8 7.0 %all-to-all-start.1 = ((f32[8,54,432]{2,1,0:T(8,128)}), f32[8,54,432]{2,1,0:T(8,128)S(1)}, u32[]{:S(2)}, u32[]{:S(2)}) async-start(f32[8,54,432]{2,1,0:T(8,128)} %schur_partial.1), calls=%async_computation.1 | async-start | bytes 1835008 | tf_op jit(solution)/shard_map/all_to_all | solution.py:174
  97.9 13.5 %all-to-all-done.1 = f32[8,54,432]{2,1,0:T(8,128)S(1)} async-done(((f32[8,54,432]{2,1,0:T(8,128)}), f32[8,54,432]{2,1,0:T(8,128)S(1)}, u32[]{:S(2)}, u32[]{:S(2)}) %all-to-all-start.1) | async-done | bytes 746528 | tf_op jit(solution)/shard_map/all_to_all | solution.py:174
  111.4 0.1 reduce_sum.11
  111.4 1.4 %fusion = f32[1,54,432]{2,0,1:T(1,128)} fusion(pred[432]{0:T(512)(128)(4,1)S(1)} %fusion.4, pred[54]{0:T(512)(128)(4,1)S(1)} %get-tuple-element.9, pred[54]{0:T(512)(128)(4,1)S(1)} %get-tuple-element.8, f32[54,432]{1,0:T(8,128)S(1)} %reduce_sum.11, f32[432]{0:T(512)S(1)} %bitcast.10, s32[]{:T(128)S(6)} %select_n.97, f32[432]{0:T(512)S(1)} %bitcast.11, ...), kind=kLoop, calls=%fused_computation.7 | loop fusion | flops 279936 | bytes 196680 | tf_op jit(solution)/shard_map/sub | solution.py:186
  (6 shorter events, 0.1 us)
Async XLA Ops:
  0.0 1.2 %copy-start = (bf16[32,4,27,128]{3,1,2,0:T(4,128)(2,1)S(1)}, bf16[32,4,27,128]{3,1,2,0:T(4,128)(2,1)}, u32[]{:S(2)}) copy-start(bf16[32,4,27,128]{3,1,2,0:T(4,128)(2,1)} %param.7) | copy-start | bytes 2654212
  1.2 0.8 copy-start.1
  2.0 0.8 copy-start.2
  2.8 0.7 copy-start.3
  3.5 0.7 copy-start.4
  4.2 0.7 copy-start.5
  6.9 12.1 %copy-start.6 = (f32[1,9,9,48]{3,0,2,1:T(1,128)S(1)}, f32[1,9,9,48]{3,0,2,1:T(1,128)}, u32[]{:S(2)}) copy-start(f32[1,9,9,48]{3,0,2,1:T(1,128)} %param.13) | copy-start | bytes 46660
  7.0 57.9 %all-to-all-start = ((bf16[32,2,30,4,128]{4,3,2,1,0:T(4,128)(2,1)}), bf16[32,2,30,4,128]{4,3,2,1,0:T(4,128)(2,1)S(1)}, u32[]{:S(2)}, u32[]{:S(2)}) async-start(bf16[32,2,30,4,128]{4,3,2,1,0:T(4,128)(2,1)} %pack.1), calls=%async_computation | async-start | bytes 3932160 | tf_op jit(solution)/shard_map/all_to_all | solution.py:172
  90.8 20.6 %all-to-all-start.1 = ((f32[8,54,432]{2,1,0:T(8,128)}), f32[8,54,432]{2,1,0:T(8,128)S(1)}, u32[]{:S(2)}, u32[]{:S(2)}) async-start(f32[8,54,432]{2,1,0:T(8,128)} %schur_partial.1), calls=%async_computation.1 | async-start | bytes 1835008 | tf_op jit(solution)/shard_map/all_to_all | solution.py:174

commit v2 on v1

v2 whole, which is shorter than its diff:
```python
import functools
import itertools

import jax
import jax.numpy as jnp
from jax import lax
from jax.experimental import pallas as pl
from jax.experimental.pallas import tpu as pltpu
from jax.sharding import PartitionSpec as P

GROUPS_OF_ROWS = 30


def pack_kernel(
    site_of, route_hbm, count_hbm, jac_hbm, block_hbm, vis_hbm, obs_hbm, out_ref,
    route_ref, count_ref, block_ref, vis_ref, obs_ref, block_scratch, fill_ref, small_sems, tile_sems,
):
    tiles = jac_hbm.shape[0]
    width = jac_hbm.shape[3]
    places = out_ref.shape[0]
    small = [
        pltpu.make_async_copy(source, target, small_sems.at[index])
        for index, (source, target) in enumerate((
            (route_hbm, route_ref), (count_hbm, count_ref), (block_hbm, block_ref),
            (vis_hbm, vis_ref), (obs_hbm, obs_ref),
        ))
    ]
    for copy in small:
        copy.start()
    dead = jnp.full((4, width), -1.0, jnp.bfloat16)

    def clear(place, carry):
        fill_ref[place] = 0
        out_ref[place, 0, 27] = dead
        out_ref[place, 1, 27] = dead
        return carry

    lax.fori_loop(0, places, clear, 0, unroll=8)
    small[0].wait()

    def send(tile, carry):
        place = site_of(route_ref[tile])
        slot = fill_ref[place]
        fill_ref[place] = slot + 1
        route_ref[tile] = 2 * place + slot
        pltpu.make_async_copy(
            jac_hbm.at[tile], out_ref.at[place, slot, pl.ds(0, 27)], tile_sems.at[tile]
        ).start()
        return carry

    lax.fori_loop(0, tiles, send, 0, unroll=4)
    for copy in small[1:]:
        copy.wait()
    block_scratch[...] = block_ref[...].astype(jnp.float32)
    slot_iota = lax.broadcasted_iota(jnp.int32, (4, width), 0)
    point_iota = lax.broadcasted_iota(jnp.int32, (4, width), 1)

    def fill(tile, carry):
        place = route_ref[tile] // 2
        slot = route_ref[tile] % 2
        obs = jnp.broadcast_to(obs_ref[pl.ds(tile, 1), :], (4, width))
        live = (slot_iota < obs) & (point_iota < count_ref[tile])
        marks = jnp.where(live, vis_ref[tile], -1).astype(jnp.float32).astype(jnp.bfloat16)
        rows = [block_scratch[c, pl.ds(tile, 1), :] for c in range(6)]
        zero = jnp.zeros_like(rows[0])
        out_ref[place, slot, 27] = marks
        out_ref[place, slot, 28] = jnp.concatenate(rows[:4], axis=0).astype(jnp.bfloat16)
        out_ref[place, slot, 29] = jnp.concatenate(rows[4:] + [zero, zero], axis=0).astype(jnp.bfloat16)
        return carry

    lax.fori_loop(0, tiles, fill, 0, unroll=4)

    def finish(tile, carry):
        pltpu.make_async_copy(jac_hbm.at[0], out_ref.at[0, 0, pl.ds(0, 27)], tile_sems.at[tile]).wait()
        return carry

    lax.fori_loop(0, tiles, finish, 0)


def pack(jac, blocks, vis, obs, counts, route, places, site_of):
    tiles, width = jac.shape[0], jac.shape[3]
    anywhere = pl.BlockSpec(memory_space=pl.ANY)
    return pl.pallas_call(
        functools.partial(pack_kernel, site_of),
        out_shape=jax.ShapeDtypeStruct((places, 2, GROUPS_OF_ROWS, 4, width), jnp.bfloat16),
        in_specs=[anywhere] * 6,
        out_specs=pl.BlockSpec(memory_space=pltpu.VMEM),
        scratch_shapes=[
            pltpu.SMEM(route.shape, jnp.int32),
            pltpu.SMEM(counts.shape, jnp.int32),
            pltpu.VMEM(blocks.shape, jnp.bfloat16),
            pltpu.VMEM(vis.shape, jnp.int32),
            pltpu.VMEM(obs.shape, jnp.int32),
            pltpu.VMEM(blocks.shape, jnp.float32),
            pltpu.SMEM((places,), jnp.int32),
            pltpu.SemaphoreType.DMA((5,)),
            pltpu.SemaphoreType.DMA((tiles,)),
        ],
        compiler_params=pltpu.CompilerParams(vmem_limit_bytes=24 * 1024 * 1024),
        cost_estimate=pl.CostEstimate(flops=1000000, bytes_accessed=3000000, transcendentals=0),
        name="pack",
    )(route, counts, jac, blocks, vis, obs)


def inverse_rows(first, second):
    xx, yy, zz, xy = (first[c : c + 1] for c in range(4))
    xz, yz = (second[c : c + 1] for c in range(2))
    cxx = yy * zz - yz * yz
    cyy = xx * zz - xz * xz
    czz = xx * yy - xy * xy
    cxy = xz * yz - xy * zz
    cxz = xy * yz - xz * yy
    cyz = xy * xz - xx * yz
    inv_det = 1.0 / (xx * cxx + xy * cxy + xz * cxz)
    ixx, iyy, izz, ixy, ixz, iyz = (c * inv_det for c in (cxx, cyy, czz, cxy, cxz, cyz))
    return ((ixx, ixy, ixz), (ixy, iyy, iyz), (ixz, iyz, izz))


def expand_slot(got_ref, source, slot, rows_ref, left_ref, right_ref, column, cameras):
    width = got_ref.shape[4]
    first = got_ref[source, slot, 28].astype(jnp.float32)
    second = got_ref[source, slot, 29].astype(jnp.float32)
    inverse = inverse_rows(first, second)
    wide = [[jnp.broadcast_to(entry, (4, width)) for entry in line] for line in inverse]
    for r in range(9):
        factors = [got_ref[source, slot, 3 * r + m].astype(jnp.float32) for m in range(3)]
        for k in range(3):
            value = factors[0] * wide[0][k] + factors[1] * wide[1][k] + factors[2] * wide[2][k]
            rows_ref[3 * r + k, 0:4] = value.astype(jnp.bfloat16).astype(jnp.float32)
            rows_ref[3 * r + k, 4:8] = factors[k]
    rows_ref[27, 0:4] = got_ref[source, slot, 27].astype(jnp.float32)
    blocks = cameras // 16
    iota = lax.broadcasted_iota(jnp.int32, (16, width), 0).astype(jnp.float32)
    masks = []
    for i in range(4):
        mark = jnp.broadcast_to(rows_ref[27, i : i + 1], (16, width)).astype(jnp.bfloat16)
        masks.append([mark == (iota + 16.0 * b).astype(jnp.bfloat16) for b in range(blocks)])
    zero = jnp.zeros((16, width), jnp.bfloat16)
    yield
    for r in range(9):
        for k in range(3):
            for side, out in ((0, left_ref), (4, right_ref)):
                sums = [zero] * blocks
                for i in range(4):
                    row = jnp.broadcast_to(rows_ref[3 * r + k, side + i : side + i + 1], (16, width))
                    row = row.astype(jnp.bfloat16)
                    sums = [jnp.where(masks[i][b], row, sums[b]) for b in range(blocks)]
                for b in range(blocks):
                    out[pl.ds(r * cameras + 16 * b, 16), pl.ds(column + 2 * k * width, width)] = sums[b]
        yield


def schur_kernel(cameras, pieces, got_ref, out_ref, *scratch):
    part, wide = 9 * cameras // pieces, 2 * got_ref.shape[4]
    sums = [pltpu.ACC(unit)((part, wide), jnp.float32) for unit in range(2) for _ in range(pieces)]
    pl.run_scoped(functools.partial(schur_body, cameras, got_ref, out_ref, *scratch), *sums)


def schur_body(cameras, got_ref, out_ref, rows_ref, left_a, left_b, right_a, right_b, *sums):
    sources = got_ref.shape[0]
    width = got_ref.shape[4]
    side = 9 * cameras
    lefts, rights = (left_a, left_b), (right_a, right_b)
    count = len(sums) // 2
    sums = (sums[:count], sums[count:])
    part = side // count
    wide = 2 * width
    for right in rights:
        right[pl.ds(side, 2 * wide - side), :] = jnp.zeros((2 * wide - side, 3 * wide), jnp.bfloat16)

    def expand(source, buffer):
        for slot in range(2):
            yield from expand_slot(
                got_ref, source, slot, rows_ref.at[slot], lefts[buffer], rights[buffer], slot * width, cameras,
            )

    def multiply(buffer):
        for k in range(3):
            columns = pl.ds(k * wide, wide)
            for unit in range(2):
                pltpu.matmul_push_rhs(
                    rights[buffer][pl.ds(unit * wide, wide), columns], k % 2, unit, transpose=True
                )
            for piece in range(count):
                value = lefts[buffer][pl.ds(piece * part, part), columns]
                for unit in range(2):
                    pltpu.matmul_acc_lhs(sums[unit][piece], value, k % 2 if piece == 0 else None)
                yield

    def both(source, buffer):
        one = expand(source, buffer)
        two = multiply(1 - buffer)
        each = -(-20 // (3 * count))
        steps, alive = 0, True
        while alive:
            alive = next(two, 1) is None
            steps += 20
            while steps >= 3 * count:
                steps -= 3 * count
                next(one, 1)
        for _ in one:
            pass

    for _ in expand(0, 0):
        pass

    def step(turn, carry):
        both(2 * turn + 1, 1)
        both(jnp.minimum(2 * turn + 2, sources - 1), 0)
        return carry

    lax.fori_loop(0, sources // 2, step, 0)
    for piece in range(count):
        rows = pl.ds(piece * part, part)
        out_ref[rows, 0:wide] = pltpu.matmul_pop(sums[0][piece])
        out_ref[rows, wide:side] = pltpu.matmul_pop(sums[1][piece])[:, : side - wide]


def schur_partial(got, cameras, shares):
    width = got.shape[4]
    side = 9 * cameras
    pieces = 9
    vmem = pl.BlockSpec(memory_space=pltpu.VMEM)
    out = pl.pallas_call(
        functools.partial(schur_kernel, cameras, pieces),
        out_shape=jax.ShapeDtypeStruct((side, side), jnp.float32),
        in_specs=[vmem],
        out_specs=vmem,
        scratch_shapes=[
            pltpu.VMEM((2, 28, 8, width), jnp.float32),
            pltpu.VMEM((side, 6 * width), jnp.bfloat16),
            pltpu.VMEM((side, 6 * width), jnp.bfloat16),
            pltpu.VMEM((4 * width, 6 * width), jnp.bfloat16),
            pltpu.VMEM((4 * width, 6 * width), jnp.bfloat16),
        ],
        compiler_params=pltpu.CompilerParams(vmem_limit_bytes=32 * 1024 * 1024),
        cost_estimate=pl.CostEstimate(flops=10000000000, bytes_accessed=3000000, transcendentals=0),
        name="schur_partial",
    )(got)
    return out.reshape(shares, side // shares, side)


def own_blocks(camera_blocks, share, share_rows):
    cameras = camera_blocks.shape[3]
    side = 9 * cameras
    row = share * share_rows + lax.broadcasted_iota(jnp.int32, (share_rows, side), 0)
    column = lax.broadcasted_iota(jnp.int32, (share_rows, side), 1)
    lines = camera_blocks[0].reshape(9, side)
    first = share * share_rows // cameras
    own = jnp.zeros((share_rows, side), jnp.float32)
    for step in range(-(-share_rows // cameras) + 1):
        line = lax.dynamic_slice_in_dim(lines, jnp.minimum(first + step, 8), 1, 0)
        own = jnp.where(row // cameras == first + step, line, own)
    return jnp.where(row % cameras == column % cameras, own, 0.0)


AXES = ("layer", "zp", "zb", "x", "pair")


def local(sizes, jac_blocks, point_blocks, visibility, obs_count, tile_count, route, camera_blocks):
    cameras = camera_blocks.shape[3]
    side = 9 * cameras
    layers, pairs, far, near, across = (lax.axis_size(a) for a in ("layer", "pair", "zp", "zb", "x"))
    shares = layers * pairs

    def site_of(group):
        return (group // across % near) * (across * pairs) + group % across * pairs + group // (across * near)

    packed = pack(
        jac_blocks.transpose(0, 2, 1, 3), point_blocks.transpose(1, 0, 2), visibility, obs_count, tile_count,
        route[:, 0], near * across * pairs, site_of,
    )
    got = lax.all_to_all(packed, ("zb", "x", "pair"), split_axis=0, concat_axis=0, tiled=True)
    partial_value = schur_partial(got, cameras, shares).reshape(layers, pairs, side // shares, side)
    layer, plane = lax.axis_index("layer"), lax.axis_index("zp")
    theirs = lax.dynamic_index_in_dim(partial_value, 1 - layer, 0, keepdims=False)
    ours = lax.dynamic_index_in_dim(partial_value, layer, 0, keepdims=False)
    ours = ours + lax.ppermute(theirs, "layer", [(0, 1), (1, 0)])
    total = None
    for turn in range(far):
        links = []
        for source in itertools.product(*(range(size) for size in sizes)):
            c, zp, zb, x, y = source
            links.append((flat(source, sizes), flat((c, y, zb, x, zp ^ turn), sizes)))
        piece = lax.dynamic_index_in_dim(ours, plane ^ turn, 0, keepdims=False)
        came = lax.ppermute(piece, AXES, links)
        total = came if total is None else total + came
    share = layer * pairs + lax.axis_index("pair")
    return (own_blocks(camera_blocks, share, side // shares) - total)[None]


def flat(place, sizes):
    index = 0
    for coordinate, size in zip(place, sizes):
        index = index * size + coordinate
    return index


def solution(mesh):
    layers, cams, pairs = mesh.devices.shape
    across = 4
    near = 2
    sizes = (layers, cams // (near * across), near, across, pairs)
    split = jax.sharding.Mesh(mesh.devices.reshape(sizes), AXES)
    cam = ("zp", "zb", "x")
    placed = (
        P(AXES, None, None, None),
        P(AXES, None, None),
        P(AXES, None, None),
        P(AXES, None),
        P(AXES),
        P(AXES, None),
        P(cam, None, None, None),
    )
    return jax.shard_map(
        functools.partial(local, sizes),
        mesh=split,
        in_specs=placed,
        out_specs=P(cam, ("layer", "pair"), None),
        check_vma=False,
    )
```

time: 113 us -> 107 us (0.947)
  waiting for transfers between devices: 59.1 us -> 47.7 us
  starting transfers between devices: 19 us -> 24.4 us
  other arithmetic: 1.6 us -> 0.35 us
    all_to_all x2 -> x1, waiting for transfers between devices: 59.1 us -> 24.1 us  [local(): lax.all_to_all(packed, ('zb', 'x', 'pair'), split_axis=0, concat_axis=0,...]
    ppermute x0 -> x5, waiting for transfers between devices: none -> 23.7 us  [the longest x4 22.6 us: local(): came = lax.ppermute(piece, AXES, links)]
    ppermute x0 -> x5, starting transfers between devices: none -> 15.2 us  [the longest x4 11.3 us: local(): came = lax.ppermute(piece, AXES, links)]
    all_to_all x2 -> x1, starting transfers between devices: 19 us -> 9.23 us  [local(): lax.all_to_all(packed, ('zb', 'x', 'pair'), split_axis=0, concat_axis=0,...]
    sub x2, other arithmetic: 1.37 us -> 0.13 us  [the longest x1 0.11 us: local(): return (own_blocks(camera_blocks, share, side // shares) - total)[None]]
  transfers between devices with their start and end apart: 2 -> 6, of which waited for: 2 -> 4; matrix products, arithmetic and copies ran while one was open for 0% -> 0% of each run, Pallas kernels for 0% -> 0%
where the time goes in v2:
time: 107 us; the launch traced here: 106 us
  waiting for transfers between devices  47.7 us (45%)
  Pallas kernels  27.7 us (26%)
  starting transfers between devices  24.4 us (23%)
  local copies, waits for them, and re-layouts  5.85 us (5%)
    all_to_all x1, waiting for transfers between devices, local(): lax.all_to_all(packed, ('zb', 'x', 'pair'), split_axis=0, concat_axis=0,...  24.1 us
    pallas_call x1, Pallas kernels, schur_partial(): pl.pallas_call(functools.partial(schur_kernel, cameras, pieces), out_shap...  23.3 us
    ppermute x4, waiting for transfers between devices, local(): came = lax.ppermute(piece, AXES, links)  22.6 us
    ppermute x4, starting transfers between devices, local(): came = lax.ppermute(piece, AXES, links)  11.3 us
    all_to_all x1, starting transfers between devices, local(): lax.all_to_all(packed, ('zb', 'x', 'pair'), split_axis=0, concat_axis=0,...  9.23 us
    unnamed x14, local copies, waits for them, and re-layouts  4.84 us
    pallas_call x1, Pallas kernels, pack(): pl.pallas_call(functools.partial(pack_kernel, site_of), out_shape=jax.Sha...  4.41 us
    ppermute x1, starting transfers between devices, local(): ours = ours + lax.ppermute(theirs, 'layer', [(0, 1), (1, 0)])  3.85 us
  transfers between devices with their start and end apart: 6, of which 4 were waited for; matrix products, arithmetic and copies ran while one was open for 0% of the time, Pallas kernels for 0%

profile of v2, /device:TPU:1, one launch (start us, length us, event | category | flops | bytes accessed | tf_op | source)
XLA Modules:
  0.0 106.3 jit_solution(3191760671810222364)
XLA Ops:
  0.0 1.2 %copy-done = bf16[32,4,27,128]{3,1,2,0:T(4,128)(2,1)S(1)} copy-done((bf16[32,4,27,128]{3,1,2,0:T(4,128)(2,1)S(1)}, bf16[32,4,27,128]{3,1,2,0:T(4,128)(2,1)}, u32[]{:S(2)}) %copy-start) | copy-done | bytes 884760
  1.2 0.8 copy-done.1
  2.0 0.8 copy-done.2
  2.8 0.7 copy-done.3
  3.5 0.7 copy-done.4
  4.2 0.7 copy-done.5
  4.8 4.4 %pack.1 = bf16[32,2,30,4,128]{4,3,2,1,0:T(4,128)(2,1)} custom-call(s32[32]{0:T(128)S(1)} %bitcast.20, s32[32]{0:T(128)S(1)} %copy-done.5, bf16[32,27,4,128]{3,2,1,0:T(4,128)(2,1)S(1)} %bitcast.18, bf16[6,32,128]{2,1,0:T(8,128)(2,1)S(1)} %bitcast.19, s32[32,4,128]{2,1,0:T(4,128)S(1)} %copy-done.1, s32[32,128]{1,0:T(8,128)S(1)} %copy-done.3), custom_call_target="tpu_custom_call" | custom-call | flops 1000000 | bytes 3000000 | tf_op jit(solution)/shard_map/pack/pallas_call | solution.py:83
  9.3 9.2 %all-to-all-start = ((bf16[32,2,30,4,128]{4,3,2,1,0:T(4,128)(2,1)}), bf16[32,2,30,4,128]{4,3,2,1,0:T(4,128)(2,1)S(1)}, u32[]{:S(2)}, u32[]{:S(2)}) async-start(bf16[32,2,30,4,128]{4,3,2,1,0:T(4,128)(2,1)} %pack.1), calls=%async_computation | async-start | bytes 3932160 | tf_op jit(solution)/shard_map/all_to_all | solution.py:273
  18.5 24.1 %all-to-all-done.got_ref = bf16[32,2,30,4,128]{4,3,2,1,0:T(4,128)(2,1)S(1)} async-done(((bf16[32,2,30,4,128]{4,3,2,1,0:T(4,128)(2,1)}), bf16[32,2,30,4,128]{4,3,2,1,0:T(4,128)(2,1)S(1)}, u32[]{:S(2)}, u32[]{:S(2)}) %all-to-all-start) | async-done | bytes 1966112 | tf_op jit(solution)/shard_map/all_to_all | solution.py:273
  42.6 23.3 %schur_partial.1 = f32[432,432]{1,0:T(8,128)S(1)} custom-call(bf16[32,2,30,4,128]{4,3,2,1,0:T(4,128)(2,1)S(1)} %all-to-all-done.got_ref), custom_call_target="tpu_custom_call" | custom-call | flops 10000000000 | bytes 3000000 | tf_op jit(solution)/shard_map/schur_partial/pallas_call | solution.py:224
  65.9 0.1 reshape_reshape.3
  66.1 3.9 %collective-permute-start = (f32[4,54,432]{2,1,0:T(8,128)S(1)}, f32[4,54,432]{2,1,0:T(8,128)S(1)}, u32[]{:S(2)}, u32[]{:S(2)}) collective-permute-start(f32[4,54,432]{2,1,0:T(8,128)S(1)} %dynamic-slice_bitcast_fusion), channel_id=1, source_target_pairs={{0,128},{128,0},{1,129},{129,1},{2,130},{130,2},{3,131},{131,3},{4... | collective-permute-start | bytes 1119752 | tf_op jit(solution)/shard_map/ppermute | solution.py:278
  70.0 0.1 reduce
  70.1 0.1 reshape_squeeze.3
  70.3 1.1 %collective-permute-done = f32[4,54,432]{2,1,0:T(8,128)S(1)} collective-permute-done((f32[4,54,432]{2,1,0:T(8,128)S(1)}, f32[4,54,432]{2,1,0:T(8,128)S(1)}, u32[]{:S(2)}, u32[]{:S(2)}) %collective-permute-start) | collective-permute-done | bytes 373280 | tf_op jit(solution)/shard_map/ppermute | solution.py:278
  71.4 0.1 bitcast_add_fusion
  71.5 0.9 collective-permute-start.4
  72.4 6.9 %collective-permute-start.3 = (f32[54,432]{1,0:T(8,128)S(1)}, f32[54,432]{1,0:T(8,128)S(1)}, u32[]{:S(2)}, u32[]{:S(2)}) collective-permute-start(f32[54,432]{1,0:T(8,128)S(1)} %get-tuple-element.7), channel_id=1, source_target_pairs={{0,2},{1,34},{2,66},{3,98},{4,6},{5,38},{6,70},{7,102},{8,10},{9,4... | collective-permute-start | bytes 279944 | tf_op jit(solution)/shard_map/ppermute | solution.py:286
  79.4 0.7 collective-permute-start.1
  80.0 2.8 %collective-permute-start.2 = (f32[54,432]{1,0:T(8,128)S(1)}, f32[54,432]{1,0:T(8,128)S(1)}, u32[]{:S(2)}, u32[]{:S(2)}) collective-permute-start(f32[54,432]{1,0:T(8,128)S(1)} %get-tuple-element.5), channel_id=1, source_target_pairs={{0,1},{1,33},{2,65},{3,97},{4,5},{5,37},{6,69},{7,101},{8,9},{9,41... | collective-permute-start | bytes 279944 | tf_op jit(solution)/shard_map/ppermute | solution.py:286
  82.8 2.0 %collective-permute-done.4 = f32[54,432]{1,0:T(8,128)S(1)} collective-permute-done((f32[54,432]{1,0:T(8,128)S(1)}, f32[54,432]{1,0:T(8,128)S(1)}, u32[]{:S(2)}, u32[]{:S(2)}) %collective-permute-start.4) | collective-permute-done | bytes 93344 | tf_op jit(solution)/shard_map/ppermute | solution.py:286
  84.9 20.6 %collective-permute-done.2 = f32[54,432]{1,0:T(8,128)S(1)} collective-permute-done((f32[54,432]{1,0:T(8,128)S(1)}, f32[54,432]{1,0:T(8,128)S(1)}, u32[]{:S(2)}, u32[]{:S(2)}) %collective-permute-start.2) | collective-permute-done | bytes 93344 | tf_op jit(solution)/shard_map/ppermute | solution.py:286
  105.4 0.1 add_subtract_fusion
  105.6 0.7 broadcast_in_dim.39
  (18 shorter events, 0.2 us)
Async XLA Ops:
  0.0 1.2 %copy-start = (bf16[32,4,27,128]{3,1,2,0:T(4,128)(2,1)S(1)}, bf16[32,4,27,128]{3,1,2,0:T(4,128)(2,1)}, u32[]{:S(2)}) copy-start(bf16[32,4,27,128]{3,1,2,0:T(4,128)(2,1)} %param.7) | copy-start | bytes 2654212
  1.2 0.8 copy-start.1
  2.0 0.8 copy-start.2
  2.8 0.7 copy-start.3
  3.5 0.7 copy-start.4
  4.2 0.7 copy-start.5
  9.3 33.3 %all-to-all-start = ((bf16[32,2,30,4,128]{4,3,2,1,0:T(4,128)(2,1)}), bf16[32,2,30,4,128]{4,3,2,1,0:T(4,128)(2,1)S(1)}, u32[]{:S(2)}, u32[]{:S(2)}) async-start(bf16[32,2,30,4,128]{4,3,2,1,0:T(4,128)(2,1)} %pack.1), calls=%async_computation | async-start | bytes 3932160 | tf_op jit(solution)/shard_map/all_to_all | solution.py:273
  65.9 4.1 %copy-start.6 = (f32[1,9,9,48]{3,0,2,1:T(1,128)S(1)}, f32[1,9,9,48]{3,0,2,1:T(1,128)}, u32[]{:S(2)}) copy-start(f32[1,9,9,48]{3,0,2,1:T(1,128)} %param.13) | copy-start | bytes 46660
  66.1 5.3 %collective-permute-start = (f32[4,54,432]{2,1,0:T(8,128)S(1)}, f32[4,54,432]{2,1,0:T(8,128)S(1)}, u32[]{:S(2)}, u32[]{:S(2)}) collective-permute-start(f32[4,54,432]{2,1,0:T(8,128)S(1)} %dynamic-slice_bitcast_fusion), channel_id=1, source_target_pairs={{0,128},{128,0},{1,129},{129,1},{2,130},{130,2},{3,131},{131,3},{4... | collective-permute-start | bytes 1119752 | tf_op jit(solution)/shard_map/ppermute | solution.py:278
  71.5 13.4 %collective-permute-start.4 = (f32[54,432]{1,0:T(8,128)S(1)}, f32[54,432]{1,0:T(8,128)S(1)}, u32[]{:S(2)}, u32[]{:S(2)}) collective-permute-start(f32[54,432]{1,0:T(8,128)S(1)} %get-tuple-element.6), channel_id=1, source_target_pairs={{0,3},{1,35},{2,67},{3,99},{4,7},{5,39},{6,71},{7,103},{8,11},{9,4... | collective-permute-start | bytes 279944 | tf_op jit(solution)/shard_map/ppermute | solution.py:286
  72.4 12.4 %collective-permute-start.3 = (f32[54,432]{1,0:T(8,128)S(1)}, f32[54,432]{1,0:T(8,128)S(1)}, u32[]{:S(2)}, u32[]{:S(2)}) collective-permute-start(f32[54,432]{1,0:T(8,128)S(1)} %get-tuple-element.7), channel_id=1, source_target_pairs={{0,2},{1,34},{2,66},{3,98},{4,6},{5,38},{6,70},{7,102},{8,10},{9,4... | collective-permute-start | bytes 279944 | tf_op jit(solution)/shard_map/ppermute | solution.py:286
  79.4 5.5 %collective-permute-start.1 = (f32[54,432]{1,0:T(8,128)S(1)}, f32[54,432]{1,0:T(8,128)S(1)}, u32[]{:S(2)}, u32[]{:S(2)}) collective-permute-start(f32[54,432]{1,0:T(8,128)S(1)} %get-tuple-element.8), channel_id=1, source_target_pairs={{0,0},{1,32},{2,64},{3,96},{4,4},{5,36},{6,68},{7,100},{8,8},{9,40... | collective-permute-start | bytes 279944 | tf_op jit(solution)/shard_map/ppermute | solution.py:286
  80.0 25.4 %collective-permute-start.2 = (f32[54,432]{1,0:T(8,128)S(1)}, f32[54,432]{1,0:T(8,128)S(1)}, u32[]{:S(2)}, u32[]{:S(2)}) collective-permute-start(f32[54,432]{1,0:T(8,128)S(1)} %get-tuple-element.5), channel_id=1, source_target_pairs={{0,1},{1,33},{2,65},{3,97},{4,5},{5,37},{6,69},{7,101},{8,9},{9,41... | collective-permute-start | bytes 279944 | tf_op jit(solution)/shard_map/ppermute | solution.py:286

commit v3 on v2

--- a/solution.py
+++ b/solution.py
@@ -79,7 +79,7 @@
 
 def pack(jac, blocks, vis, obs, counts, route, places, site_of):
     tiles, width = jac.shape[0], jac.shape[3]
-    anywhere = pl.BlockSpec(memory_space=pl.ANY)
+    anywhere = pl.BlockSpec(memory_space=pltpu.HBM)
     return pl.pallas_call(
         functools.partial(pack_kernel, site_of),
         out_shape=jax.ShapeDtypeStruct((places, 2, GROUPS_OF_ROWS, 4, width), jnp.bfloat16),
@@ -264,7 +264,9 @@
     shares = layers * pairs
 
     def site_of(group):
-        return (group // across % near) * (across * pairs) + group % across * pairs + group // (across * near)
+        side_z = group // across % near
+        y = (group // (across * near) + 2 * lax.axis_index("zp") + 2 * side_z) % pairs
+        return side_z * (across * pairs) + group % across * pairs + y
 
     packed = pack(
         jac_blocks.transpose(0, 2, 1, 3), point_blocks.transpose(1, 0, 2), visibility, obs_count, tile_count,
@@ -281,7 +283,7 @@
         links = []
         for source in itertools.product(*(range(size) for size in sizes)):
             c, zp, zb, x, y = source
-            links.append((flat(source, sizes), flat((c, y, zb, x, zp ^ turn), sizes)))
+            links.append((flat(source, sizes), flat((c, (y + 2 * zp + 2 * zb) % far, zb, x, zp ^ turn), sizes)))
         piece = lax.dynamic_index_in_dim(ours, plane ^ turn, 0, keepdims=False)
         came = lax.ppermute(piece, AXES, links)
         total = came if total is None else total + came

time: 107 us -> 99.1 us (0.926)
  waiting for transfers between devices: 47.7 us -> 36.5 us
  starting transfers between devices: 24.4 us -> 27.7 us
    ppermute x4, waiting for transfers between devices: 22.6 us -> 11.4 us  [local(): came = lax.ppermute(piece, AXES, links)]
    ppermute x4, starting transfers between devices: 11.3 us -> 14.6 us  [local(): came = lax.ppermute(piece, AXES, links)]
  transfers between devices with their start and end apart: 6 -> 6, of which waited for: 4 -> 3; matrix products, arithmetic and copies ran while one was open for 0% -> 0% of each run, Pallas kernels for 0% -> 0%
where the time goes in v3:
time: 99.1 us; the launch traced here: 98.6 us
  waiting for transfers between devices  36.5 us (37%)
  Pallas kernels  27.9 us (28%)
  starting transfers between devices  27.7 us (28%)
  local copies, waits for them, and re-layouts  5.85 us (6%)
    all_to_all x1, waiting for transfers between devices, local(): lax.all_to_all(packed, ('zb', 'x', 'pair'), split_axis=0, concat_axis=0,...  24.1 us
    pallas_call x1, Pallas kernels, schur_partial(): pl.pallas_call(functools.partial(schur_kernel, cameras, pieces), out_shap...  23.3 us
    ppermute x4, starting transfers between devices, local(): came = lax.ppermute(piece, AXES, links)  14.6 us
    ppermute x4, waiting for transfers between devices, local(): came = lax.ppermute(piece, AXES, links)  11.4 us
    all_to_all x1, starting transfers between devices, local(): lax.all_to_all(packed, ('zb', 'x', 'pair'), split_axis=0, concat_axis=0,...  9.23 us
    unnamed x14, local copies, waits for them, and re-layouts  4.84 us
    pallas_call x1, Pallas kernels, pack(): pl.pallas_call(functools.partial(pack_kernel, site_of), out_shape=jax.Sha...  4.57 us
    ppermute x1, starting transfers between devices, local(): ours = ours + lax.ppermute(theirs, 'layer', [(0, 1), (1, 0)])  3.85 us
  transfers between devices with their start and end apart: 6, of which 3 were waited for; matrix products, arithmetic and copies ran while one was open for 0% of the time, Pallas kernels for 0%

profile of v3, /device:TPU:1, one launch (start us, length us, event | category | flops | bytes accessed | tf_op | source)
XLA Modules:
  0.0 98.6 jit_solution(7859537098708969116)
XLA Ops:
  0.0 1.2 %copy-done = bf16[32,4,27,128]{3,1,2,0:T(4,128)(2,1)S(1)} copy-done((bf16[32,4,27,128]{3,1,2,0:T(4,128)(2,1)S(1)}, bf16[32,4,27,128]{3,1,2,0:T(4,128)(2,1)}, u32[]{:S(2)}) %copy-start) | copy-done | bytes 884760
  1.2 0.8 copy-done.1
  2.0 0.8 copy-done.2
  2.8 0.7 copy-done.3
  3.5 0.7 copy-done.4
  4.2 0.7 copy-done.5
  4.8 4.6 %pack.1 = bf16[32,2,30,4,128]{4,3,2,1,0:T(4,128)(2,1)} custom-call(s32[32]{0:T(128)S(1)} %bitcast.20, s32[32]{0:T(128)S(1)} %copy-done.5, bf16[32,27,4,128]{3,2,1,0:T(4,128)(2,1)S(1)} %bitcast.18, bf16[6,32,128]{2,1,0:T(8,128)(2,1)S(1)} %bitcast.19, s32[32,4,128]{2,1,0:T(4,128)S(1)} %copy-done.1, s32[32,128]{1,0:T(8,128)S(1)} %copy-done.3), custom_call_target="tpu_custom_call" | custom-call | flops 1000000 | bytes 3000000 | tf_op jit(solution)/shard_map/pack/pallas_call | solution.py:83
  9.4 9.2 %all-to-all-start = ((bf16[32,2,30,4,128]{4,3,2,1,0:T(4,128)(2,1)}), bf16[32,2,30,4,128]{4,3,2,1,0:T(4,128)(2,1)S(1)}, u32[]{:S(2)}, u32[]{:S(2)}) async-start(bf16[32,2,30,4,128]{4,3,2,1,0:T(4,128)(2,1)} %pack.1), calls=%async_computation | async-start | bytes 3932160 | tf_op jit(solution)/shard_map/all_to_all | solution.py:275
  18.7 24.1 %all-to-all-done.got_ref = bf16[32,2,30,4,128]{4,3,2,1,0:T(4,128)(2,1)S(1)} async-done(((bf16[32,2,30,4,128]{4,3,2,1,0:T(4,128)(2,1)}), bf16[32,2,30,4,128]{4,3,2,1,0:T(4,128)(2,1)S(1)}, u32[]{:S(2)}, u32[]{:S(2)}) %all-to-all-start) | async-done | bytes 1966112 | tf_op jit(solution)/shard_map/all_to_all | solution.py:275
  42.7 23.3 %schur_partial.1 = f32[432,432]{1,0:T(8,128)S(1)} custom-call(bf16[32,2,30,4,128]{4,3,2,1,0:T(4,128)(2,1)S(1)} %all-to-all-done.got_ref), custom_call_target="tpu_custom_call" | custom-call | flops 10000000000 | bytes 3000000 | tf_op jit(solution)/shard_map/schur_partial/pallas_call | solution.py:224
  66.1 0.0 copy-start.6
  66.1 0.1 reshape_reshape.3
  66.2 3.9 %collective-permute-start = (f32[4,54,432]{2,1,0:T(8,128)S(1)}, f32[4,54,432]{2,1,0:T(8,128)S(1)}, u32[]{:S(2)}, u32[]{:S(2)}) collective-permute-start(f32[4,54,432]{2,1,0:T(8,128)S(1)} %dynamic-slice_bitcast_fusion), channel_id=1, source_target_pairs={{0,128},{128,0},{1,129},{129,1},{2,130},{130,2},{3,131},{131,3},{4... | collective-permute-start | bytes 1119752 | tf_op jit(solution)/shard_map/ppermute | solution.py:280
  70.2 0.1 reduce
  70.3 0.1 reshape_squeeze.3
  70.5 1.1 %collective-permute-done = f32[4,54,432]{2,1,0:T(8,128)S(1)} collective-permute-done((f32[4,54,432]{2,1,0:T(8,128)S(1)}, f32[4,54,432]{2,1,0:T(8,128)S(1)}, u32[]{:S(2)}, u32[]{:S(2)}) %collective-permute-start) | collective-permute-done | bytes 373280 | tf_op jit(solution)/shard_map/ppermute | solution.py:280
  71.5 0.1 bitcast_add_fusion
  71.7 0.9 collective-permute-start.4
  72.6 8.8 %collective-permute-start.3 = (f32[54,432]{1,0:T(8,128)S(1)}, f32[54,432]{1,0:T(8,128)S(1)}, u32[]{:S(2)}, u32[]{:S(2)}) collective-permute-start(f32[54,432]{1,0:T(8,128)S(1)} %get-tuple-element.7), channel_id=1, source_target_pairs={{0,2},{1,34},{2,66},{3,98},{4,6},{5,38},{6,70},{7,102},{8,10},{9,4... | collective-permute-start | bytes 279944 | tf_op jit(solution)/shard_map/ppermute | solution.py:288
  81.4 0.7 collective-permute-start.1
  82.1 4.2 %collective-permute-start.2 = (f32[54,432]{1,0:T(8,128)S(1)}, f32[54,432]{1,0:T(8,128)S(1)}, u32[]{:S(2)}, u32[]{:S(2)}) collective-permute-start(f32[54,432]{1,0:T(8,128)S(1)} %get-tuple-element.5), channel_id=1, source_target_pairs={{0,1},{1,33},{2,65},{3,97},{4,5},{5,37},{6,69},{7,101},{8,9},{9,41... | collective-permute-start | bytes 279944 | tf_op jit(solution)/shard_map/ppermute | solution.py:288
  86.4 11.4 %collective-permute-done.2 = f32[54,432]{1,0:T(8,128)S(1)} collective-permute-done((f32[54,432]{1,0:T(8,128)S(1)}, f32[54,432]{1,0:T(8,128)S(1)}, u32[]{:S(2)}, u32[]{:S(2)}) %collective-permute-start.2) | collective-permute-done | bytes 93344 | tf_op jit(solution)/shard_map/ppermute | solution.py:288
  97.7 0.1 add_subtract_fusion
  97.9 0.7 broadcast_in_dim.39
  (18 shorter events, 0.2 us)
Async XLA Ops:
  0.0 1.2 %copy-start = (bf16[32,4,27,128]{3,1,2,0:T(4,128)(2,1)S(1)}, bf16[32,4,27,128]{3,1,2,0:T(4,128)(2,1)}, u32[]{:S(2)}) copy-start(bf16[32,4,27,128]{3,1,2,0:T(4,128)(2,1)} %param.7) | copy-start | bytes 2654212
  1.2 0.8 copy-start.1
  2.0 0.8 copy-start.2
  2.8 0.7 copy-start.3
  3.5 0.7 copy-start.4
  4.2 0.7 copy-start.5
  9.4 33.3 %all-to-all-start = ((bf16[32,2,30,4,128]{4,3,2,1,0:T(4,128)(2,1)}), bf16[32,2,30,4,128]{4,3,2,1,0:T(4,128)(2,1)S(1)}, u32[]{:S(2)}, u32[]{:S(2)}) async-start(bf16[32,2,30,4,128]{4,3,2,1,0:T(4,128)(2,1)} %pack.1), calls=%async_computation | async-start | bytes 3932160 | tf_op jit(solution)/shard_map/all_to_all | solution.py:275
  66.1 4.1 %copy-start.6 = (f32[1,9,9,48]{3,0,2,1:T(1,128)S(1)}, f32[1,9,9,48]{3,0,2,1:T(1,128)}, u32[]{:S(2)}) copy-start(f32[1,9,9,48]{3,0,2,1:T(1,128)} %param.13) | copy-start | bytes 46660
  66.2 5.3 %collective-permute-start = (f32[4,54,432]{2,1,0:T(8,128)S(1)}, f32[4,54,432]{2,1,0:T(8,128)S(1)}, u32[]{:S(2)}, u32[]{:S(2)}) collective-permute-start(f32[4,54,432]{2,1,0:T(8,128)S(1)} %dynamic-slice_bitcast_fusion), channel_id=1, source_target_pairs={{0,128},{128,0},{1,129},{129,1},{2,130},{130,2},{3,131},{131,3},{4... | collective-permute-start | bytes 1119752 | tf_op jit(solution)/shard_map/ppermute | solution.py:280
  71.7 14.7 %collective-permute-start.4 = (f32[54,432]{1,0:T(8,128)S(1)}, f32[54,432]{1,0:T(8,128)S(1)}, u32[]{:S(2)}, u32[]{:S(2)}) collective-permute-start(f32[54,432]{1,0:T(8,128)S(1)} %get-tuple-element.6), channel_id=1, source_target_pairs={{0,3},{1,35},{2,67},{3,99},{4,7},{5,39},{6,71},{7,103},{8,11},{9,4... | collective-permute-start | bytes 279944 | tf_op jit(solution)/shard_map/ppermute | solution.py:288
  72.6 13.7 %collective-permute-start.3 = (f32[54,432]{1,0:T(8,128)S(1)}, f32[54,432]{1,0:T(8,128)S(1)}, u32[]{:S(2)}, u32[]{:S(2)}) collective-permute-start(f32[54,432]{1,0:T(8,128)S(1)} %get-tuple-element.7), channel_id=1, source_target_pairs={{0,2},{1,34},{2,66},{3,98},{4,6},{5,38},{6,70},{7,102},{8,10},{9,4... | collective-permute-start | bytes 279944 | tf_op jit(solution)/shard_map/ppermute | solution.py:288
  81.4 4.9 %collective-permute-start.1 = (f32[54,432]{1,0:T(8,128)S(1)}, f32[54,432]{1,0:T(8,128)S(1)}, u32[]{:S(2)}, u32[]{:S(2)}) collective-permute-start(f32[54,432]{1,0:T(8,128)S(1)} %get-tuple-element.8), channel_id=1, source_target_pairs={{0,0},{1,32},{2,64},{3,96},{4,4},{5,36},{6,68},{7,100},{8,8},{9,40... | collective-permute-start | bytes 279944 | tf_op jit(solution)/shard_map/ppermute | solution.py:288
  82.1 15.6 %collective-permute-start.2 = (f32[54,432]{1,0:T(8,128)S(1)}, f32[54,432]{1,0:T(8,128)S(1)}, u32[]{:S(2)}, u32[]{:S(2)}) collective-permute-start(f32[54,432]{1,0:T(8,128)S(1)} %get-tuple-element.5), channel_id=1, source_target_pairs={{0,1},{1,33},{2,65},{3,97},{4,5},{5,37},{6,69},{7,101},{8,9},{9,41... | collective-permute-start | bytes 279944 | tf_op jit(solution)/shard_map/ppermute | solution.py:288

commit v4 on v3

--- a/solution.py
+++ b/solution.py
@@ -96,7 +96,7 @@
             pltpu.SemaphoreType.DMA((5,)),
             pltpu.SemaphoreType.DMA((tiles,)),
         ],
-        compiler_params=pltpu.CompilerParams(vmem_limit_bytes=24 * 1024 * 1024),
+        compiler_params=pltpu.CompilerParams(vmem_limit_bytes=60 * 1024 * 1024),
         cost_estimate=pl.CostEstimate(flops=1000000, bytes_accessed=3000000, transcendentals=0),
         name="pack",
     )(route, counts, jac, blocks, vis, obs)
@@ -122,31 +122,33 @@
     second = got_ref[source, slot, 29].astype(jnp.float32)
     inverse = inverse_rows(first, second)
     wide = [[jnp.broadcast_to(entry, (4, width)) for entry in line] for line in inverse]
+    rows_ref[27, 0, 0:4] = got_ref[source, slot, 27].astype(jnp.float32)
+    iota = lax.broadcasted_iota(jnp.int32, (8, width), 0).astype(jnp.float32)
+    marks = [jnp.broadcast_to(rows_ref[27, 0, i : i + 1], (8, width)) for i in range(4)]
+    picks = []
+    for b in range(cameras // 8):
+        pick = jnp.full((8, width), 4, jnp.int32)
+        for i in range(4):
+            pick = jnp.where(marks[i] == iota + 8.0 * b, i, pick)
+        picks.append(pick)
+    yield
     for r in range(9):
         factors = [got_ref[source, slot, 3 * r + m].astype(jnp.float32) for m in range(3)]
         for k in range(3):
             value = factors[0] * wide[0][k] + factors[1] * wide[1][k] + factors[2] * wide[2][k]
-            rows_ref[3 * r + k, 0:4] = value.astype(jnp.bfloat16).astype(jnp.float32)
-            rows_ref[3 * r + k, 4:8] = factors[k]
-    rows_ref[27, 0:4] = got_ref[source, slot, 27].astype(jnp.float32)
-    blocks = cameras // 16
-    iota = lax.broadcasted_iota(jnp.int32, (16, width), 0).astype(jnp.float32)
-    masks = []
-    for i in range(4):
-        mark = jnp.broadcast_to(rows_ref[27, i : i + 1], (16, width)).astype(jnp.bfloat16)
-        masks.append([mark == (iota + 16.0 * b).astype(jnp.bfloat16) for b in range(blocks)])
-    zero = jnp.zeros((16, width), jnp.bfloat16)
-    yield
-    for r in range(9):
+            rows_ref[3 * r + k, 0, 0:4] = value
+            rows_ref[3 * r + k, 1, 0:4] = factors[k]
         for k in range(3):
-            for side, out in ((0, left_ref), (4, right_ref)):
-                sums = [zero] * blocks
-                for i in range(4):
-                    row = jnp.broadcast_to(rows_ref[3 * r + k, side + i : side + i + 1], (16, width))
-                    row = row.astype(jnp.bfloat16)
-                    sums = [jnp.where(masks[i][b], row, sums[b]) for b in range(blocks)]
-                for b in range(blocks):
-                    out[pl.ds(r * cameras + 16 * b, 16), pl.ds(column + 2 * k * width, width)] = sums[b]
+            for side, out in enumerate((left_ref, right_ref)):
+                table = rows_ref[3 * r + k, side]
+                for b in range(0, cameras // 8, 2):
+                    pair = [
+                        jnp.take_along_axis(table, picks[b + half], axis=0, mode="promise_in_bounds")
+                        for half in range(2)
+                    ]
+                    out[pl.ds(r * cameras + 8 * b, 16), pl.ds(column + 2 * k * width, width)] = jnp.concatenate(
+                        pair, axis=0
+                    ).astype(jnp.bfloat16)
         yield
 
 
@@ -165,6 +167,7 @@
     sums = (sums[:count], sums[count:])
     part = side // count
     wide = 2 * width
+    rows_ref[...] = jnp.zeros_like(rows_ref)
     for right in rights:
         right[pl.ds(side, 2 * wide - side), :] = jnp.zeros((2 * wide - side, 3 * wide), jnp.bfloat16)
 
@@ -227,7 +230,7 @@
         in_specs=[vmem],
         out_specs=vmem,
         scratch_shapes=[
-            pltpu.VMEM((2, 28, 8, width), jnp.float32),
+            pltpu.VMEM((2, 28, 2, 8, width), jnp.float32),
             pltpu.VMEM((side, 6 * width), jnp.bfloat16),
             pltpu.VMEM((side, 6 * width), jnp.bfloat16),
             pltpu.VMEM((4 * width, 6 * width), jnp.bfloat16),

time: 99.1 us -> 87.5 us (0.88)
  Pallas kernels: 27.9 us -> 21.3 us
  local copies, waits for them, and re-layouts: 5.85 us -> 1.02 us
    pallas_call x1, Pallas kernels: 23.3 us -> 17.3 us  [schur_partial(): pl.pallas_call(functools.partial(schur_kernel, cameras, pieces), out_shap...]
    unnamed x14 -> x2, local copies, waits for them, and re-layouts: 4.84 us -> 0.01 us
where the time goes in v4:
time: 87.5 us; the launch traced here: 87.1 us
  waiting for transfers between devices  36.5 us (42%)
  starting transfers between devices  27.7 us (32%)
  Pallas kernels  21.3 us (24%)
  local copies, waits for them, and re-layouts  1.02 us (1%)
    all_to_all x1, waiting for transfers between devices, local(): lax.all_to_all(packed, ('zb', 'x', 'pair'), split_axis=0, concat_axis=0,...  24.1 us
    pallas_call x1, Pallas kernels, schur_partial(): pl.pallas_call(functools.partial(schur_kernel, cameras, pieces), out_shap...  17.3 us
    ppermute x4, starting transfers between devices, local(): came = lax.ppermute(piece, AXES, links)  14.7 us
    ppermute x4, waiting for transfers between devices, local(): came = lax.ppermute(piece, AXES, links)  11.4 us
    all_to_all x1, starting transfers between devices, local(): lax.all_to_all(packed, ('zb', 'x', 'pair'), split_axis=0, concat_axis=0,...  9.23 us
    pallas_call x1, Pallas kernels, pack(): pl.pallas_call(functools.partial(pack_kernel, site_of), out_shape=jax.Sha...  3.93 us
    ppermute x1, starting transfers between devices, local(): ours = ours + lax.ppermute(theirs, 'layer', [(0, 1), (1, 0)])  3.83 us
  transfers between devices with their start and end apart: 6, of which 3 were waited for; matrix products, arithmetic and copies ran while one was open for 0% of the time, Pallas kernels for 0%

profile of v4, /device:TPU:1, one launch (start us, length us, event | category | flops | bytes accessed | tf_op | source)
XLA Modules:
  0.0 87.1 jit_solution(6016388572044247310)
XLA Ops:
  0.0 3.9 %pack.1 = bf16[32,2,30,4,128]{4,3,2,1,0:T(4,128)(2,1)} custom-call(s32[32]{0:T(128)} %bitcast.23, s32[32]{0:T(128)} %count_hbm.1, bf16[32,27,4,128]{3,2,1,0:T(4,128)(2,1)} %bitcast.18, bf16[6,32,128]{2,1,0:T(8,128)(2,1)} %bitcast.19, s32[32,4,128]{2,1,0:T(4,128)} %vis_hbm.1, s32[32,128]{1,0:T(8,128)} %obs_hbm.1), custom_call_target="tpu_custom_call" | custom-call | flops 1000000 | bytes 3000000 | tf_op jit(solution)/shard_map/pack/pallas_call | solution.py:83
  3.9 9.2 %all-to-all-start = ((bf16[32,2,30,4,128]{4,3,2,1,0:T(4,128)(2,1)}), bf16[32,2,30,4,128]{4,3,2,1,0:T(4,128)(2,1)S(1)}, u32[]{:S(2)}, u32[]{:S(2)}) async-start(bf16[32,2,30,4,128]{4,3,2,1,0:T(4,128)(2,1)} %pack.1), calls=%async_computation | async-start | bytes 3932160 | tf_op jit(solution)/shard_map/all_to_all | solution.py:278
  13.2 24.1 %all-to-all-done.got_ref = bf16[32,2,30,4,128]{4,3,2,1,0:T(4,128)(2,1)S(1)} async-done(((bf16[32,2,30,4,128]{4,3,2,1,0:T(4,128)(2,1)}), bf16[32,2,30,4,128]{4,3,2,1,0:T(4,128)(2,1)S(1)}, u32[]{:S(2)}, u32[]{:S(2)}) %all-to-all-start) | async-done | bytes 1966112 | tf_op jit(solution)/shard_map/all_to_all | solution.py:278
  37.3 17.3 %schur_partial.1 = f32[432,432]{1,0:T(8,128)S(1)} custom-call(bf16[32,2,30,4,128]{4,3,2,1,0:T(4,128)(2,1)S(1)} %all-to-all-done.got_ref), custom_call_target="tpu_custom_call" | custom-call | flops 10000000000 | bytes 3000000 | tf_op jit(solution)/shard_map/schur_partial/pallas_call | solution.py:227
  54.6 0.0 copy-start
  54.6 0.1 reshape_reshape.3
  54.8 3.8 %collective-permute-start = (f32[4,54,432]{2,1,0:T(8,128)S(1)}, f32[4,54,432]{2,1,0:T(8,128)S(1)}, u32[]{:S(2)}, u32[]{:S(2)}) collective-permute-start(f32[4,54,432]{2,1,0:T(8,128)S(1)} %dynamic-slice_bitcast_fusion), channel_id=1, source_target_pairs={{0,128},{128,0},{1,129},{129,1},{2,130},{130,2},{3,131},{131,3},{4... | collective-permute-start | bytes 1119752 | tf_op jit(solution)/shard_map/ppermute | solution.py:283
  58.7 0.0 copy-done
  58.7 0.1 reduce
  58.8 0.1 reshape_squeeze.3
  59.0 1.1 %collective-permute-done = f32[4,54,432]{2,1,0:T(8,128)S(1)} collective-permute-done((f32[4,54,432]{2,1,0:T(8,128)S(1)}, f32[4,54,432]{2,1,0:T(8,128)S(1)}, u32[]{:S(2)}, u32[]{:S(2)}) %collective-permute-start) | collective-permute-done | bytes 373280 | tf_op jit(solution)/shard_map/ppermute | solution.py:283
  60.1 0.1 bitcast_add_fusion
  60.2 1.0 %collective-permute-start.4 = (f32[54,432]{1,0:T(8,128)S(1)}, f32[54,432]{1,0:T(8,128)S(1)}, u32[]{:S(2)}, u32[]{:S(2)}) collective-permute-start(f32[54,432]{1,0:T(8,128)S(1)} %get-tuple-element.6), channel_id=1, source_target_pairs={{0,3},{1,35},{2,67},{3,99},{4,7},{5,39},{6,71},{7,103},{8,11},{9,4... | collective-permute-start | bytes 279944 | tf_op jit(solution)/shard_map/ppermute | solution.py:291
  61.1 8.8 %collective-permute-start.3 = (f32[54,432]{1,0:T(8,128)S(1)}, f32[54,432]{1,0:T(8,128)S(1)}, u32[]{:S(2)}, u32[]{:S(2)}) collective-permute-start(f32[54,432]{1,0:T(8,128)S(1)} %get-tuple-element.7), channel_id=1, source_target_pairs={{0,2},{1,34},{2,66},{3,98},{4,6},{5,38},{6,70},{7,102},{8,10},{9,4... | collective-permute-start | bytes 279944 | tf_op jit(solution)/shard_map/ppermute | solution.py:291
  70.0 0.7 collective-permute-start.1
  70.6 4.2 %collective-permute-start.2 = (f32[54,432]{1,0:T(8,128)S(1)}, f32[54,432]{1,0:T(8,128)S(1)}, u32[]{:S(2)}, u32[]{:S(2)}) collective-permute-start(f32[54,432]{1,0:T(8,128)S(1)} %get-tuple-element.5), channel_id=1, source_target_pairs={{0,1},{1,33},{2,65},{3,97},{4,5},{5,37},{6,69},{7,101},{8,9},{9,41... | collective-permute-start | bytes 279944 | tf_op jit(solution)/shard_map/ppermute | solution.py:291
  74.9 0.0 collective-permute-done.4
  74.9 0.0 collective-permute-done.3
  74.9 0.0 collective-permute-done.1
  74.9 11.4 %collective-permute-done.2 = f32[54,432]{1,0:T(8,128)S(1)} collective-permute-done((f32[54,432]{1,0:T(8,128)S(1)}, f32[54,432]{1,0:T(8,128)S(1)}, u32[]{:S(2)}, u32[]{:S(2)}) %collective-permute-start.2) | collective-permute-done | bytes 93344 | tf_op jit(solution)/shard_map/ppermute | solution.py:291
  86.3 0.1 add_subtract_fusion
  86.4 0.7 broadcast_in_dim.39
  (8 shorter events, 0.2 us)
Async XLA Ops:
  3.9 33.3 %all-to-all-start = ((bf16[32,2,30,4,128]{4,3,2,1,0:T(4,128)(2,1)}), bf16[32,2,30,4,128]{4,3,2,1,0:T(4,128)(2,1)S(1)}, u32[]{:S(2)}, u32[]{:S(2)}) async-start(bf16[32,2,30,4,128]{4,3,2,1,0:T(4,128)(2,1)} %pack.1), calls=%async_computation | async-start | bytes 3932160 | tf_op jit(solution)/shard_map/all_to_all | solution.py:278
  54.6 4.1 %copy-start = (f32[1,9,9,48]{3,0,2,1:T(1,128)S(1)}, f32[1,9,9,48]{3,0,2,1:T(1,128)}, u32[]{:S(2)}) copy-start(f32[1,9,9,48]{3,0,2,1:T(1,128)} %param.13) | copy-start | bytes 46660
  54.8 5.3 %collective-permute-start = (f32[4,54,432]{2,1,0:T(8,128)S(1)}, f32[4,54,432]{2,1,0:T(8,128)S(1)}, u32[]{:S(2)}, u32[]{:S(2)}) collective-permute-start(f32[4,54,432]{2,1,0:T(8,128)S(1)} %dynamic-slice_bitcast_fusion), channel_id=1, source_target_pairs={{0,128},{128,0},{1,129},{129,1},{2,130},{130,2},{3,131},{131,3},{4... | collective-permute-start | bytes 1119752 | tf_op jit(solution)/shard_map/ppermute | solution.py:283
  60.2 14.7 %collective-permute-start.4 = (f32[54,432]{1,0:T(8,128)S(1)}, f32[54,432]{1,0:T(8,128)S(1)}, u32[]{:S(2)}, u32[]{:S(2)}) collective-permute-start(f32[54,432]{1,0:T(8,128)S(1)} %get-tuple-element.6), channel_id=1, source_target_pairs={{0,3},{1,35},{2,67},{3,99},{4,7},{5,39},{6,71},{7,103},{8,11},{9,4... | collective-permute-start | bytes 279944 | tf_op jit(solution)/shard_map/ppermute | solution.py:291
  61.1 13.7 %collective-permute-start.3 = (f32[54,432]{1,0:T(8,128)S(1)}, f32[54,432]{1,0:T(8,128)S(1)}, u32[]{:S(2)}, u32[]{:S(2)}) collective-permute-start(f32[54,432]{1,0:T(8,128)S(1)} %get-tuple-element.7), channel_id=1, source_target_pairs={{0,2},{1,34},{2,66},{3,98},{4,6},{5,38},{6,70},{7,102},{8,10},{9,4... | collective-permute-start | bytes 279944 | tf_op jit(solution)/shard_map/ppermute | solution.py:291
  70.0 4.9 %collective-permute-start.1 = (f32[54,432]{1,0:T(8,128)S(1)}, f32[54,432]{1,0:T(8,128)S(1)}, u32[]{:S(2)}, u32[]{:S(2)}) collective-permute-start(f32[54,432]{1,0:T(8,128)S(1)} %get-tuple-element.8), channel_id=1, source_target_pairs={{0,0},{1,32},{2,64},{3,96},{4,4},{5,36},{6,68},{7,100},{8,8},{9,40... | collective-permute-start | bytes 279944 | tf_op jit(solution)/shard_map/ppermute | solution.py:291
  70.6 15.6 %collective-permute-start.2 = (f32[54,432]{1,0:T(8,128)S(1)}, f32[54,432]{1,0:T(8,128)S(1)}, u32[]{:S(2)}, u32[]{:S(2)}) collective-permute-start(f32[54,432]{1,0:T(8,128)S(1)} %get-tuple-element.5), channel_id=1, source_target_pairs={{0,1},{1,33},{2,65},{3,97},{4,5},{5,37},{6,69},{7,101},{8,9},{9,41... | collective-permute-start | bytes 279944 | tf_op jit(solution)/shard_map/ppermute | solution.py:291

commit v5 on v4

--- a/solution.py
+++ b/solution.py
@@ -134,13 +134,12 @@
     yield
     for r in range(9):
         factors = [got_ref[source, slot, 3 * r + m].astype(jnp.float32) for m in range(3)]
+        values = [
+            factors[0] * wide[0][k] + factors[1] * wide[1][k] + factors[2] * wide[2][k] for k in range(3)
+        ]
         for k in range(3):
-            value = factors[0] * wide[0][k] + factors[1] * wide[1][k] + factors[2] * wide[2][k]
-            rows_ref[3 * r + k, 0, 0:4] = value
-            rows_ref[3 * r + k, 1, 0:4] = factors[k]
-        for k in range(3):
-            for side, out in enumerate((left_ref, right_ref)):
-                table = rows_ref[3 * r + k, side]
+            for value, out in ((values[k], left_ref), (factors[k], right_ref)):
+                table = jnp.concatenate([value, jnp.zeros_like(value)], axis=0)
                 for b in range(0, cameras // 8, 2):
                     pair = [
                         jnp.take_along_axis(table, picks[b + half], axis=0, mode="promise_in_bounds")
@@ -268,7 +267,7 @@
 
     def site_of(group):
         side_z = group // across % near
-        y = (group // (across * near) + 2 * lax.axis_index("zp") + 2 * side_z) % pairs
+        y = (group // (across * near) + pairs - lax.axis_index("zp") + 2 * side_z) % pairs
         return side_z * (across * pairs) + group % across * pairs + y
 
     packed = pack(
@@ -277,7 +276,7 @@
     )
     got = lax.all_to_all(packed, ("zb", "x", "pair"), split_axis=0, concat_axis=0, tiled=True)
     partial_value = schur_partial(got, cameras, shares).reshape(layers, pairs, side // shares, side)
-    layer, plane = lax.axis_index("layer"), lax.axis_index("zp")
+    layer, row = lax.axis_index("layer"), lax.axis_index("pair")
     theirs = lax.dynamic_index_in_dim(partial_value, 1 - layer, 0, keepdims=False)
     ours = lax.dynamic_index_in_dim(partial_value, layer, 0, keepdims=False)
     ours = ours + lax.ppermute(theirs, "layer", [(0, 1), (1, 0)])
@@ -286,12 +285,12 @@
         links = []
         for source in itertools.product(*(range(size) for size in sizes)):
             c, zp, zb, x, y = source
-            links.append((flat(source, sizes), flat((c, (y + 2 * zp + 2 * zb) % far, zb, x, zp ^ turn), sizes)))
-        piece = lax.dynamic_index_in_dim(ours, plane ^ turn, 0, keepdims=False)
+            links.append((flat(source, sizes), flat((c, (y + zp + 2 * zb) % far, zb, x, y ^ turn), sizes)))
+        piece = lax.dynamic_slice_in_dim(ours, row ^ turn, 1, 0)
         came = lax.ppermute(piece, AXES, links)
         total = came if total is None else total + came
-    share = layer * pairs + lax.axis_index("pair")
-    return (own_blocks(camera_blocks, share, side // shares) - total)[None]
+    share = layer * pairs + row
+    return own_blocks(camera_blocks, share, side // shares)[None] - total
 
 
 def flat(place, sizes):

time: 87.5 us -> 87.5 us (level)
  the two profiles are of different devices: /device:TPU:1 before, /device:TPU:25 now
where the time goes in v5:
time: 87.5 us; the launch traced here: 87.1 us
  waiting for transfers between devices  40.6 us (46%)
  starting transfers between devices  25.6 us (29%)
  Pallas kernels  19.2 us (22%)
  local copies, waits for them, and re-layouts  1.05 us (1%)
    all_to_all x1, waiting for transfers between devices, local(): lax.all_to_all(packed, ('zb', 'x', 'pair'), split_axis=0, concat_axis=0,...  24 us
    ppermute x4, waiting for transfers between devices, local(): came = lax.ppermute(piece, AXES, links)  15.5 us
    pallas_call x1, Pallas kernels, schur_partial(): pl.pallas_call(functools.partial(schur_kernel, cameras, pieces), out_shap...  15.3 us
    ppermute x4, starting transfers between devices, local(): came = lax.ppermute(piece, AXES, links)  15.2 us
    all_to_all x1, starting transfers between devices, local(): lax.all_to_all(packed, ('zb', 'x', 'pair'), split_axis=0, concat_axis=0,...  8.11 us
    pallas_call x1, Pallas kernels, pack(): pl.pallas_call(functools.partial(pack_kernel, site_of), out_shape=jax.Sha...  3.92 us
    ppermute x1, starting transfers between devices, local(): ours = ours + lax.ppermute(theirs, 'layer', [(0, 1), (1, 0)])  2.29 us
  transfers between devices with their start and end apart: 6, of which 3 were waited for; matrix products, arithmetic and copies ran while one was open for 0% of the time, Pallas kernels for 0%

profile of v5, /device:TPU:25, one launch (start us, length us, event | category | flops | bytes accessed | tf_op | source)
XLA Modules:
  0.0 87.1 jit_solution(9773553148617184761)
XLA Ops:
  0.0 3.9 %pack.1 = bf16[32,2,30,4,128]{4,3,2,1,0:T(4,128)(2,1)} custom-call(s32[32]{0:T(128)} %bitcast.15, s32[32]{0:T(128)} %count_hbm.1, bf16[32,27,4,128]{3,2,1,0:T(4,128)(2,1)} %bitcast.10, bf16[6,32,128]{2,1,0:T(8,128)(2,1)} %bitcast.11, s32[32,4,128]{2,1,0:T(4,128)} %vis_hbm.1, s32[32,128]{1,0:T(8,128)} %obs_hbm.1), custom_call_target="tpu_custom_call" | custom-call | flops 1000000 | bytes 3000000 | tf_op jit(solution)/shard_map/pack/pallas_call | solution.py:83
  3.9 8.1 %all-to-all-start = ((bf16[32,2,30,4,128]{4,3,2,1,0:T(4,128)(2,1)}), bf16[32,2,30,4,128]{4,3,2,1,0:T(4,128)(2,1)S(1)}, u32[]{:S(2)}, u32[]{:S(2)}) async-start(bf16[32,2,30,4,128]{4,3,2,1,0:T(4,128)(2,1)} %pack.1), calls=%async_computation | async-start | bytes 3932160 | tf_op jit(solution)/shard_map/all_to_all | solution.py:277
  12.1 24.0 %all-to-all-done.got_ref = bf16[32,2,30,4,128]{4,3,2,1,0:T(4,128)(2,1)S(1)} async-done(((bf16[32,2,30,4,128]{4,3,2,1,0:T(4,128)(2,1)}), bf16[32,2,30,4,128]{4,3,2,1,0:T(4,128)(2,1)S(1)}, u32[]{:S(2)}, u32[]{:S(2)}) %all-to-all-start) | async-done | bytes 1966112 | tf_op jit(solution)/shard_map/all_to_all | solution.py:277
  36.1 15.3 %schur_partial.1 = f32[432,432]{1,0:T(8,128)S(1)} custom-call(bf16[32,2,30,4,128]{4,3,2,1,0:T(4,128)(2,1)S(1)} %all-to-all-done.got_ref), custom_call_target="tpu_custom_call" | custom-call | flops 10000000000 | bytes 3000000 | tf_op jit(solution)/shard_map/schur_partial/pallas_call | solution.py:226
  51.4 0.0 copy-start
  51.4 0.1 reshape_reshape.3
  51.6 2.3 %collective-permute-start = (f32[4,54,432]{2,1,0:T(8,128)S(1)}, f32[4,54,432]{2,1,0:T(8,128)S(1)}, u32[]{:S(2)}, u32[]{:S(2)}) collective-permute-start(f32[4,54,432]{2,1,0:T(8,128)S(1)} %dynamic-slice_bitcast_fusion), channel_id=1, source_target_pairs={{0,128},{128,0},{1,129},{129,1},{2,130},{130,2},{3,131},{131,3},{4... | collective-permute-start | bytes 1119752 | tf_op jit(solution)/shard_map/ppermute | solution.py:282
  54.0 0.0 copy-done
  54.0 0.1 reduce
  54.1 0.1 reshape_squeeze.3
  54.3 1.1 %collective-permute-done = f32[4,54,432]{2,1,0:T(8,128)S(1)} collective-permute-done((f32[4,54,432]{2,1,0:T(8,128)S(1)}, f32[4,54,432]{2,1,0:T(8,128)S(1)}, u32[]{:S(2)}, u32[]{:S(2)}) %collective-permute-start) | collective-permute-done | bytes 373280 | tf_op jit(solution)/shard_map/ppermute | solution.py:282
  55.3 0.1 bitcast_add_fusion
  55.5 6.7 %collective-permute-start.4 = (f32[1,54,432]{2,1,0:T(8,128)S(1)}, f32[1,54,432]{2,1,0:T(8,128)S(1)}, u32[]{:S(2)}, u32[]{:S(2)}) collective-permute-start(f32[1,54,432]{2,1,0:T(8,128)S(1)} %get-tuple-element.6), channel_id=1, source_target_pairs={{0,3},{1,34},{2,65},{3,96},{4,7},{5,38},{6,69},{7,100},{8,11},{9,4... | collective-permute-start | bytes 279944 | tf_op jit(solution)/shard_map/ppermute | solution.py:290
  62.2 0.0 collective-permute-start.3
  62.2 4.9 %collective-permute-start.1 = (f32[1,54,432]{2,1,0:T(8,128)S(1)}, f32[1,54,432]{2,1,0:T(8,128)S(1)}, u32[]{:S(2)}, u32[]{:S(2)}) collective-permute-start(f32[1,54,432]{2,1,0:T(8,128)S(1)} %get-tuple-element.8), channel_id=1, source_target_pairs={{0,0},{1,33},{2,66},{3,99},{4,4},{5,37},{6,70},{7,103},{8,8},{9,41... | collective-permute-start | bytes 279944 | tf_op jit(solution)/shard_map/ppermute | solution.py:290
  67.1 3.6 %collective-permute-start.2 = (f32[1,54,432]{2,1,0:T(8,128)S(1)}, f32[1,54,432]{2,1,0:T(8,128)S(1)}, u32[]{:S(2)}, u32[]{:S(2)}) collective-permute-start(f32[1,54,432]{2,1,0:T(8,128)S(1)} %get-tuple-element.5), channel_id=1, source_target_pairs={{0,1},{1,32},{2,67},{3,98},{4,5},{5,36},{6,71},{7,102},{8,9},{9,40... | collective-permute-start | bytes 279944 | tf_op jit(solution)/shard_map/ppermute | solution.py:290
  70.7 0.0 collective-permute-done.4
  70.7 0.0 collective-permute-done.3
  70.7 0.0 collective-permute-done.1
  70.7 15.5 %collective-permute-done.2 = f32[1,54,432]{2,1,0:T(8,128)S(1)} collective-permute-done((f32[1,54,432]{2,1,0:T(8,128)S(1)}, f32[1,54,432]{2,1,0:T(8,128)S(1)}, u32[]{:S(2)}, u32[]{:S(2)}) %collective-permute-start.2) | collective-permute-done | bytes 93344 | tf_op jit(solution)/shard_map/ppermute | solution.py:290
  86.2 0.1 add_subtract_fusion
  86.4 0.8 copy.10
  (8 shorter events, 0.2 us)
Async XLA Ops:
  3.9 32.2 %all-to-all-start = ((bf16[32,2,30,4,128]{4,3,2,1,0:T(4,128)(2,1)}), bf16[32,2,30,4,128]{4,3,2,1,0:T(4,128)(2,1)S(1)}, u32[]{:S(2)}, u32[]{:S(2)}) async-start(bf16[32,2,30,4,128]{4,3,2,1,0:T(4,128)(2,1)} %pack.1), calls=%async_computation | async-start | bytes 3932160 | tf_op jit(solution)/shard_map/all_to_all | solution.py:277
  51.4 2.5 %copy-start = (f32[1,9,9,48]{3,0,2,1:T(1,128)S(1)}, f32[1,9,9,48]{3,0,2,1:T(1,128)}, u32[]{:S(2)}) copy-start(f32[1,9,9,48]{3,0,2,1:T(1,128)} %param.13) | copy-start | bytes 46660
  51.6 3.7 %collective-permute-start = (f32[4,54,432]{2,1,0:T(8,128)S(1)}, f32[4,54,432]{2,1,0:T(8,128)S(1)}, u32[]{:S(2)}, u32[]{:S(2)}) collective-permute-start(f32[4,54,432]{2,1,0:T(8,128)S(1)} %dynamic-slice_bitcast_fusion), channel_id=1, source_target_pairs={{0,128},{128,0},{1,129},{129,1},{2,130},{130,2},{3,131},{131,3},{4... | collective-permute-start | bytes 1119752 | tf_op jit(solution)/shard_map/ppermute | solution.py:282
  55.5 15.3 %collective-permute-start.4 = (f32[1,54,432]{2,1,0:T(8,128)S(1)}, f32[1,54,432]{2,1,0:T(8,128)S(1)}, u32[]{:S(2)}, u32[]{:S(2)}) collective-permute-start(f32[1,54,432]{2,1,0:T(8,128)S(1)} %get-tuple-element.6), channel_id=1, source_target_pairs={{0,3},{1,34},{2,65},{3,96},{4,7},{5,38},{6,69},{7,100},{8,11},{9,4... | collective-permute-start | bytes 279944 | tf_op jit(solution)/shard_map/ppermute | solution.py:290
  62.2 8.5 %collective-permute-start.3 = (f32[1,54,432]{2,1,0:T(8,128)S(1)}, f32[1,54,432]{2,1,0:T(8,128)S(1)}, u32[]{:S(2)}, u32[]{:S(2)}) collective-permute-start(f32[1,54,432]{2,1,0:T(8,128)S(1)} %get-tuple-element.7), channel_id=1, source_target_pairs={{0,2},{1,35},{2,64},{3,97},{4,6},{5,39},{6,68},{7,101},{8,10},{9,4... | collective-permute-start | bytes 279944 | tf_op jit(solution)/shard_map/ppermute | solution.py:290
  62.2 8.5 %collective-permute-start.1 = (f32[1,54,432]{2,1,0:T(8,128)S(1)}, f32[1,54,432]{2,1,0:T(8,128)S(1)}, u32[]{:S(2)}, u32[]{:S(2)}) collective-permute-start(f32[1,54,432]{2,1,0:T(8,128)S(1)} %get-tuple-element.8), channel_id=1, source_target_pairs={{0,0},{1,33},{2,66},{3,99},{4,4},{5,37},{6,70},{7,103},{8,8},{9,41... | collective-permute-start | bytes 279944 | tf_op jit(solution)/shard_map/ppermute | solution.py:290
  67.1 19.2 %collective-permute-start.2 = (f32[1,54,432]{2,1,0:T(8,128)S(1)}, f32[1,54,432]{2,1,0:T(8,128)S(1)}, u32[]{:S(2)}, u32[]{:S(2)}) collective-permute-start(f32[1,54,432]{2,1,0:T(8,128)S(1)} %get-tuple-element.5), channel_id=1, source_target_pairs={{0,1},{1,32},{2,67},{3,98},{4,5},{5,36},{6,71},{7,102},{8,9},{9,40... | collective-permute-start | bytes 279944 | tf_op jit(solution)/shard_map/ppermute | solution.py:290

commit v6 on v5

--- a/solution.py
+++ b/solution.py
@@ -157,7 +157,7 @@
     pl.run_scoped(functools.partial(schur_body, cameras, got_ref, out_ref, *scratch), *sums)
 
 
-def schur_body(cameras, got_ref, out_ref, rows_ref, left_a, left_b, right_a, right_b, *sums):
+def schur_body(cameras, got_ref, out_ref, total_ref, rows_ref, left_a, left_b, right_a, right_b, *sums):
     sources = got_ref.shape[0]
     width = got_ref.shape[4]
     side = 9 * cameras
@@ -214,8 +214,61 @@
     lax.fori_loop(0, sources // 2, step, 0)
     for piece in range(count):
         rows = pl.ds(piece * part, part)
-        out_ref[rows, 0:wide] = pltpu.matmul_pop(sums[0][piece])
-        out_ref[rows, wide:side] = pltpu.matmul_pop(sums[1][piece])[:, : side - wide]
+        total_ref[rows, 0:wide] = pltpu.matmul_pop(sums[0][piece])
+        total_ref[rows, wide:side] = pltpu.matmul_pop(sums[1][piece])[:, : side - wide]
+    share = side // out_ref.shape[0]
+    full, half = side // width, share // 2
+    rest = side - full * width
+    for piece in range(out_ref.shape[0]):
+        for lane in range(full):
+            out_ref[piece, pl.ds(lane * share, share)] = total_ref[
+                pl.ds(piece * share, share), lane * width : (lane + 1) * width
+            ]
+        for step in range(2):
+            out_ref[piece, pl.ds(full * share, half), step * rest : (step + 1) * rest] = total_ref[
+                pl.ds(piece * share + step * half, half), full * width : side
+            ]
+
+
+def finish_kernel(cameras, lines_ref, *refs):
+    pieces, out_ref = refs[:-1], refs[-1]
+    share, side = out_ref.shape
+    width = pieces[0].shape[2]
+    total = pieces[0][0]
+    for piece in pieces[1:]:
+        total = total + piece[0]
+    start = (lax.axis_index("layer") * lax.axis_size("pair") + lax.axis_index("pair")) * share
+    first = start // cameras
+    row = start + lax.broadcasted_iota(jnp.int32, (share, side), 0)
+    column = lax.broadcasted_iota(jnp.int32, (share, side), 1)
+    own = jnp.zeros((share, side), jnp.float32)
+    for step in range(-(-share // cameras) + 1):
+        line = lines_ref[pl.ds(jnp.minimum(first + step, lines_ref.shape[0] - 1), 1), :]
+        own = jnp.where(row // cameras == first + step, jnp.broadcast_to(line, (share, side)), own)
+    own = jnp.where(row % cameras == column % cameras, own, 0.0)
+    full, half = side // width, share // 2
+    rest = side - full * width
+    for lane in range(full):
+        columns = slice(lane * width, (lane + 1) * width)
+        out_ref[:, columns] = own[:, columns] - total[lane * share : (lane + 1) * share]
+    for step in range(2):
+        rows, columns = slice(step * half, (step + 1) * half), slice(full * width, side)
+        out_ref[rows, columns] = (
+            own[rows, columns] - total[full * share : full * share + half, step * rest : (step + 1) * rest]
+        )
+
+
+def finish(lines, pieces, cameras, share):
+    vmem = pl.BlockSpec(memory_space=pltpu.VMEM)
+    return pl.pallas_call(
+        functools.partial(finish_kernel, cameras),
+        out_shape=jax.ShapeDtypeStruct((share, lines.shape[1]), jnp.float32),
+        in_specs=[vmem] * (1 + len(pieces)),
+        out_specs=vmem,
+        compiler_params=pltpu.CompilerParams(vmem_limit_bytes=16 * 1024 * 1024),
+        cost_estimate=pl.CostEstimate(flops=200000, bytes_accessed=500000, transcendentals=0),
+        name="finish",
+    )(lines, *pieces)
 
 
 def schur_partial(got, cameras, shares):
@@ -223,12 +276,15 @@
     side = 9 * cameras
     pieces = 9
     vmem = pl.BlockSpec(memory_space=pltpu.VMEM)
-    out = pl.pallas_call(
+    share = side // shares
+    lines = side // width * share + share // 2
+    return pl.pallas_call(
         functools.partial(schur_kernel, cameras, pieces),
-        out_shape=jax.ShapeDtypeStruct((side, side), jnp.float32),
+        out_shape=jax.ShapeDtypeStruct((shares, lines + -lines % 8, width), jnp.float32),
         in_specs=[vmem],
         out_specs=vmem,
         scratch_shapes=[
+            pltpu.VMEM((side, side), jnp.float32),
             pltpu.VMEM((2, 28, 2, 8, width), jnp.float32),
             pltpu.VMEM((side, 6 * width), jnp.bfloat16),
             pltpu.VMEM((side, 6 * width), jnp.bfloat16),
@@ -239,21 +295,6 @@
         cost_estimate=pl.CostEstimate(flops=10000000000, bytes_accessed=3000000, transcendentals=0),
         name="schur_partial",
     )(got)
-    return out.reshape(shares, side // shares, side)
-
-
-def own_blocks(camera_blocks, share, share_rows):
-    cameras = camera_blocks.shape[3]
-    side = 9 * cameras
-    row = share * share_rows + lax.broadcasted_iota(jnp.int32, (share_rows, side), 0)
-    column = lax.broadcasted_iota(jnp.int32, (share_rows, side), 1)
-    lines = camera_blocks[0].reshape(9, side)
-    first = share * share_rows // cameras
-    own = jnp.zeros((share_rows, side), jnp.float32)
-    for step in range(-(-share_rows // cameras) + 1):
-        line = lax.dynamic_slice_in_dim(lines, jnp.minimum(first + step, 8), 1, 0)
-        own = jnp.where(row // cameras == first + step, line, own)
-    return jnp.where(row % cameras == column % cameras, own, 0.0)
 
 
 AXES = ("layer", "zp", "zb", "x", "pair")
@@ -274,23 +315,24 @@
         jac_blocks.transpose(0, 2, 1, 3), point_blocks.transpose(1, 0, 2), visibility, obs_count, tile_count,
         route[:, 0], near * across * pairs, site_of,
     )
+    lines = camera_blocks[0].reshape(9, side)
     got = lax.all_to_all(packed, ("zb", "x", "pair"), split_axis=0, concat_axis=0, tiled=True)
-    partial_value = schur_partial(got, cameras, shares).reshape(layers, pairs, side // shares, side)
+    got, lines = lax.optimization_barrier((got, lines))
+    partial_value = schur_partial(got, cameras, shares)
+    partial_value = partial_value.reshape((layers, pairs) + partial_value.shape[1:])
     layer, row = lax.axis_index("layer"), lax.axis_index("pair")
     theirs = lax.dynamic_index_in_dim(partial_value, 1 - layer, 0, keepdims=False)
     ours = lax.dynamic_index_in_dim(partial_value, layer, 0, keepdims=False)
     ours = ours + lax.ppermute(theirs, "layer", [(0, 1), (1, 0)])
-    total = None
+    pieces = []
     for turn in range(far):
         links = []
         for source in itertools.product(*(range(size) for size in sizes)):
             c, zp, zb, x, y = source
             links.append((flat(source, sizes), flat((c, (y + zp + 2 * zb) % far, zb, x, y ^ turn), sizes)))
         piece = lax.dynamic_slice_in_dim(ours, row ^ turn, 1, 0)
-        came = lax.ppermute(piece, AXES, links)
-        total = came if total is None else total + came
-    share = layer * pairs + row
-    return own_blocks(camera_blocks, share, side // shares)[None] - total
+        pieces.append(lax.ppermute(piece, AXES, links))
+    return finish(lines, pieces, cameras, side // shares)[None]
 
 
 def flat(place, sizes):

time: 87.5 us -> 85.9 us (0.982)
  the two profiles are of different devices: /device:TPU:25 before, /device:TPU:8 now
where the time goes in v6:
time: 85.9 us; the launch traced here: 85.5 us
  waiting for transfers between devices  43.1 us (50%)
  starting transfers between devices  21.8 us (25%)
  Pallas kernels  19.4 us (23%)
  local copies, waits for them, and re-layouts  0.92 us (1%)
    all_to_all x1, waiting for transfers between devices, local(): lax.all_to_all(packed, ('zb', 'x', 'pair'), split_axis=0, concat_axis=0,...  25.3 us
    ppermute x4, waiting for transfers between devices, local(): pieces.append(lax.ppermute(piece, AXES, links))  16 us
    pallas_call x1, Pallas kernels, schur_partial(): pl.pallas_call(functools.partial(schur_kernel, cameras, pieces), out_shap...  15.4 us
    ppermute x4, starting transfers between devices, local(): pieces.append(lax.ppermute(piece, AXES, links))  12.8 us
    all_to_all x1, starting transfers between devices, local(): lax.all_to_all(packed, ('zb', 'x', 'pair'), split_axis=0, concat_axis=0,...  8.9 us
    pallas_call x1, Pallas kernels, pack(): pl.pallas_call(functools.partial(pack_kernel, site_of), out_shape=jax.Sha...  3.95 us
  transfers between devices with their start and end apart: 6, of which 4 were waited for; matrix products, arithmetic and copies ran while one was open for 0% of the time, Pallas kernels for 0%

profile of v6, /device:TPU:8, one launch (start us, length us, event | category | flops | bytes accessed | tf_op | source)
XLA Modules:
  0.0 85.5 jit_solution(9727338457304666448)
XLA Ops:
  0.0 3.9 %pack.1 = bf16[32,2,30,4,128]{4,3,2,1,0:T(4,128)(2,1)} custom-call(s32[32]{0:T(128)} %bitcast.14, s32[32]{0:T(128)} %count_hbm.1, bf16[32,27,4,128]{3,2,1,0:T(4,128)(2,1)} %bitcast.12, bf16[6,32,128]{2,1,0:T(8,128)(2,1)} %bitcast.13, s32[32,4,128]{2,1,0:T(4,128)} %vis_hbm.1, s32[32,128]{1,0:T(8,128)} %obs_hbm.1), custom_call_target="tpu_custom_call" | custom-call | flops 1000000 | bytes 3000000 | tf_op jit(solution)/shard_map/pack/pallas_call | solution.py:83
  4.0 0.0 copy-start
  4.0 8.9 %all-to-all-start = ((bf16[32,2,30,4,128]{4,3,2,1,0:T(4,128)(2,1)}), bf16[32,2,30,4,128]{4,3,2,1,0:T(4,128)(2,1)S(1)}, u32[]{:S(2)}, u32[]{:S(2)}) async-start(bf16[32,2,30,4,128]{4,3,2,1,0:T(4,128)(2,1)} %pack.1), calls=%async_computation | async-start | bytes 3932160 | tf_op jit(solution)/shard_map/all_to_all | solution.py:319
  12.9 0.0 copy-done
  12.9 0.1 reduce
  13.0 0.1 reshape_squeeze.3.lines_ref
  13.1 25.3 %all-to-all-done.got_ref = bf16[32,2,30,4,128]{4,3,2,1,0:T(4,128)(2,1)S(1)} async-done(((bf16[32,2,30,4,128]{4,3,2,1,0:T(4,128)(2,1)}), bf16[32,2,30,4,128]{4,3,2,1,0:T(4,128)(2,1)S(1)}, u32[]{:S(2)}, u32[]{:S(2)}) %all-to-all-start) | async-done | bytes 1966112 | tf_op jit(solution)/shard_map/all_to_all | solution.py:319
  38.4 15.4 %schur_partial.1 = f32[8,192,128]{2,1,0:T(8,128)S(1)} custom-call(bf16[32,2,30,4,128]{4,3,2,1,0:T(4,128)(2,1)S(1)} %all-to-all-done.got_ref), custom_call_target="tpu_custom_call" | custom-call | flops 10000000000 | bytes 3000000 | tf_op jit(solution)/shard_map/schur_partial/pallas_call | solution.py:281
  53.9 0.1 collective-permute-start
  54.0 1.7 %collective-permute-done = f32[4,192,128]{2,1,0:T(8,128)S(1)} collective-permute-done((f32[4,192,128]{2,1,0:T(8,128)S(1)}, f32[4,192,128]{2,1,0:T(8,128)S(1)}, u32[]{:S(2)}, u32[]{:S(2)}) %collective-permute-start) | collective-permute-done | bytes 393248 | tf_op jit(solution)/shard_map/ppermute | solution.py:326
  55.8 5.2 %collective-permute-start.1 = (f32[1,192,128]{2,1,0:T(8,128)S(1)}, f32[1,192,128]{2,1,0:T(8,128)S(1)}, u32[]{:S(2)}, u32[]{:S(2)}) collective-permute-start(f32[1,192,128]{2,1,0:T(8,128)S(1)} %get-tuple-element.12), channel_id=1, source_target_pairs={{0,0},{1,33},{2,66},{3,99},{4,4},{5,37},{6,70},{7,103},{8,8},{9,41... | collective-permute-start | bytes 294920 | tf_op jit(solution)/shard_map/ppermute | solution.py:334
  61.0 0.1 collective-permute-start.2
  61.1 7.5 %collective-permute-start.3 = (f32[1,192,128]{2,1,0:T(8,128)S(1)}, f32[1,192,128]{2,1,0:T(8,128)S(1)}, u32[]{:S(2)}, u32[]{:S(2)}) collective-permute-start(f32[1,192,128]{2,1,0:T(8,128)S(1)} %get-tuple-element.10), channel_id=1, source_target_pairs={{0,2},{1,35},{2,64},{3,97},{4,6},{5,39},{6,68},{7,101},{8,10},{9,4... | collective-permute-start | bytes 294920 | tf_op jit(solution)/shard_map/ppermute | solution.py:334
  68.6 0.0 collective-permute-start.4
  68.6 0.0 collective-permute-done.1.refs_0_
  68.6 0.0 collective-permute-done.2.refs_1_
  68.6 5.7 %collective-permute-done.3.refs_2_ = f32[1,192,128]{2,1,0:T(8,128)S(1)} collective-permute-done((f32[1,192,128]{2,1,0:T(8,128)S(1)}, f32[1,192,128]{2,1,0:T(8,128)S(1)}, u32[]{:S(2)}, u32[]{:S(2)}) %collective-permute-start.3) | collective-permute-done | bytes 98336 | tf_op jit(solution)/shard_map/ppermute | solution.py:334
  74.3 10.4 %collective-permute-done.4.refs_3_ = f32[1,192,128]{2,1,0:T(8,128)S(1)} collective-permute-done((f32[1,192,128]{2,1,0:T(8,128)S(1)}, f32[1,192,128]{2,1,0:T(8,128)S(1)}, u32[]{:S(2)}, u32[]{:S(2)}) %collective-permute-start.4) | collective-permute-done | bytes 98336 | tf_op jit(solution)/shard_map/ppermute | solution.py:334
  84.7 0.1 finish.1
  84.7 0.8 copy.8
  (3 shorter events, 0.1 us)
Async XLA Ops:
  4.0 8.9 %copy-start = (f32[1,9,9,48]{3,0,2,1:T(1,128)S(1)}, f32[1,9,9,48]{3,0,2,1:T(1,128)}, u32[]{:S(2)}) copy-start(f32[1,9,9,48]{3,0,2,1:T(1,128)} %param.13) | copy-start | bytes 46660
  4.0 34.5 %all-to-all-start = ((bf16[32,2,30,4,128]{4,3,2,1,0:T(4,128)(2,1)}), bf16[32,2,30,4,128]{4,3,2,1,0:T(4,128)(2,1)S(1)}, u32[]{:S(2)}, u32[]{:S(2)}) async-start(bf16[32,2,30,4,128]{4,3,2,1,0:T(4,128)(2,1)} %pack.1), calls=%async_computation | async-start | bytes 3932160 | tf_op jit(solution)/shard_map/all_to_all | solution.py:319
  53.9 1.8 %collective-permute-start = (f32[4,192,128]{2,1,0:T(8,128)S(1)}, f32[4,192,128]{2,1,0:T(8,128)S(1)}, u32[]{:S(2)}, u32[]{:S(2)}) collective-permute-start(f32[4,192,128]{2,1,0:T(8,128)S(1)} %dynamic-slice_bitcast_fusion), channel_id=1, source_target_pairs={{0,128},{128,0},{1,129},{129,1},{2,130},{130,2},{3,131},{131,3},{4... | collective-permute-start | bytes 1179656 | tf_op jit(solution)/shard_map/ppermute | solution.py:326
  55.8 12.8 %collective-permute-start.1 = (f32[1,192,128]{2,1,0:T(8,128)S(1)}, f32[1,192,128]{2,1,0:T(8,128)S(1)}, u32[]{:S(2)}, u32[]{:S(2)}) collective-permute-start(f32[1,192,128]{2,1,0:T(8,128)S(1)} %get-tuple-element.12), channel_id=1, source_target_pairs={{0,0},{1,33},{2,66},{3,99},{4,4},{5,37},{6,70},{7,103},{8,8},{9,41... | collective-permute-start | bytes 294920 | tf_op jit(solution)/shard_map/ppermute | solution.py:334
  61.0 7.6 %collective-permute-start.2 = (f32[1,192,128]{2,1,0:T(8,128)S(1)}, f32[1,192,128]{2,1,0:T(8,128)S(1)}, u32[]{:S(2)}, u32[]{:S(2)}) collective-permute-start(f32[1,192,128]{2,1,0:T(8,128)S(1)} %get-tuple-element.11), channel_id=1, source_target_pairs={{0,1},{1,32},{2,67},{3,98},{4,5},{5,36},{6,71},{7,102},{8,9},{9,40... | collective-permute-start | bytes 294920 | tf_op jit(solution)/shard_map/ppermute | solution.py:334
  61.1 13.2 %collective-permute-start.3 = (f32[1,192,128]{2,1,0:T(8,128)S(1)}, f32[1,192,128]{2,1,0:T(8,128)S(1)}, u32[]{:S(2)}, u32[]{:S(2)}) collective-permute-start(f32[1,192,128]{2,1,0:T(8,128)S(1)} %get-tuple-element.10), channel_id=1, source_target_pairs={{0,2},{1,35},{2,64},{3,97},{4,6},{5,39},{6,68},{7,101},{8,10},{9,4... | collective-permute-start | bytes 294920 | tf_op jit(solution)/shard_map/ppermute | solution.py:334
  68.6 16.1 %collective-permute-start.4 = (f32[1,192,128]{2,1,0:T(8,128)S(1)}, f32[1,192,128]{2,1,0:T(8,128)S(1)}, u32[]{:S(2)}, u32[]{:S(2)}) collective-permute-start(f32[1,192,128]{2,1,0:T(8,128)S(1)} %get-tuple-element.9), channel_id=1, source_target_pairs={{0,3},{1,34},{2,65},{3,96},{4,7},{5,38},{6,69},{7,100},{8,11},{9,4... | collective-permute-start | bytes 294920 | tf_op jit(solution)/shard_map/ppermute | solution.py:334

commit v7 on v6

--- a/solution.py
+++ b/solution.py
@@ -220,6 +220,9 @@
     full, half = side // width, share // 2
     rest = side - full * width
     for piece in range(out_ref.shape[0]):
+        out_ref[piece, pl.ds(full * share, out_ref.shape[1] - full * share)] = jnp.zeros(
+            (out_ref.shape[1] - full * share, width), jnp.float32
+        )
         for lane in range(full):
             out_ref[piece, pl.ds(lane * share, share)] = total_ref[
                 pl.ds(piece * share, share), lane * width : (lane + 1) * width
@@ -230,13 +233,43 @@
             ]
 
 
+def send_kernel(used, ours_ref, came_ref, *out_refs):
+    layer, row = lax.axis_index("layer"), lax.axis_index("pair")
+    lines, width = came_ref.shape[1:]
+    line = lax.broadcasted_iota(jnp.int32, (lines, width), 0)
+    for turn, out_ref in enumerate(out_refs):
+        value = ours_ref[layer, row ^ turn] + came_ref[row ^ turn]
+        largest = jnp.maximum(jnp.max(jnp.abs(value), axis=0, keepdims=True), 2e-34)
+        power = jnp.floor(jnp.log2(largest)) - 14.0
+        steps = jnp.clip(jnp.round(value * jnp.exp2(-power)), -32767.0, 32767.0)
+        steps = jnp.where(line == used, jnp.broadcast_to(power, steps.shape), steps)
+        out_ref[...] = steps.astype(jnp.int32).astype(jnp.int16)
+
+
+def to_send(ours, came, used):
+    vmem = pl.BlockSpec(memory_space=pltpu.VMEM)
+    shape = jax.ShapeDtypeStruct(came.shape[1:], jnp.int16)
+    return pl.pallas_call(
+        functools.partial(send_kernel, used),
+        out_shape=[shape] * came.shape[0],
+        in_specs=[vmem, vmem],
+        out_specs=[vmem] * came.shape[0],
+        compiler_params=pltpu.CompilerParams(vmem_limit_bytes=16 * 1024 * 1024),
+        cost_estimate=pl.CostEstimate(flops=1000000, bytes_accessed=2000000, transcendentals=0),
+        name="to_send",
+    )(ours, came)
+
+
 def finish_kernel(cameras, lines_ref, *refs):
     pieces, out_ref = refs[:-1], refs[-1]
     share, side = out_ref.shape
-    width = pieces[0].shape[2]
-    total = pieces[0][0]
-    for piece in pieces[1:]:
-        total = total + piece[0]
+    width = pieces[0].shape[1]
+    used = side // width * share + share // 2
+    total = None
+    for piece in pieces:
+        steps = piece[...].astype(jnp.int32).astype(jnp.float32)
+        value = steps * jnp.broadcast_to(jnp.exp2(steps[used : used + 1]), steps.shape)
+        total = value if total is None else total + value
     start = (lax.axis_index("layer") * lax.axis_size("pair") + lax.axis_index("pair")) * share
     first = start // cameras
     row = start + lax.broadcasted_iota(jnp.int32, (share, side), 0)
@@ -320,19 +353,20 @@
     got, lines = lax.optimization_barrier((got, lines))
     partial_value = schur_partial(got, cameras, shares)
     partial_value = partial_value.reshape((layers, pairs) + partial_value.shape[1:])
-    layer, row = lax.axis_index("layer"), lax.axis_index("pair")
+    layer = lax.axis_index("layer")
     theirs = lax.dynamic_index_in_dim(partial_value, 1 - layer, 0, keepdims=False)
-    ours = lax.dynamic_index_in_dim(partial_value, layer, 0, keepdims=False)
-    ours = ours + lax.ppermute(theirs, "layer", [(0, 1), (1, 0)])
+    came = lax.ppermute(theirs, "layer", [(0, 1), (1, 0)])
+    share = side // shares
+    width = partial_value.shape[3]
+    parcels = to_send(partial_value, came, side // width * share + share // 2)
     pieces = []
     for turn in range(far):
         links = []
         for source in itertools.product(*(range(size) for size in sizes)):
             c, zp, zb, x, y = source
             links.append((flat(source, sizes), flat((c, (y + zp + 2 * zb) % far, zb, x, y ^ turn), sizes)))
-        piece = lax.dynamic_slice_in_dim(ours, row ^ turn, 1, 0)
-        pieces.append(lax.ppermute(piece, AXES, links))
-    return finish(lines, pieces, cameras, side // shares)[None]
+        pieces.append(lax.ppermute(parcels[turn], AXES, links))
+    return finish(lines, pieces, cameras, share)[None]
 
 
 def flat(place, sizes):

time: 85.9 us -> 80 us (0.931)
  the two profiles are of different devices: /device:TPU:8 before, /device:TPU:58 now
where the time goes in v7:
time: 80 us; the launch traced here: 79.6 us
  waiting for transfers between devices  36.2 us (45%)
  starting transfers between devices  22.8 us (28%)
  Pallas kernels  19.6 us (25%)
  local copies, waits for them, and re-layouts  0.88 us (1%)
    all_to_all x1, waiting for transfers between devices, local(): lax.all_to_all(packed, ('zb', 'x', 'pair'), split_axis=0, concat_axis=0,...  24.3 us
    pallas_call x1, Pallas kernels, schur_partial(): pl.pallas_call(functools.partial(schur_kernel, cameras, pieces), out_shap...  15.4 us
    ppermute x4, starting transfers between devices, local(): pieces.append(lax.ppermute(parcels[turn], AXES, links))  14.5 us
    ppermute x4, waiting for transfers between devices, local(): pieces.append(lax.ppermute(parcels[turn], AXES, links))  10.1 us
    all_to_all x1, starting transfers between devices, local(): lax.all_to_all(packed, ('zb', 'x', 'pair'), split_axis=0, concat_axis=0,...  8.23 us
    pallas_call x1, Pallas kernels, pack(): pl.pallas_call(functools.partial(pack_kernel, site_of), out_shape=jax.Sha...  3.95 us
    ppermute x1, waiting for transfers between devices, local(): came = lax.ppermute(theirs, 'layer', [(0, 1), (1, 0)])  1.71 us
  transfers between devices with their start and end apart: 6, of which 4 were waited for; matrix products, arithmetic and copies ran while one was open for 0% of the time, Pallas kernels for 0%

profile of v7, /device:TPU:58, one launch (start us, length us, event | category | flops | bytes accessed | tf_op | source)
XLA Modules:
  0.0 79.6 jit_solution(11658760145938521006)
XLA Ops:
  0.0 3.9 %pack.1 = bf16[32,2,30,4,128]{4,3,2,1,0:T(4,128)(2,1)} custom-call(s32[32]{0:T(128)} %bitcast.12, s32[32]{0:T(128)} %count_hbm.1, bf16[32,27,4,128]{3,2,1,0:T(4,128)(2,1)} %bitcast.10, bf16[6,32,128]{2,1,0:T(8,128)(2,1)} %bitcast.11, s32[32,4,128]{2,1,0:T(4,128)} %vis_hbm.1, s32[32,128]{1,0:T(8,128)} %obs_hbm.1), custom_call_target="tpu_custom_call" | custom-call | flops 1000000 | bytes 3000000 | tf_op jit(solution)/shard_map/pack/pallas_call | solution.py:83
  4.0 0.0 copy-start
  4.0 8.2 %all-to-all-start = ((bf16[32,2,30,4,128]{4,3,2,1,0:T(4,128)(2,1)}), bf16[32,2,30,4,128]{4,3,2,1,0:T(4,128)(2,1)S(1)}, u32[]{:S(2)}, u32[]{:S(2)}) async-start(bf16[32,2,30,4,128]{4,3,2,1,0:T(4,128)(2,1)} %pack.1), calls=%async_computation | async-start | bytes 3932160 | tf_op jit(solution)/shard_map/all_to_all | solution.py:352
  12.2 0.0 copy-done
  12.2 0.1 reduce
  12.3 0.1 reshape_squeeze.3.lines_ref
  12.4 24.3 %all-to-all-done.got_ref = bf16[32,2,30,4,128]{4,3,2,1,0:T(4,128)(2,1)S(1)} async-done(((bf16[32,2,30,4,128]{4,3,2,1,0:T(4,128)(2,1)}), bf16[32,2,30,4,128]{4,3,2,1,0:T(4,128)(2,1)S(1)}, u32[]{:S(2)}, u32[]{:S(2)}) %all-to-all-start) | async-done | bytes 1966112 | tf_op jit(solution)/shard_map/all_to_all | solution.py:352
  36.8 15.4 %schur_partial.1 = f32[8,192,128]{2,1,0:T(8,128)S(1)} custom-call(bf16[32,2,30,4,128]{4,3,2,1,0:T(4,128)(2,1)S(1)} %all-to-all-done.got_ref), custom_call_target="tpu_custom_call" | custom-call | flops 10000000000 | bytes 3000000 | tf_op jit(solution)/shard_map/schur_partial/pallas_call | solution.py:314
  52.2 0.1 collective-permute-start
  52.3 1.7 %collective-permute-done.came_ref = f32[4,192,128]{2,1,0:T(8,128)S(1)} collective-permute-done((f32[4,192,128]{2,1,0:T(8,128)S(1)}, f32[4,192,128]{2,1,0:T(8,128)S(1)}, u32[]{:S(2)}, u32[]{:S(2)}) %collective-permute-start) | collective-permute-done | bytes 393248 | tf_op jit(solution)/shard_map/ppermute | solution.py:358
  54.0 0.1 to_send.1
  54.2 5.2 %collective-permute-start.1 = (s16[192,128]{1,0:T(8,128)(2,1)S(1)}, s16[192,128]{1,0:T(8,128)(2,1)S(1)}, u32[]{:S(2)}, u32[]{:S(2)}) collective-permute-start(s16[192,128]{1,0:T(8,128)(2,1)S(1)} %get-tuple-element.13), channel_id=1, source_target_pairs={{0,0},{1,33},{2,66},{3,99},{4,4},{5,37},{6,70},{7,103},{8,8},{9,41... | collective-permute-start | bytes 147464 | tf_op jit(solution)/shard_map/ppermute | solution.py:368
  59.3 0.1 collective-permute-start.2
  59.4 9.2 %collective-permute-start.3 = (s16[192,128]{1,0:T(8,128)(2,1)S(1)}, s16[192,128]{1,0:T(8,128)(2,1)S(1)}, u32[]{:S(2)}, u32[]{:S(2)}) collective-permute-start(s16[192,128]{1,0:T(8,128)(2,1)S(1)} %get-tuple-element.15), channel_id=1, source_target_pairs={{0,2},{1,35},{2,64},{3,97},{4,6},{5,39},{6,68},{7,101},{8,10},{9,4... | collective-permute-start | bytes 147464 | tf_op jit(solution)/shard_map/ppermute | solution.py:368
  68.6 0.0 collective-permute-start.4
  68.6 0.0 collective-permute-done.1.refs_0_
  68.6 0.0 collective-permute-done.2.refs_1_
  68.6 3.1 %collective-permute-done.3.refs_2_ = s16[192,128]{1,0:T(8,128)(2,1)S(1)} collective-permute-done((s16[192,128]{1,0:T(8,128)(2,1)S(1)}, s16[192,128]{1,0:T(8,128)(2,1)S(1)}, u32[]{:S(2)}, u32[]{:S(2)}) %collective-permute-start.3) | collective-permute-done | bytes 49184 | tf_op jit(solution)/shard_map/ppermute | solution.py:368
  71.8 7.0 %collective-permute-done.4.refs_3_ = s16[192,128]{1,0:T(8,128)(2,1)S(1)} collective-permute-done((s16[192,128]{1,0:T(8,128)(2,1)S(1)}, s16[192,128]{1,0:T(8,128)(2,1)S(1)}, u32[]{:S(2)}, u32[]{:S(2)}) %collective-permute-start.4) | collective-permute-done | bytes 49184 | tf_op jit(solution)/shard_map/ppermute | solution.py:368
  78.8 0.1 finish.1
  78.9 0.8 copy.8
  (1 shorter events, 0.0 us)
Async XLA Ops:
  4.0 8.3 %copy-start = (f32[1,9,9,48]{3,0,2,1:T(1,128)S(1)}, f32[1,9,9,48]{3,0,2,1:T(1,128)}, u32[]{:S(2)}) copy-start(f32[1,9,9,48]{3,0,2,1:T(1,128)} %param.13) | copy-start | bytes 46660
  4.0 32.8 %all-to-all-start = ((bf16[32,2,30,4,128]{4,3,2,1,0:T(4,128)(2,1)}), bf16[32,2,30,4,128]{4,3,2,1,0:T(4,128)(2,1)S(1)}, u32[]{:S(2)}, u32[]{:S(2)}) async-start(bf16[32,2,30,4,128]{4,3,2,1,0:T(4,128)(2,1)} %pack.1), calls=%async_computation | async-start | bytes 3932160 | tf_op jit(solution)/shard_map/all_to_all | solution.py:352
  52.2 1.8 %collective-permute-start = (f32[4,192,128]{2,1,0:T(8,128)S(1)}, f32[4,192,128]{2,1,0:T(8,128)S(1)}, u32[]{:S(2)}, u32[]{:S(2)}) collective-permute-start(f32[4,192,128]{2,1,0:T(8,128)S(1)} %dynamic-slice_bitcast_fusion), channel_id=1, source_target_pairs={{0,128},{128,0},{1,129},{129,1},{2,130},{130,2},{3,131},{131,3},{4... | collective-permute-start | bytes 1179656 | tf_op jit(solution)/shard_map/ppermute | solution.py:358
  54.2 14.5 %collective-permute-start.1 = (s16[192,128]{1,0:T(8,128)(2,1)S(1)}, s16[192,128]{1,0:T(8,128)(2,1)S(1)}, u32[]{:S(2)}, u32[]{:S(2)}) collective-permute-start(s16[192,128]{1,0:T(8,128)(2,1)S(1)} %get-tuple-element.13), channel_id=1, source_target_pairs={{0,0},{1,33},{2,66},{3,99},{4,4},{5,37},{6,70},{7,103},{8,8},{9,41... | collective-permute-start | bytes 147464 | tf_op jit(solution)/shard_map/ppermute | solution.py:368
  59.3 9.3 %collective-permute-start.2 = (s16[192,128]{1,0:T(8,128)(2,1)S(1)}, s16[192,128]{1,0:T(8,128)(2,1)S(1)}, u32[]{:S(2)}, u32[]{:S(2)}) collective-permute-start(s16[192,128]{1,0:T(8,128)(2,1)S(1)} %get-tuple-element.14), channel_id=1, source_target_pairs={{0,1},{1,32},{2,67},{3,98},{4,5},{5,36},{6,71},{7,102},{8,9},{9,40... | collective-permute-start | bytes 147464 | tf_op jit(solution)/shard_map/ppermute | solution.py:368
  59.4 12.3 %collective-permute-start.3 = (s16[192,128]{1,0:T(8,128)(2,1)S(1)}, s16[192,128]{1,0:T(8,128)(2,1)S(1)}, u32[]{:S(2)}, u32[]{:S(2)}) collective-permute-start(s16[192,128]{1,0:T(8,128)(2,1)S(1)} %get-tuple-element.15), channel_id=1, source_target_pairs={{0,2},{1,35},{2,64},{3,97},{4,6},{5,39},{6,68},{7,101},{8,10},{9,4... | collective-permute-start | bytes 147464 | tf_op jit(solution)/shard_map/ppermute | solution.py:368
  68.6 10.1 %collective-permute-start.4 = (s16[192,128]{1,0:T(8,128)(2,1)S(1)}, s16[192,128]{1,0:T(8,128)(2,1)S(1)}, u32[]{:S(2)}, u32[]{:S(2)}) collective-permute-start(s16[192,128]{1,0:T(8,128)(2,1)S(1)} %get-tuple-element.16), channel_id=1, source_target_pairs={{0,3},{1,34},{2,65},{3,96},{4,7},{5,38},{6,69},{7,100},{8,11},{9,4... | collective-permute-start | bytes 147464 | tf_op jit(solution)/shard_map/ppermute | solution.py:368

commit v8 on v7

--- a/solution.py
+++ b/solution.py
@@ -237,39 +237,57 @@
     layer, row = lax.axis_index("layer"), lax.axis_index("pair")
     lines, width = came_ref.shape[1:]
     line = lax.broadcasted_iota(jnp.int32, (lines, width), 0)
-    for turn, out_ref in enumerate(out_refs):
+    for turn, (out_ref, part) in enumerate((ref, part) for ref in out_refs for part in range(2)):
         value = ours_ref[layer, row ^ turn] + came_ref[row ^ turn]
         largest = jnp.maximum(jnp.max(jnp.abs(value), axis=0, keepdims=True), 2e-34)
         power = jnp.floor(jnp.log2(largest)) - 14.0
         steps = jnp.clip(jnp.round(value * jnp.exp2(-power)), -32767.0, 32767.0)
         steps = jnp.where(line == used, jnp.broadcast_to(power, steps.shape), steps)
-        out_ref[...] = steps.astype(jnp.int32).astype(jnp.int16)
+        out_ref[part] = steps.astype(jnp.int32).astype(jnp.int16)
 
 
 def to_send(ours, came, used):
     vmem = pl.BlockSpec(memory_space=pltpu.VMEM)
-    shape = jax.ShapeDtypeStruct(came.shape[1:], jnp.int16)
+    parcels = came.shape[0] // 2
+    shape = jax.ShapeDtypeStruct((2,) + came.shape[1:], jnp.int16)
     return pl.pallas_call(
         functools.partial(send_kernel, used),
-        out_shape=[shape] * came.shape[0],
+        out_shape=[shape] * parcels,
         in_specs=[vmem, vmem],
-        out_specs=[vmem] * came.shape[0],
+        out_specs=[vmem] * parcels,
         compiler_params=pltpu.CompilerParams(vmem_limit_bytes=16 * 1024 * 1024),
         cost_estimate=pl.CostEstimate(flops=1000000, bytes_accessed=2000000, transcendentals=0),
         name="to_send",
     )(ours, came)
 
 
-def finish_kernel(cameras, lines_ref, *refs):
-    pieces, out_ref = refs[:-1], refs[-1]
+def value_of(parcel, part, used):
+    steps = parcel[part].astype(jnp.int32).astype(jnp.float32)
+    return steps * jnp.broadcast_to(jnp.exp2(steps[used : used + 1]), steps.shape)
+
+
+def beside_kernel(used, first, second, out_ref):
+    out_ref[...] = value_of(first, 1, used) + value_of(second, 1, used)
+
+
+def for_beside(parcels, used):
+    vmem = pl.BlockSpec(memory_space=pltpu.VMEM)
+    return pl.pallas_call(
+        functools.partial(beside_kernel, used),
+        out_shape=jax.ShapeDtypeStruct(parcels[0].shape[1:], jnp.float32),
+        in_specs=[vmem, vmem],
+        out_specs=vmem,
+        compiler_params=pltpu.CompilerParams(vmem_limit_bytes=16 * 1024 * 1024),
+        cost_estimate=pl.CostEstimate(flops=100000, bytes_accessed=300000, transcendentals=0),
+        name="for_beside",
+    )(*parcels)
+
+
+def finish_kernel(cameras, lines_ref, came_ref, first, second, out_ref):
     share, side = out_ref.shape
-    width = pieces[0].shape[1]
+    width = came_ref.shape[1]
     used = side // width * share + share // 2
-    total = None
-    for piece in pieces:
-        steps = piece[...].astype(jnp.int32).astype(jnp.float32)
-        value = steps * jnp.broadcast_to(jnp.exp2(steps[used : used + 1]), steps.shape)
-        total = value if total is None else total + value
+    total = value_of(first, 0, used) + value_of(second, 0, used) + came_ref[...]
     start = (lax.axis_index("layer") * lax.axis_size("pair") + lax.axis_index("pair")) * share
     first = start // cameras
     row = start + lax.broadcasted_iota(jnp.int32, (share, side), 0)
@@ -360,12 +378,14 @@
     width = partial_value.shape[3]
     parcels = to_send(partial_value, came, side // width * share + share // 2)
     pieces = []
-    for turn in range(far):
+    for turn in range(pairs // 2):
         links = []
         for source in itertools.product(*(range(size) for size in sizes)):
             c, zp, zb, x, y = source
-            links.append((flat(source, sizes), flat((c, (y + zp + 2 * zb) % far, zb, x, y ^ turn), sizes)))
+            links.append((flat(source, sizes), flat((c, (y + zp + 2 * zb) % far, zb, x, y ^ (2 * turn)), sizes)))
         pieces.append(lax.ppermute(parcels[turn], AXES, links))
+    beside = for_beside(pieces, side // width * share + share // 2)
+    pieces.insert(0, lax.ppermute(beside, "pair", [(y, y ^ 1) for y in range(pairs)]))
     return finish(lines, pieces, cameras, share)[None]
 
 

time: 80 us -> 80.9 us (1.011)
  the two profiles are of different devices: /device:TPU:58 before, /device:TPU:64 now
where the time goes in v8:
time: 80.9 us; the launch traced here: 80.6 us
  waiting for transfers between devices  42.8 us (53%)
  Pallas kernels  19.6 us (24%)
  starting transfers between devices  17.1 us (21%)
  local copies, waits for them, and re-layouts  0.88 us (1%)
    all_to_all x1, waiting for transfers between devices, local(): lax.all_to_all(packed, ('zb', 'x', 'pair'), split_axis=0, concat_axis=0,...  26.7 us
    pallas_call x1, Pallas kernels, schur_partial(): pl.pallas_call(functools.partial(schur_kernel, cameras, pieces), out_shap...  15.4 us
    ppermute x2, waiting for transfers between devices, local(): pieces.append(lax.ppermute(parcels[turn], AXES, links))  9.81 us
    all_to_all x1, starting transfers between devices, local(): lax.all_to_all(packed, ('zb', 'x', 'pair'), split_axis=0, concat_axis=0,...  8.68 us
    ppermute x2, starting transfers between devices, local(): pieces.append(lax.ppermute(parcels[turn], AXES, links))  8.24 us
    ppermute x1, waiting for transfers between devices, local(): lax.ppermute(beside, 'pair', [(y, y ^ 1) for y in range(pairs)])  4.6 us
    pallas_call x1, Pallas kernels, pack(): pl.pallas_call(functools.partial(pack_kernel, site_of), out_shape=jax.Sha...  3.93 us
    ppermute x1, waiting for transfers between devices, local(): came = lax.ppermute(theirs, 'layer', [(0, 1), (1, 0)])  1.71 us
  transfers between devices with their start and end apart: 5, of which 4 were waited for; matrix products, arithmetic and copies ran while one was open for 0% of the time, Pallas kernels for 0%

profile of v8, /device:TPU:64, one launch (start us, length us, event | category | flops | bytes accessed | tf_op | source)
XLA Modules:
  0.0 80.6 jit_solution(11403197117881376696)
XLA Ops:
  0.0 3.9 %pack.1 = bf16[32,2,30,4,128]{4,3,2,1,0:T(4,128)(2,1)} custom-call(s32[32]{0:T(128)} %bitcast.12, s32[32]{0:T(128)} %count_hbm.1, bf16[32,27,4,128]{3,2,1,0:T(4,128)(2,1)} %bitcast.10, bf16[6,32,128]{2,1,0:T(8,128)(2,1)} %bitcast.11, s32[32,4,128]{2,1,0:T(4,128)} %vis_hbm.1, s32[32,128]{1,0:T(8,128)} %obs_hbm.1), custom_call_target="tpu_custom_call" | custom-call | flops 1000000 | bytes 3000000 | tf_op jit(solution)/shard_map/pack/pallas_call | solution.py:83
  3.9 0.0 copy-start
  4.0 8.7 %all-to-all-start = ((bf16[32,2,30,4,128]{4,3,2,1,0:T(4,128)(2,1)}), bf16[32,2,30,4,128]{4,3,2,1,0:T(4,128)(2,1)S(1)}, u32[]{:S(2)}, u32[]{:S(2)}) async-start(bf16[32,2,30,4,128]{4,3,2,1,0:T(4,128)(2,1)} %pack.1), calls=%async_computation | async-start | bytes 3932160 | tf_op jit(solution)/shard_map/all_to_all | solution.py:370
  12.6 0.0 copy-done
  12.7 0.1 reduce
  12.8 0.1 reshape_squeeze.3.lines_ref
  12.9 26.7 %all-to-all-done.got_ref = bf16[32,2,30,4,128]{4,3,2,1,0:T(4,128)(2,1)S(1)} async-done(((bf16[32,2,30,4,128]{4,3,2,1,0:T(4,128)(2,1)}), bf16[32,2,30,4,128]{4,3,2,1,0:T(4,128)(2,1)S(1)}, u32[]{:S(2)}, u32[]{:S(2)}) %all-to-all-start) | async-done | bytes 1966112 | tf_op jit(solution)/shard_map/all_to_all | solution.py:370
  39.5 15.4 %schur_partial.1 = f32[8,192,128]{2,1,0:T(8,128)S(1)} custom-call(bf16[32,2,30,4,128]{4,3,2,1,0:T(4,128)(2,1)S(1)} %all-to-all-done.got_ref), custom_call_target="tpu_custom_call" | custom-call | flops 10000000000 | bytes 3000000 | tf_op jit(solution)/shard_map/schur_partial/pallas_call | solution.py:332
  55.0 0.1 collective-permute-start
  55.1 1.7 %collective-permute-done.came_ref = f32[4,192,128]{2,1,0:T(8,128)S(1)} collective-permute-done((f32[4,192,128]{2,1,0:T(8,128)S(1)}, f32[4,192,128]{2,1,0:T(8,128)S(1)}, u32[]{:S(2)}, u32[]{:S(2)}) %collective-permute-start) | collective-permute-done | bytes 393248 | tf_op jit(solution)/shard_map/ppermute | solution.py:376
  56.8 0.1 to_send.1
  56.9 0.7 collective-permute-start.1
  57.6 7.6 %collective-permute-start.2 = (s16[2,192,128]{2,1,0:T(8,128)(2,1)S(1)}, s16[2,192,128]{2,1,0:T(8,128)(2,1)S(1)}, u32[]{:S(2)}, u32[]{:S(2)}) collective-permute-start(s16[2,192,128]{2,1,0:T(8,128)(2,1)S(1)} %get-tuple-element.12), channel_id=1, source_target_pairs={{0,2},{1,35},{2,64},{3,97},{4,6},{5,39},{6,68},{7,101},{8,10},{9,4... | collective-permute-start | bytes 294920 | tf_op jit(solution)/shard_map/ppermute | solution.py:386
  65.2 0.0 collective-permute-done.1.first
  65.2 9.8 %collective-permute-done.2.second = s16[2,192,128]{2,1,0:T(8,128)(2,1)S(1)} collective-permute-done((s16[2,192,128]{2,1,0:T(8,128)(2,1)S(1)}, s16[2,192,128]{2,1,0:T(8,128)(2,1)S(1)}, u32[]{:S(2)}, u32[]{:S(2)}) %collective-permute-start.2) | collective-permute-done | bytes 98336 | tf_op jit(solution)/shard_map/ppermute | solution.py:386
  75.0 0.1 collective-permute-start.3
  75.1 4.6 %collective-permute-done.3.came_ref = f32[192,128]{1,0:T(8,128)S(1)} collective-permute-done((f32[192,128]{1,0:T(8,128)S(1)}, f32[192,128]{1,0:T(8,128)S(1)}, u32[]{:S(2)}, u32[]{:S(2)}) %collective-permute-start.3) | collective-permute-done | bytes 98336 | tf_op jit(solution)/shard_map/ppermute | solution.py:388
  79.7 0.1 finish.1
  79.8 0.8 copy.8
  (2 shorter events, 0.1 us)
Async XLA Ops:
  3.9 8.7 %copy-start = (f32[1,9,9,48]{3,0,2,1:T(1,128)S(1)}, f32[1,9,9,48]{3,0,2,1:T(1,128)}, u32[]{:S(2)}) copy-start(f32[1,9,9,48]{3,0,2,1:T(1,128)} %param.13) | copy-start | bytes 46660
  4.0 35.6 %all-to-all-start = ((bf16[32,2,30,4,128]{4,3,2,1,0:T(4,128)(2,1)}), bf16[32,2,30,4,128]{4,3,2,1,0:T(4,128)(2,1)S(1)}, u32[]{:S(2)}, u32[]{:S(2)}) async-start(bf16[32,2,30,4,128]{4,3,2,1,0:T(4,128)(2,1)} %pack.1), calls=%async_computation | async-start | bytes 3932160 | tf_op jit(solution)/shard_map/all_to_all | solution.py:370
  55.0 1.8 %collective-permute-start = (f32[4,192,128]{2,1,0:T(8,128)S(1)}, f32[4,192,128]{2,1,0:T(8,128)S(1)}, u32[]{:S(2)}, u32[]{:S(2)}) collective-permute-start(f32[4,192,128]{2,1,0:T(8,128)S(1)} %dynamic-slice_bitcast_fusion), channel_id=1, source_target_pairs={{0,128},{128,0},{1,129},{129,1},{2,130},{130,2},{3,131},{131,3},{4... | collective-permute-start | bytes 1179656 | tf_op jit(solution)/shard_map/ppermute | solution.py:376
  56.9 8.3 %collective-permute-start.1 = (s16[2,192,128]{2,1,0:T(8,128)(2,1)S(1)}, s16[2,192,128]{2,1,0:T(8,128)(2,1)S(1)}, u32[]{:S(2)}, u32[]{:S(2)}) collective-permute-start(s16[2,192,128]{2,1,0:T(8,128)(2,1)S(1)} %get-tuple-element.11), channel_id=1, source_target_pairs={{0,0},{1,33},{2,66},{3,99},{4,4},{5,37},{6,70},{7,103},{8,8},{9,41... | collective-permute-start | bytes 294920 | tf_op jit(solution)/shard_map/ppermute | solution.py:386
  57.6 17.4 %collective-permute-start.2 = (s16[2,192,128]{2,1,0:T(8,128)(2,1)S(1)}, s16[2,192,128]{2,1,0:T(8,128)(2,1)S(1)}, u32[]{:S(2)}, u32[]{:S(2)}) collective-permute-start(s16[2,192,128]{2,1,0:T(8,128)(2,1)S(1)} %get-tuple-element.12), channel_id=1, source_target_pairs={{0,2},{1,35},{2,64},{3,97},{4,6},{5,39},{6,68},{7,101},{8,10},{9,4... | collective-permute-start | bytes 294920 | tf_op jit(solution)/shard_map/ppermute | solution.py:386
  75.0 4.7 %collective-permute-start.3 = (f32[192,128]{1,0:T(8,128)S(1)}, f32[192,128]{1,0:T(8,128)S(1)}, u32[]{:S(2)}, u32[]{:S(2)}) collective-permute-start(f32[192,128]{1,0:T(8,128)S(1)} %for_beside.1), channel_id=1, source_target_pairs={{0,1},{1,0},{2,3},{3,2},{4,5},{5,4},{6,7},{7,6},{8,9},{9,8},{10,11... | collective-permute-start | bytes 294920 | tf_op jit(solution)/shard_map/ppermute | solution.py:388

commit v9 on v7

--- a/solution.py
+++ b/solution.py
@@ -262,7 +262,7 @@
 
 def finish_kernel(cameras, lines_ref, *refs):
     pieces, out_ref = refs[:-1], refs[-1]
-    share, side = out_ref.shape
+    share, _, side = out_ref.shape
     width = pieces[0].shape[1]
     used = side // width * share + share // 2
     total = None
@@ -283,10 +283,10 @@
     rest = side - full * width
     for lane in range(full):
         columns = slice(lane * width, (lane + 1) * width)
-        out_ref[:, columns] = own[:, columns] - total[lane * share : (lane + 1) * share]
+        out_ref[:, 0, columns] = own[:, columns] - total[lane * share : (lane + 1) * share]
     for step in range(2):
         rows, columns = slice(step * half, (step + 1) * half), slice(full * width, side)
-        out_ref[rows, columns] = (
+        out_ref[rows, 0, columns] = (
             own[rows, columns] - total[full * share : full * share + half, step * rest : (step + 1) * rest]
         )
 
@@ -295,7 +295,7 @@
     vmem = pl.BlockSpec(memory_space=pltpu.VMEM)
     return pl.pallas_call(
         functools.partial(finish_kernel, cameras),
-        out_shape=jax.ShapeDtypeStruct((share, lines.shape[1]), jnp.float32),
+        out_shape=jax.ShapeDtypeStruct((share, 1, lines.shape[1]), jnp.float32),
         in_specs=[vmem] * (1 + len(pieces)),
         out_specs=vmem,
         compiler_params=pltpu.CompilerParams(vmem_limit_bytes=16 * 1024 * 1024),
@@ -360,13 +360,13 @@
     width = partial_value.shape[3]
     parcels = to_send(partial_value, came, side // width * share + share // 2)
     pieces = []
-    for turn in range(far):
+    for turn in sorted(range(far), key=lambda turn: -min(turn, pairs - turn)):
         links = []
         for source in itertools.product(*(range(size) for size in sizes)):
             c, zp, zb, x, y = source
             links.append((flat(source, sizes), flat((c, (y + zp + 2 * zb) % far, zb, x, y ^ turn), sizes)))
         pieces.append(lax.ppermute(parcels[turn], AXES, links))
-    return finish(lines, pieces, cameras, share)[None]
+    return finish(lines, pieces, cameras, share).transpose(1, 0, 2)
 
 
 def flat(place, sizes):

time: 80 us -> 79.2 us (0.990)
  the two profiles are of different devices: /device:TPU:58 before, /device:TPU:34 now
where the time goes in v9:
time: 79.2 us; the launch traced here: 78.9 us
  waiting for transfers between devices  35.5 us (45%)
  starting transfers between devices  22.7 us (29%)
  Pallas kernels  20.3 us (26%)
    all_to_all x1, waiting for transfers between devices, local(): lax.all_to_all(packed, ('zb', 'x', 'pair'), split_axis=0, concat_axis=0,...  26.7 us
    pallas_call x1, Pallas kernels, schur_partial(): pl.pallas_call(functools.partial(schur_kernel, cameras, pieces), out_shap...  15.4 us
    ppermute x4, starting transfers between devices, local(): pieces.append(lax.ppermute(parcels[turn], AXES, links))  14.1 us
    all_to_all x1, starting transfers between devices, local(): lax.all_to_all(packed, ('zb', 'x', 'pair'), split_axis=0, concat_axis=0,...  8.55 us
    ppermute x4, waiting for transfers between devices, local(): pieces.append(lax.ppermute(parcels[turn], AXES, links))  7 us
    pallas_call x1, Pallas kernels, pack(): pl.pallas_call(functools.partial(pack_kernel, site_of), out_shape=jax.Sha...  3.95 us
    ppermute x1, waiting for transfers between devices, local(): came = lax.ppermute(theirs, 'layer', [(0, 1), (1, 0)])  1.71 us
  transfers between devices with their start and end apart: 6, of which 4 were waited for; matrix products, arithmetic and copies ran while one was open for 0% of the time, Pallas kernels for 0%

profile of v9, /device:TPU:34, one launch (start us, length us, event | category | flops | bytes accessed | tf_op | source)
XLA Modules:
  0.0 78.9 jit_solution(10608872324458154657)
XLA Ops:
  0.0 3.9 %pack.1 = bf16[32,2,30,4,128]{4,3,2,1,0:T(4,128)(2,1)} custom-call(s32[32]{0:T(128)} %bitcast.11, s32[32]{0:T(128)} %count_hbm.1, bf16[32,27,4,128]{3,2,1,0:T(4,128)(2,1)} %bitcast.9, bf16[6,32,128]{2,1,0:T(8,128)(2,1)} %bitcast.10, s32[32,4,128]{2,1,0:T(4,128)} %vis_hbm.1, s32[32,128]{1,0:T(8,128)} %obs_hbm.1), custom_call_target="tpu_custom_call" | custom-call | flops 1000000 | bytes 3000000 | tf_op jit(solution)/shard_map/pack/pallas_call | solution.py:83
  4.0 0.0 copy-start
  4.0 8.5 %all-to-all-start = ((bf16[32,2,30,4,128]{4,3,2,1,0:T(4,128)(2,1)}), bf16[32,2,30,4,128]{4,3,2,1,0:T(4,128)(2,1)S(1)}, u32[]{:S(2)}, u32[]{:S(2)}) async-start(bf16[32,2,30,4,128]{4,3,2,1,0:T(4,128)(2,1)} %pack.1), calls=%async_computation | async-start | bytes 3932160 | tf_op jit(solution)/shard_map/all_to_all | solution.py:352
  12.5 0.0 copy-done
  12.5 0.1 reduce
  12.6 0.1 reshape_squeeze.3.lines_ref
  12.7 26.7 %all-to-all-done.got_ref = bf16[32,2,30,4,128]{4,3,2,1,0:T(4,128)(2,1)S(1)} async-done(((bf16[32,2,30,4,128]{4,3,2,1,0:T(4,128)(2,1)}), bf16[32,2,30,4,128]{4,3,2,1,0:T(4,128)(2,1)S(1)}, u32[]{:S(2)}, u32[]{:S(2)}) %all-to-all-start) | async-done | bytes 1966112 | tf_op jit(solution)/shard_map/all_to_all | solution.py:352
  39.5 15.4 %schur_partial.1 = f32[8,192,128]{2,1,0:T(8,128)S(1)} custom-call(bf16[32,2,30,4,128]{4,3,2,1,0:T(4,128)(2,1)S(1)} %all-to-all-done.got_ref), custom_call_target="tpu_custom_call" | custom-call | flops 10000000000 | bytes 3000000 | tf_op jit(solution)/shard_map/schur_partial/pallas_call | solution.py:314
  55.0 0.1 collective-permute-start
  55.1 1.7 %collective-permute-done.came_ref = f32[4,192,128]{2,1,0:T(8,128)S(1)} collective-permute-done((f32[4,192,128]{2,1,0:T(8,128)S(1)}, f32[4,192,128]{2,1,0:T(8,128)S(1)}, u32[]{:S(2)}, u32[]{:S(2)}) %collective-permute-start) | collective-permute-done | bytes 393248 | tf_op jit(solution)/shard_map/ppermute | solution.py:358
  56.8 0.1 to_send.1
  56.9 5.9 %collective-permute-start.1 = (s16[192,128]{1,0:T(8,128)(2,1)S(1)}, s16[192,128]{1,0:T(8,128)(2,1)S(1)}, u32[]{:S(2)}, u32[]{:S(2)}) collective-permute-start(s16[192,128]{1,0:T(8,128)(2,1)S(1)} %get-tuple-element.13), channel_id=1, source_target_pairs={{0,2},{1,35},{2,64},{3,97},{4,6},{5,39},{6,68},{7,101},{8,10},{9,4... | collective-permute-start | bytes 147464 | tf_op jit(solution)/shard_map/ppermute | solution.py:368
  62.8 1.0 %collective-permute-start.2 = (s16[192,128]{1,0:T(8,128)(2,1)S(1)}, s16[192,128]{1,0:T(8,128)(2,1)S(1)}, u32[]{:S(2)}, u32[]{:S(2)}) collective-permute-start(s16[192,128]{1,0:T(8,128)(2,1)S(1)} %get-tuple-element.14), channel_id=1, source_target_pairs={{0,1},{1,32},{2,67},{3,98},{4,5},{5,36},{6,71},{7,102},{8,9},{9,40... | collective-permute-start | bytes 147464 | tf_op jit(solution)/shard_map/ppermute | solution.py:368
  63.8 3.9 %collective-permute-start.3 = (s16[192,128]{1,0:T(8,128)(2,1)S(1)}, s16[192,128]{1,0:T(8,128)(2,1)S(1)}, u32[]{:S(2)}, u32[]{:S(2)}) collective-permute-start(s16[192,128]{1,0:T(8,128)(2,1)S(1)} %get-tuple-element.15), channel_id=1, source_target_pairs={{0,3},{1,34},{2,65},{3,96},{4,7},{5,38},{6,69},{7,100},{8,11},{9,4... | collective-permute-start | bytes 147464 | tf_op jit(solution)/shard_map/ppermute | solution.py:368
  67.7 3.3 %collective-permute-start.4 = (s16[192,128]{1,0:T(8,128)(2,1)S(1)}, s16[192,128]{1,0:T(8,128)(2,1)S(1)}, u32[]{:S(2)}, u32[]{:S(2)}) collective-permute-start(s16[192,128]{1,0:T(8,128)(2,1)S(1)} %get-tuple-element.16), channel_id=1, source_target_pairs={{0,0},{1,33},{2,66},{3,99},{4,4},{5,37},{6,70},{7,103},{8,8},{9,41... | collective-permute-start | bytes 147464 | tf_op jit(solution)/shard_map/ppermute | solution.py:368
  71.0 0.0 collective-permute-done.1.refs_0_
  71.0 0.0 collective-permute-done.2.refs_1_
  71.0 1.1 %collective-permute-done.3.refs_2_ = s16[192,128]{1,0:T(8,128)(2,1)S(1)} collective-permute-done((s16[192,128]{1,0:T(8,128)(2,1)S(1)}, s16[192,128]{1,0:T(8,128)(2,1)S(1)}, u32[]{:S(2)}, u32[]{:S(2)}) %collective-permute-start.3) | collective-permute-done | bytes 49184 | tf_op jit(solution)/shard_map/ppermute | solution.py:368
  72.1 5.9 %collective-permute-done.4.refs_3_ = s16[192,128]{1,0:T(8,128)(2,1)S(1)} collective-permute-done((s16[192,128]{1,0:T(8,128)(2,1)S(1)}, s16[192,128]{1,0:T(8,128)(2,1)S(1)}, u32[]{:S(2)}, u32[]{:S(2)}) %collective-permute-start.4) | collective-permute-done | bytes 49184 | tf_op jit(solution)/shard_map/ppermute | solution.py:368
  78.0 0.8 %finish.1 = f32[54,1,432]{2,1,0:T(1,128)} custom-call(f32[9,432]{1,0:T(8,128)S(1)} %reshape_squeeze.3.lines_ref, s16[192,128]{1,0:T(8,128)(2,1)S(1)} %collective-permute-done.1.refs_0_, s16[192,128]{1,0:T(8,128)(2,1)S(1)} %collective-permute-done.2.refs_1_, s16[192,128]{1,0:T(8,128)(2,1)S(1)} %collective-permute-done.3.refs_2_, ...), custom_call_target="tpu_custom_call" | custom-call | flops 200000 | bytes 500000 | tf_op jit(solution)/shard_map/finish/pallas_call | solution.py:296
  (1 shorter events, 0.0 us)
Async XLA Ops:
  4.0 8.6 %copy-start = (f32[1,9,9,48]{3,0,2,1:T(1,128)S(1)}, f32[1,9,9,48]{3,0,2,1:T(1,128)}, u32[]{:S(2)}) copy-start(f32[1,9,9,48]{3,0,2,1:T(1,128)} %param.13) | copy-start | bytes 46660
  4.0 35.5 %all-to-all-start = ((bf16[32,2,30,4,128]{4,3,2,1,0:T(4,128)(2,1)}), bf16[32,2,30,4,128]{4,3,2,1,0:T(4,128)(2,1)S(1)}, u32[]{:S(2)}, u32[]{:S(2)}) async-start(bf16[32,2,30,4,128]{4,3,2,1,0:T(4,128)(2,1)} %pack.1), calls=%async_computation | async-start | bytes 3932160 | tf_op jit(solution)/shard_map/all_to_all | solution.py:352
  55.0 1.8 %collective-permute-start = (f32[4,192,128]{2,1,0:T(8,128)S(1)}, f32[4,192,128]{2,1,0:T(8,128)S(1)}, u32[]{:S(2)}, u32[]{:S(2)}) collective-permute-start(f32[4,192,128]{2,1,0:T(8,128)S(1)} %dynamic-slice_bitcast_fusion), channel_id=1, source_target_pairs={{0,128},{128,0},{1,129},{129,1},{2,130},{130,2},{3,131},{131,3},{4... | collective-permute-start | bytes 1179656 | tf_op jit(solution)/shard_map/ppermute | solution.py:358
  56.9 14.1 %collective-permute-start.1 = (s16[192,128]{1,0:T(8,128)(2,1)S(1)}, s16[192,128]{1,0:T(8,128)(2,1)S(1)}, u32[]{:S(2)}, u32[]{:S(2)}) collective-permute-start(s16[192,128]{1,0:T(8,128)(2,1)S(1)} %get-tuple-element.13), channel_id=1, source_target_pairs={{0,2},{1,35},{2,64},{3,97},{4,6},{5,39},{6,68},{7,101},{8,10},{9,4... | collective-permute-start | bytes 147464 | tf_op jit(solution)/shard_map/ppermute | solution.py:368
  62.8 8.2 %collective-permute-start.2 = (s16[192,128]{1,0:T(8,128)(2,1)S(1)}, s16[192,128]{1,0:T(8,128)(2,1)S(1)}, u32[]{:S(2)}, u32[]{:S(2)}) collective-permute-start(s16[192,128]{1,0:T(8,128)(2,1)S(1)} %get-tuple-element.14), channel_id=1, source_target_pairs={{0,1},{1,32},{2,67},{3,98},{4,5},{5,36},{6,71},{7,102},{8,9},{9,40... | collective-permute-start | bytes 147464 | tf_op jit(solution)/shard_map/ppermute | solution.py:368
  63.8 8.3 %collective-permute-start.3 = (s16[192,128]{1,0:T(8,128)(2,1)S(1)}, s16[192,128]{1,0:T(8,128)(2,1)S(1)}, u32[]{:S(2)}, u32[]{:S(2)}) collective-permute-start(s16[192,128]{1,0:T(8,128)(2,1)S(1)} %get-tuple-element.15), channel_id=1, source_target_pairs={{0,3},{1,34},{2,65},{3,96},{4,7},{5,38},{6,69},{7,100},{8,11},{9,4... | collective-permute-start | bytes 147464 | tf_op jit(solution)/shard_map/ppermute | solution.py:368
  67.7 10.4 %collective-permute-start.4 = (s16[192,128]{1,0:T(8,128)(2,1)S(1)}, s16[192,128]{1,0:T(8,128)(2,1)S(1)}, u32[]{:S(2)}, u32[]{:S(2)}) collective-permute-start(s16[192,128]{1,0:T(8,128)(2,1)S(1)} %get-tuple-element.16), channel_id=1, source_target_pairs={{0,0},{1,33},{2,66},{3,99},{4,4},{5,37},{6,70},{7,103},{8,8},{9,41... | collective-permute-start | bytes 147464 | tf_op jit(solution)/shard_map/ppermute | solution.py:368

commit v10 on v9

--- a/solution.py
+++ b/solution.py
@@ -36,10 +36,11 @@
         return carry
 
     lax.fori_loop(0, places, clear, 0, unroll=8)
+    plane = lax.axis_index("zp")
     small[0].wait()
 
     def send(tile, carry):
-        place = site_of(route_ref[tile])
+        place = site_of(route_ref[tile], plane)
         slot = fill_ref[place]
         fill_ref[place] = slot + 1
         route_ref[tile] = 2 * place + slot
@@ -56,8 +57,8 @@
     point_iota = lax.broadcasted_iota(jnp.int32, (4, width), 1)
 
     def fill(tile, carry):
-        place = route_ref[tile] // 2
-        slot = route_ref[tile] % 2
+        place = route_ref[tile] >> 1
+        slot = route_ref[tile] & 1
         obs = jnp.broadcast_to(obs_ref[pl.ds(tile, 1), :], (4, width))
         live = (slot_iota < obs) & (point_iota < count_ref[tile])
         marks = jnp.where(live, vis_ref[tile], -1).astype(jnp.float32).astype(jnp.bfloat16)
@@ -339,10 +340,10 @@
     layers, pairs, far, near, across = (lax.axis_size(a) for a in ("layer", "pair", "zp", "zb", "x"))
     shares = layers * pairs
 
-    def site_of(group):
-        side_z = group // across % near
-        y = (group // (across * near) + pairs - lax.axis_index("zp") + 2 * side_z) % pairs
-        return side_z * (across * pairs) + group % across * pairs + y
+    def site_of(group, plane):
+        side_z = (group >> bits(across)) & (near - 1)
+        y = ((group >> bits(across * near)) + pairs - plane + 2 * side_z) & (pairs - 1)
+        return side_z * (across * pairs) + (group & (across - 1)) * pairs + y
 
     packed = pack(
         jac_blocks.transpose(0, 2, 1, 3), point_blocks.transpose(1, 0, 2), visibility, obs_count, tile_count,
@@ -369,6 +370,11 @@
     return finish(lines, pieces, cameras, share).transpose(1, 0, 2)
 
 
+def bits(size):
+    assert size & (size - 1) == 0
+    return size.bit_length() - 1
+
+
 def flat(place, sizes):
     index = 0
     for coordinate, size in zip(place, sizes):

time: 79.2 us -> 78.9 us (level)
  no operation moved by 1% of the time
where the time goes in v10:
time: 78.9 us; the launch traced here: 78.5 us
  waiting for transfers between devices  35.4 us (45%)
  starting transfers between devices  22.8 us (29%)
  Pallas kernels  20 us (25%)
    all_to_all x1, waiting for transfers between devices, local(): lax.all_to_all(packed, ('zb', 'x', 'pair'), split_axis=0, concat_axis=0,...  26.7 us
    pallas_call x1, Pallas kernels, schur_partial(): pl.pallas_call(functools.partial(schur_kernel, cameras, pieces), out_shap...  15.4 us
    ppermute x4, starting transfers between devices, local(): pieces.append(lax.ppermute(parcels[turn], AXES, links))  14.2 us
    all_to_all x1, starting transfers between devices, local(): lax.all_to_all(packed, ('zb', 'x', 'pair'), split_axis=0, concat_axis=0,...  8.55 us
    ppermute x4, waiting for transfers between devices, local(): pieces.append(lax.ppermute(parcels[turn], AXES, links))  6.99 us
    pallas_call x1, Pallas kernels, pack(): pl.pallas_call(functools.partial(pack_kernel, site_of), out_shape=jax.Sha...  3.62 us
    ppermute x1, waiting for transfers between devices, local(): came = lax.ppermute(theirs, 'layer', [(0, 1), (1, 0)])  1.71 us
  transfers between devices with their start and end apart: 6, of which 4 were waited for; matrix products, arithmetic and copies ran while one was open for 0% of the time, Pallas kernels for 0%

profile of v10, /device:TPU:34, one launch (start us, length us, event | category | flops | bytes accessed | tf_op | source)
XLA Modules:
  0.0 78.5 jit_solution(10669089794013643341)
XLA Ops:
  0.0 3.6 %pack.1 = bf16[32,2,30,4,128]{4,3,2,1,0:T(4,128)(2,1)} custom-call(s32[32]{0:T(128)} %bitcast.11, s32[32]{0:T(128)} %count_hbm.1, bf16[32,27,4,128]{3,2,1,0:T(4,128)(2,1)} %bitcast.9, bf16[6,32,128]{2,1,0:T(8,128)(2,1)} %bitcast.10, s32[32,4,128]{2,1,0:T(4,128)} %vis_hbm.1, s32[32,128]{1,0:T(8,128)} %obs_hbm.1), custom_call_target="tpu_custom_call" | custom-call | flops 1000000 | bytes 3000000 | tf_op jit(solution)/shard_map/pack/pallas_call | solution.py:84
  3.6 0.0 copy-start
  3.6 8.5 %all-to-all-start = ((bf16[32,2,30,4,128]{4,3,2,1,0:T(4,128)(2,1)}), bf16[32,2,30,4,128]{4,3,2,1,0:T(4,128)(2,1)S(1)}, u32[]{:S(2)}, u32[]{:S(2)}) async-start(bf16[32,2,30,4,128]{4,3,2,1,0:T(4,128)(2,1)} %pack.1), calls=%async_computation | async-start | bytes 3932160 | tf_op jit(solution)/shard_map/all_to_all | solution.py:353
  12.2 0.0 copy-done
  12.2 0.1 reduce
  12.3 0.1 reshape_squeeze.3.lines_ref
  12.4 26.7 %all-to-all-done.got_ref = bf16[32,2,30,4,128]{4,3,2,1,0:T(4,128)(2,1)S(1)} async-done(((bf16[32,2,30,4,128]{4,3,2,1,0:T(4,128)(2,1)}), bf16[32,2,30,4,128]{4,3,2,1,0:T(4,128)(2,1)S(1)}, u32[]{:S(2)}, u32[]{:S(2)}) %all-to-all-start) | async-done | bytes 1966112 | tf_op jit(solution)/shard_map/all_to_all | solution.py:353
  39.2 15.4 %schur_partial.1 = f32[8,192,128]{2,1,0:T(8,128)S(1)} custom-call(bf16[32,2,30,4,128]{4,3,2,1,0:T(4,128)(2,1)S(1)} %all-to-all-done.got_ref), custom_call_target="tpu_custom_call" | custom-call | flops 10000000000 | bytes 3000000 | tf_op jit(solution)/shard_map/schur_partial/pallas_call | solution.py:315
  54.6 0.1 collective-permute-start
  54.7 1.7 %collective-permute-done.came_ref = f32[4,192,128]{2,1,0:T(8,128)S(1)} collective-permute-done((f32[4,192,128]{2,1,0:T(8,128)S(1)}, f32[4,192,128]{2,1,0:T(8,128)S(1)}, u32[]{:S(2)}, u32[]{:S(2)}) %collective-permute-start) | collective-permute-done | bytes 393248 | tf_op jit(solution)/shard_map/ppermute | solution.py:359
  56.4 0.1 to_send.1
  56.5 6.0 %collective-permute-start.1 = (s16[192,128]{1,0:T(8,128)(2,1)S(1)}, s16[192,128]{1,0:T(8,128)(2,1)S(1)}, u32[]{:S(2)}, u32[]{:S(2)}) collective-permute-start(s16[192,128]{1,0:T(8,128)(2,1)S(1)} %get-tuple-element.13), channel_id=1, source_target_pairs={{0,2},{1,35},{2,64},{3,97},{4,6},{5,39},{6,68},{7,101},{8,10},{9,4... | collective-permute-start | bytes 147464 | tf_op jit(solution)/shard_map/ppermute | solution.py:369
  62.5 1.0 %collective-permute-start.2 = (s16[192,128]{1,0:T(8,128)(2,1)S(1)}, s16[192,128]{1,0:T(8,128)(2,1)S(1)}, u32[]{:S(2)}, u32[]{:S(2)}) collective-permute-start(s16[192,128]{1,0:T(8,128)(2,1)S(1)} %get-tuple-element.14), channel_id=1, source_target_pairs={{0,1},{1,32},{2,67},{3,98},{4,5},{5,36},{6,71},{7,102},{8,9},{9,40... | collective-permute-start | bytes 147464 | tf_op jit(solution)/shard_map/ppermute | solution.py:369
  63.5 3.9 %collective-permute-start.3 = (s16[192,128]{1,0:T(8,128)(2,1)S(1)}, s16[192,128]{1,0:T(8,128)(2,1)S(1)}, u32[]{:S(2)}, u32[]{:S(2)}) collective-permute-start(s16[192,128]{1,0:T(8,128)(2,1)S(1)} %get-tuple-element.15), channel_id=1, source_target_pairs={{0,3},{1,34},{2,65},{3,96},{4,7},{5,38},{6,69},{7,100},{8,11},{9,4... | collective-permute-start | bytes 147464 | tf_op jit(solution)/shard_map/ppermute | solution.py:369
  67.3 3.3 %collective-permute-start.4 = (s16[192,128]{1,0:T(8,128)(2,1)S(1)}, s16[192,128]{1,0:T(8,128)(2,1)S(1)}, u32[]{:S(2)}, u32[]{:S(2)}) collective-permute-start(s16[192,128]{1,0:T(8,128)(2,1)S(1)} %get-tuple-element.16), channel_id=1, source_target_pairs={{0,0},{1,33},{2,66},{3,99},{4,4},{5,37},{6,70},{7,103},{8,8},{9,41... | collective-permute-start | bytes 147464 | tf_op jit(solution)/shard_map/ppermute | solution.py:369
  70.7 0.0 collective-permute-done.1.refs_0_
  70.7 0.0 collective-permute-done.2.refs_1_
  70.7 1.1 %collective-permute-done.3.refs_2_ = s16[192,128]{1,0:T(8,128)(2,1)S(1)} collective-permute-done((s16[192,128]{1,0:T(8,128)(2,1)S(1)}, s16[192,128]{1,0:T(8,128)(2,1)S(1)}, u32[]{:S(2)}, u32[]{:S(2)}) %collective-permute-start.3) | collective-permute-done | bytes 49184 | tf_op jit(solution)/shard_map/ppermute | solution.py:369
  71.8 5.9 %collective-permute-done.4.refs_3_ = s16[192,128]{1,0:T(8,128)(2,1)S(1)} collective-permute-done((s16[192,128]{1,0:T(8,128)(2,1)S(1)}, s16[192,128]{1,0:T(8,128)(2,1)S(1)}, u32[]{:S(2)}, u32[]{:S(2)}) %collective-permute-start.4) | collective-permute-done | bytes 49184 | tf_op jit(solution)/shard_map/ppermute | solution.py:369
  77.7 0.8 %finish.1 = f32[54,1,432]{2,1,0:T(1,128)} custom-call(f32[9,432]{1,0:T(8,128)S(1)} %reshape_squeeze.3.lines_ref, s16[192,128]{1,0:T(8,128)(2,1)S(1)} %collective-permute-done.1.refs_0_, s16[192,128]{1,0:T(8,128)(2,1)S(1)} %collective-permute-done.2.refs_1_, s16[192,128]{1,0:T(8,128)(2,1)S(1)} %collective-permute-done.3.refs_2_, ...), custom_call_target="tpu_custom_call" | custom-call | flops 200000 | bytes 500000 | tf_op jit(solution)/shard_map/finish/pallas_call | solution.py:297
  (1 shorter events, 0.0 us)
Async XLA Ops:
  3.6 8.6 %copy-start = (f32[1,9,9,48]{3,0,2,1:T(1,128)S(1)}, f32[1,9,9,48]{3,0,2,1:T(1,128)}, u32[]{:S(2)}) copy-start(f32[1,9,9,48]{3,0,2,1:T(1,128)} %param.13) | copy-start | bytes 46660
  3.6 35.5 %all-to-all-start = ((bf16[32,2,30,4,128]{4,3,2,1,0:T(4,128)(2,1)}), bf16[32,2,30,4,128]{4,3,2,1,0:T(4,128)(2,1)S(1)}, u32[]{:S(2)}, u32[]{:S(2)}) async-start(bf16[32,2,30,4,128]{4,3,2,1,0:T(4,128)(2,1)} %pack.1), calls=%async_computation | async-start | bytes 3932160 | tf_op jit(solution)/shard_map/all_to_all | solution.py:353
  54.6 1.8 %collective-permute-start = (f32[4,192,128]{2,1,0:T(8,128)S(1)}, f32[4,192,128]{2,1,0:T(8,128)S(1)}, u32[]{:S(2)}, u32[]{:S(2)}) collective-permute-start(f32[4,192,128]{2,1,0:T(8,128)S(1)} %dynamic-slice_bitcast_fusion), channel_id=1, source_target_pairs={{0,128},{128,0},{1,129},{129,1},{2,130},{130,2},{3,131},{131,3},{4... | collective-permute-start | bytes 1179656 | tf_op jit(solution)/shard_map/ppermute | solution.py:359
  56.5 14.2 %collective-permute-start.1 = (s16[192,128]{1,0:T(8,128)(2,1)S(1)}, s16[192,128]{1,0:T(8,128)(2,1)S(1)}, u32[]{:S(2)}, u32[]{:S(2)}) collective-permute-start(s16[192,128]{1,0:T(8,128)(2,1)S(1)} %get-tuple-element.13), channel_id=1, source_target_pairs={{0,2},{1,35},{2,64},{3,97},{4,6},{5,39},{6,68},{7,101},{8,10},{9,4... | collective-permute-start | bytes 147464 | tf_op jit(solution)/shard_map/ppermute | solution.py:369
  62.5 8.2 %collective-permute-start.2 = (s16[192,128]{1,0:T(8,128)(2,1)S(1)}, s16[192,128]{1,0:T(8,128)(2,1)S(1)}, u32[]{:S(2)}, u32[]{:S(2)}) collective-permute-start(s16[192,128]{1,0:T(8,128)(2,1)S(1)} %get-tuple-element.14), channel_id=1, source_target_pairs={{0,1},{1,32},{2,67},{3,98},{4,5},{5,36},{6,71},{7,102},{8,9},{9,40... | collective-permute-start | bytes 147464 | tf_op jit(solution)/shard_map/ppermute | solution.py:369
  63.5 8.3 %collective-permute-start.3 = (s16[192,128]{1,0:T(8,128)(2,1)S(1)}, s16[192,128]{1,0:T(8,128)(2,1)S(1)}, u32[]{:S(2)}, u32[]{:S(2)}) collective-permute-start(s16[192,128]{1,0:T(8,128)(2,1)S(1)} %get-tuple-element.15), channel_id=1, source_target_pairs={{0,3},{1,34},{2,65},{3,96},{4,7},{5,38},{6,69},{7,100},{8,11},{9,4... | collective-permute-start | bytes 147464 | tf_op jit(solution)/shard_map/ppermute | solution.py:369
  67.3 10.4 %collective-permute-start.4 = (s16[192,128]{1,0:T(8,128)(2,1)S(1)}, s16[192,128]{1,0:T(8,128)(2,1)S(1)}, u32[]{:S(2)}, u32[]{:S(2)}) collective-permute-start(s16[192,128]{1,0:T(8,128)(2,1)S(1)} %get-tuple-element.16), channel_id=1, source_target_pairs={{0,0},{1,33},{2,66},{3,99},{4,4},{5,37},{6,70},{7,103},{8,8},{9,41... | collective-permute-start | bytes 147464 | tf_op jit(solution)/shard_map/ppermute | solution.py:369

commit v11 on v10

--- a/solution.py
+++ b/solution.py
@@ -261,7 +261,33 @@
     )(ours, came)
 
 
-def finish_kernel(cameras, lines_ref, *refs):
+def own_kernel(cameras, lines_ref, out_ref):
+    share, side = out_ref.shape
+    start = (lax.axis_index("layer") * lax.axis_size("pair") + lax.axis_index("pair")) * share
+    first = start // cameras
+    row = start + lax.broadcasted_iota(jnp.int32, (share, side), 0)
+    column = lax.broadcasted_iota(jnp.int32, (share, side), 1)
+    own = jnp.zeros((share, side), jnp.float32)
+    for step in range(-(-share // cameras) + 1):
+        line = lines_ref[pl.ds(jnp.minimum(first + step, lines_ref.shape[0] - 1), 1), :]
+        own = jnp.where(row // cameras == first + step, jnp.broadcast_to(line, (share, side)), own)
+    out_ref[...] = jnp.where(row % cameras == column % cameras, own, 0.0)
+
+
+def own_blocks(lines, cameras, share):
+    vmem = pl.BlockSpec(memory_space=pltpu.VMEM)
+    return pl.pallas_call(
+        functools.partial(own_kernel, cameras),
+        out_shape=jax.ShapeDtypeStruct((share, lines.shape[1]), jnp.float32),
+        in_specs=[vmem],
+        out_specs=vmem,
+        compiler_params=pltpu.CompilerParams(vmem_limit_bytes=16 * 1024 * 1024),
+        cost_estimate=pl.CostEstimate(flops=200000, bytes_accessed=100000, transcendentals=0),
+        name="own_blocks",
+    )(lines)
+
+
+def finish_kernel(own_ref, *refs):
     pieces, out_ref = refs[:-1], refs[-1]
     share, _, side = out_ref.shape
     width = pieces[0].shape[1]
@@ -271,15 +297,7 @@
         steps = piece[...].astype(jnp.int32).astype(jnp.float32)
         value = steps * jnp.broadcast_to(jnp.exp2(steps[used : used + 1]), steps.shape)
         total = value if total is None else total + value
-    start = (lax.axis_index("layer") * lax.axis_size("pair") + lax.axis_index("pair")) * share
-    first = start // cameras
-    row = start + lax.broadcasted_iota(jnp.int32, (share, side), 0)
-    column = lax.broadcasted_iota(jnp.int32, (share, side), 1)
-    own = jnp.zeros((share, side), jnp.float32)
-    for step in range(-(-share // cameras) + 1):
-        line = lines_ref[pl.ds(jnp.minimum(first + step, lines_ref.shape[0] - 1), 1), :]
-        own = jnp.where(row // cameras == first + step, jnp.broadcast_to(line, (share, side)), own)
-    own = jnp.where(row % cameras == column % cameras, own, 0.0)
+    own = own_ref[...]
     full, half = side // width, share // 2
     rest = side - full * width
     for lane in range(full):
@@ -292,17 +310,18 @@
         )
 
 
-def finish(lines, pieces, cameras, share):
+def finish(own, pieces):
+    share, side = own.shape
     vmem = pl.BlockSpec(memory_space=pltpu.VMEM)
     return pl.pallas_call(
-        functools.partial(finish_kernel, cameras),
-        out_shape=jax.ShapeDtypeStruct((share, 1, lines.shape[1]), jnp.float32),
+        finish_kernel,
+        out_shape=jax.ShapeDtypeStruct((share, 1, side), jnp.float32),
         in_specs=[vmem] * (1 + len(pieces)),
         out_specs=vmem,
         compiler_params=pltpu.CompilerParams(vmem_limit_bytes=16 * 1024 * 1024),
         cost_estimate=pl.CostEstimate(flops=200000, bytes_accessed=500000, transcendentals=0),
         name="finish",
-    )(lines, *pieces)
+    )(own, *pieces)
 
 
 def schur_partial(got, cameras, shares):
@@ -349,9 +368,9 @@
         jac_blocks.transpose(0, 2, 1, 3), point_blocks.transpose(1, 0, 2), visibility, obs_count, tile_count,
         route[:, 0], near * across * pairs, site_of,
     )
-    lines = camera_blocks[0].reshape(9, side)
+    own = own_blocks(camera_blocks[0].reshape(9, side), cameras, side // shares)
     got = lax.all_to_all(packed, ("zb", "x", "pair"), split_axis=0, concat_axis=0, tiled=True)
-    got, lines = lax.optimization_barrier((got, lines))
+    got, own = lax.optimization_barrier((got, own))
     partial_value = schur_partial(got, cameras, shares)
     partial_value = partial_value.reshape((layers, pairs) + partial_value.shape[1:])
     layer = lax.axis_index("layer")
@@ -367,7 +386,7 @@
             c, zp, zb, x, y = source
             links.append((flat(source, sizes), flat((c, (y + zp + 2 * zb) % far, zb, x, y ^ turn), sizes)))
         pieces.append(lax.ppermute(parcels[turn], AXES, links))
-    return finish(lines, pieces, cameras, share).transpose(1, 0, 2)
+    return finish(own, pieces).transpose(1, 0, 2)
 
 
 def bits(size):

time: 78.9 us -> 78.8 us (level)
  no operation moved by 1% of the time
where the time goes in v11:
time: 78.8 us; the launch traced here: 78.5 us
  waiting for transfers between devices  35.4 us (45%)
  starting transfers between devices  22.8 us (29%)
  Pallas kernels  20 us (25%)
    all_to_all x1, waiting for transfers between devices, local(): lax.all_to_all(packed, ('zb', 'x', 'pair'), split_axis=0, concat_axis=0,...  26.7 us
    pallas_call x1, Pallas kernels, schur_partial(): pl.pallas_call(functools.partial(schur_kernel, cameras, pieces), out_shap...  15.4 us
    ppermute x4, starting transfers between devices, local(): pieces.append(lax.ppermute(parcels[turn], AXES, links))  14.2 us
    all_to_all x1, starting transfers between devices, local(): lax.all_to_all(packed, ('zb', 'x', 'pair'), split_axis=0, concat_axis=0,...  8.55 us
    ppermute x4, waiting for transfers between devices, local(): pieces.append(lax.ppermute(parcels[turn], AXES, links))  6.99 us
    pallas_call x1, Pallas kernels, pack(): pl.pallas_call(functools.partial(pack_kernel, site_of), out_shape=jax.Sha...  3.62 us
    ppermute x1, waiting for transfers between devices, local(): came = lax.ppermute(theirs, 'layer', [(0, 1), (1, 0)])  1.71 us
  transfers between devices with their start and end apart: 6, of which 4 were waited for; matrix products, arithmetic and copies ran while one was open for 0% of the time, Pallas kernels for 0%

profile of v11, /device:TPU:34, one launch (start us, length us, event | category | flops | bytes accessed | tf_op | source)
XLA Modules:
  0.0 78.5 jit_solution(6258713861131341247)
XLA Ops:
  0.0 3.6 %pack.1 = bf16[32,2,30,4,128]{4,3,2,1,0:T(4,128)(2,1)} custom-call(s32[32]{0:T(128)} %bitcast.11, s32[32]{0:T(128)} %count_hbm.1, bf16[32,27,4,128]{3,2,1,0:T(4,128)(2,1)} %bitcast.9, bf16[6,32,128]{2,1,0:T(8,128)(2,1)} %bitcast.10, s32[32,4,128]{2,1,0:T(4,128)} %vis_hbm.1, s32[32,128]{1,0:T(8,128)} %obs_hbm.1), custom_call_target="tpu_custom_call" | custom-call | flops 1000000 | bytes 3000000 | tf_op jit(solution)/shard_map/pack/pallas_call | solution.py:84
  3.6 0.0 copy-start
  3.6 8.5 %all-to-all-start = ((bf16[32,2,30,4,128]{4,3,2,1,0:T(4,128)(2,1)}), bf16[32,2,30,4,128]{4,3,2,1,0:T(4,128)(2,1)S(1)}, u32[]{:S(2)}, u32[]{:S(2)}) async-start(bf16[32,2,30,4,128]{4,3,2,1,0:T(4,128)(2,1)} %pack.1), calls=%async_computation | async-start | bytes 3932160 | tf_op jit(solution)/shard_map/all_to_all | solution.py:372
  12.2 0.0 copy-done
  12.2 0.1 reduce
  12.3 0.1 reshape_squeeze.3.lines_ref
  12.4 0.1 own_blocks.1.own_ref
  12.5 26.7 %all-to-all-done.got_ref = bf16[32,2,30,4,128]{4,3,2,1,0:T(4,128)(2,1)S(1)} async-done(((bf16[32,2,30,4,128]{4,3,2,1,0:T(4,128)(2,1)}), bf16[32,2,30,4,128]{4,3,2,1,0:T(4,128)(2,1)S(1)}, u32[]{:S(2)}, u32[]{:S(2)}) %all-to-all-start) | async-done | bytes 1966112 | tf_op jit(solution)/shard_map/all_to_all | solution.py:372
  39.2 15.4 %schur_partial.1 = f32[8,192,128]{2,1,0:T(8,128)S(1)} custom-call(bf16[32,2,30,4,128]{4,3,2,1,0:T(4,128)(2,1)S(1)} %all-to-all-done.got_ref), custom_call_target="tpu_custom_call" | custom-call | flops 10000000000 | bytes 3000000 | tf_op jit(solution)/shard_map/schur_partial/pallas_call | solution.py:334
  54.6 0.1 collective-permute-start
  54.7 1.7 %collective-permute-done.came_ref = f32[4,192,128]{2,1,0:T(8,128)S(1)} collective-permute-done((f32[4,192,128]{2,1,0:T(8,128)S(1)}, f32[4,192,128]{2,1,0:T(8,128)S(1)}, u32[]{:S(2)}, u32[]{:S(2)}) %collective-permute-start) | collective-permute-done | bytes 393248 | tf_op jit(solution)/shard_map/ppermute | solution.py:378
  56.4 0.1 to_send.1
  56.5 6.0 %collective-permute-start.1 = (s16[192,128]{1,0:T(8,128)(2,1)S(1)}, s16[192,128]{1,0:T(8,128)(2,1)S(1)}, u32[]{:S(2)}, u32[]{:S(2)}) collective-permute-start(s16[192,128]{1,0:T(8,128)(2,1)S(1)} %get-tuple-element.13), channel_id=1, source_target_pairs={{0,2},{1,35},{2,64},{3,97},{4,6},{5,39},{6,68},{7,101},{8,10},{9,4... | collective-permute-start | bytes 147464 | tf_op jit(solution)/shard_map/ppermute | solution.py:388
  62.5 1.0 %collective-permute-start.2 = (s16[192,128]{1,0:T(8,128)(2,1)S(1)}, s16[192,128]{1,0:T(8,128)(2,1)S(1)}, u32[]{:S(2)}, u32[]{:S(2)}) collective-permute-start(s16[192,128]{1,0:T(8,128)(2,1)S(1)} %get-tuple-element.14), channel_id=1, source_target_pairs={{0,1},{1,32},{2,67},{3,98},{4,5},{5,36},{6,71},{7,102},{8,9},{9,40... | collective-permute-start | bytes 147464 | tf_op jit(solution)/shard_map/ppermute | solution.py:388
  63.5 3.9 %collective-permute-start.3 = (s16[192,128]{1,0:T(8,128)(2,1)S(1)}, s16[192,128]{1,0:T(8,128)(2,1)S(1)}, u32[]{:S(2)}, u32[]{:S(2)}) collective-permute-start(s16[192,128]{1,0:T(8,128)(2,1)S(1)} %get-tuple-element.15), channel_id=1, source_target_pairs={{0,3},{1,34},{2,65},{3,96},{4,7},{5,38},{6,69},{7,100},{8,11},{9,4... | collective-permute-start | bytes 147464 | tf_op jit(solution)/shard_map/ppermute | solution.py:388
  67.3 3.3 %collective-permute-start.4 = (s16[192,128]{1,0:T(8,128)(2,1)S(1)}, s16[192,128]{1,0:T(8,128)(2,1)S(1)}, u32[]{:S(2)}, u32[]{:S(2)}) collective-permute-start(s16[192,128]{1,0:T(8,128)(2,1)S(1)} %get-tuple-element.16), channel_id=1, source_target_pairs={{0,0},{1,33},{2,66},{3,99},{4,4},{5,37},{6,70},{7,103},{8,8},{9,41... | collective-permute-start | bytes 147464 | tf_op jit(solution)/shard_map/ppermute | solution.py:388
  70.7 0.0 collective-permute-done.1.refs_0_
  70.7 0.0 collective-permute-done.2.refs_1_
  70.7 1.1 %collective-permute-done.3.refs_2_ = s16[192,128]{1,0:T(8,128)(2,1)S(1)} collective-permute-done((s16[192,128]{1,0:T(8,128)(2,1)S(1)}, s16[192,128]{1,0:T(8,128)(2,1)S(1)}, u32[]{:S(2)}, u32[]{:S(2)}) %collective-permute-start.3) | collective-permute-done | bytes 49184 | tf_op jit(solution)/shard_map/ppermute | solution.py:388
  71.8 5.9 %collective-permute-done.4.refs_3_ = s16[192,128]{1,0:T(8,128)(2,1)S(1)} collective-permute-done((s16[192,128]{1,0:T(8,128)(2,1)S(1)}, s16[192,128]{1,0:T(8,128)(2,1)S(1)}, u32[]{:S(2)}, u32[]{:S(2)}) %collective-permute-start.4) | collective-permute-done | bytes 49184 | tf_op jit(solution)/shard_map/ppermute | solution.py:388
  77.7 0.8 finish.1
  (1 shorter events, 0.0 us)
Async XLA Ops:
  3.6 8.6 %copy-start = (f32[1,9,9,48]{3,0,2,1:T(1,128)S(1)}, f32[1,9,9,48]{3,0,2,1:T(1,128)}, u32[]{:S(2)}) copy-start(f32[1,9,9,48]{3,0,2,1:T(1,128)} %param.13) | copy-start | bytes 46660
  3.6 35.5 %all-to-all-start = ((bf16[32,2,30,4,128]{4,3,2,1,0:T(4,128)(2,1)}), bf16[32,2,30,4,128]{4,3,2,1,0:T(4,128)(2,1)S(1)}, u32[]{:S(2)}, u32[]{:S(2)}) async-start(bf16[32,2,30,4,128]{4,3,2,1,0:T(4,128)(2,1)} %pack.1), calls=%async_computation | async-start | bytes 3932160 | tf_op jit(solution)/shard_map/all_to_all | solution.py:372
  54.6 1.8 %collective-permute-start = (f32[4,192,128]{2,1,0:T(8,128)S(1)}, f32[4,192,128]{2,1,0:T(8,128)S(1)}, u32[]{:S(2)}, u32[]{:S(2)}) collective-permute-start(f32[4,192,128]{2,1,0:T(8,128)S(1)} %dynamic-slice_bitcast_fusion), channel_id=1, source_target_pairs={{0,128},{128,0},{1,129},{129,1},{2,130},{130,2},{3,131},{131,3},{4... | collective-permute-start | bytes 1179656 | tf_op jit(solution)/shard_map/ppermute | solution.py:378
  56.5 14.2 %collective-permute-start.1 = (s16[192,128]{1,0:T(8,128)(2,1)S(1)}, s16[192,128]{1,0:T(8,128)(2,1)S(1)}, u32[]{:S(2)}, u32[]{:S(2)}) collective-permute-start(s16[192,128]{1,0:T(8,128)(2,1)S(1)} %get-tuple-element.13), channel_id=1, source_target_pairs={{0,2},{1,35},{2,64},{3,97},{4,6},{5,39},{6,68},{7,101},{8,10},{9,4... | collective-permute-start | bytes 147464 | tf_op jit(solution)/shard_map/ppermute | solution.py:388
  62.5 8.2 %collective-permute-start.2 = (s16[192,128]{1,0:T(8,128)(2,1)S(1)}, s16[192,128]{1,0:T(8,128)(2,1)S(1)}, u32[]{:S(2)}, u32[]{:S(2)}) collective-permute-start(s16[192,128]{1,0:T(8,128)(2,1)S(1)} %get-tuple-element.14), channel_id=1, source_target_pairs={{0,1},{1,32},{2,67},{3,98},{4,5},{5,36},{6,71},{7,102},{8,9},{9,40... | collective-permute-start | bytes 147464 | tf_op jit(solution)/shard_map/ppermute | solution.py:388
  63.5 8.3 %collective-permute-start.3 = (s16[192,128]{1,0:T(8,128)(2,1)S(1)}, s16[192,128]{1,0:T(8,128)(2,1)S(1)}, u32[]{:S(2)}, u32[]{:S(2)}) collective-permute-start(s16[192,128]{1,0:T(8,128)(2,1)S(1)} %get-tuple-element.15), channel_id=1, source_target_pairs={{0,3},{1,34},{2,65},{3,96},{4,7},{5,38},{6,69},{7,100},{8,11},{9,4... | collective-permute-start | bytes 147464 | tf_op jit(solution)/shard_map/ppermute | solution.py:388
  67.3 10.4 %collective-permute-start.4 = (s16[192,128]{1,0:T(8,128)(2,1)S(1)}, s16[192,128]{1,0:T(8,128)(2,1)S(1)}, u32[]{:S(2)}, u32[]{:S(2)}) collective-permute-start(s16[192,128]{1,0:T(8,128)(2,1)S(1)} %get-tuple-element.16), channel_id=1, source_target_pairs={{0,0},{1,33},{2,66},{3,99},{4,4},{5,37},{6,70},{7,103},{8,8},{9,41... | collective-permute-start | bytes 147464 | tf_op jit(solution)/shard_map/ppermute | solution.py:388

commit v12 on v11

--- a/solution.py
+++ b/solution.py
@@ -380,7 +380,7 @@
     width = partial_value.shape[3]
     parcels = to_send(partial_value, came, side // width * share + share // 2)
     pieces = []
-    for turn in sorted(range(far), key=lambda turn: -min(turn, pairs - turn)):
+    for turn in sorted(range(far), key=lambda turn: (turn % 2, -turn)):
         links = []
         for source in itertools.product(*(range(size) for size in sizes)):
             c, zp, zb, x, y = source

time: 78.8 us -> 79 us (level)
  the two profiles are of different devices: /device:TPU:34 before, /device:TPU:40 now
where the time goes in v12:
time: 79 us; the launch traced here: 78.6 us
  waiting for transfers between devices  32.8 us (42%)
  starting transfers between devices  25.5 us (32%)
  Pallas kernels  20 us (25%)
    all_to_all x1, waiting for transfers between devices, local(): lax.all_to_all(packed, ('zb', 'x', 'pair'), split_axis=0, concat_axis=0,...  24.3 us
    ppermute x4, starting transfers between devices, local(): pieces.append(lax.ppermute(parcels[turn], AXES, links))  16.9 us
    pallas_call x1, Pallas kernels, schur_partial(): pl.pallas_call(functools.partial(schur_kernel, cameras, pieces), out_shap...  15.4 us
    all_to_all x1, starting transfers between devices, local(): lax.all_to_all(packed, ('zb', 'x', 'pair'), split_axis=0, concat_axis=0,...  8.45 us
    ppermute x4, waiting for transfers between devices, local(): pieces.append(lax.ppermute(parcels[turn], AXES, links))  6.75 us
    pallas_call x1, Pallas kernels, pack(): pl.pallas_call(functools.partial(pack_kernel, site_of), out_shape=jax.Sha...  3.62 us
    ppermute x1, waiting for transfers between devices, local(): came = lax.ppermute(theirs, 'layer', [(0, 1), (1, 0)])  1.71 us
  transfers between devices with their start and end apart: 6, of which 3 were waited for; matrix products, arithmetic and copies ran while one was open for 0% of the time, Pallas kernels for 0%

profile of v12, /device:TPU:40, one launch (start us, length us, event | category | flops | bytes accessed | tf_op | source)
XLA Modules:
  0.0 78.6 jit_solution(1818708103398254557)
XLA Ops:
  0.0 3.6 %pack.1 = bf16[32,2,30,4,128]{4,3,2,1,0:T(4,128)(2,1)} custom-call(s32[32]{0:T(128)} %bitcast.11, s32[32]{0:T(128)} %count_hbm.1, bf16[32,27,4,128]{3,2,1,0:T(4,128)(2,1)} %bitcast.9, bf16[6,32,128]{2,1,0:T(8,128)(2,1)} %bitcast.10, s32[32,4,128]{2,1,0:T(4,128)} %vis_hbm.1, s32[32,128]{1,0:T(8,128)} %obs_hbm.1), custom_call_target="tpu_custom_call" | custom-call | flops 1000000 | bytes 3000000 | tf_op jit(solution)/shard_map/pack/pallas_call | solution.py:84
  3.6 0.0 copy-start
  3.6 8.5 %all-to-all-start = ((bf16[32,2,30,4,128]{4,3,2,1,0:T(4,128)(2,1)}), bf16[32,2,30,4,128]{4,3,2,1,0:T(4,128)(2,1)S(1)}, u32[]{:S(2)}, u32[]{:S(2)}) async-start(bf16[32,2,30,4,128]{4,3,2,1,0:T(4,128)(2,1)} %pack.1), calls=%async_computation | async-start | bytes 3932160 | tf_op jit(solution)/shard_map/all_to_all | solution.py:372
  12.1 0.0 copy-done
  12.1 0.1 reduce
  12.2 0.1 reshape_squeeze.3.lines_ref
  12.3 0.1 own_blocks.1.own_ref
  12.4 24.3 %all-to-all-done.got_ref = bf16[32,2,30,4,128]{4,3,2,1,0:T(4,128)(2,1)S(1)} async-done(((bf16[32,2,30,4,128]{4,3,2,1,0:T(4,128)(2,1)}), bf16[32,2,30,4,128]{4,3,2,1,0:T(4,128)(2,1)S(1)}, u32[]{:S(2)}, u32[]{:S(2)}) %all-to-all-start) | async-done | bytes 1966112 | tf_op jit(solution)/shard_map/all_to_all | solution.py:372
  36.7 15.4 %schur_partial.1 = f32[8,192,128]{2,1,0:T(8,128)S(1)} custom-call(bf16[32,2,30,4,128]{4,3,2,1,0:T(4,128)(2,1)S(1)} %all-to-all-done.got_ref), custom_call_target="tpu_custom_call" | custom-call | flops 10000000000 | bytes 3000000 | tf_op jit(solution)/shard_map/schur_partial/pallas_call | solution.py:334
  52.2 0.1 collective-permute-start
  52.3 1.7 %collective-permute-done.came_ref = f32[4,192,128]{2,1,0:T(8,128)S(1)} collective-permute-done((f32[4,192,128]{2,1,0:T(8,128)S(1)}, f32[4,192,128]{2,1,0:T(8,128)S(1)}, u32[]{:S(2)}, u32[]{:S(2)}) %collective-permute-start) | collective-permute-done | bytes 393248 | tf_op jit(solution)/shard_map/ppermute | solution.py:378
  54.0 0.1 to_send.1
  54.1 6.7 %collective-permute-start.1 = (s16[192,128]{1,0:T(8,128)(2,1)S(1)}, s16[192,128]{1,0:T(8,128)(2,1)S(1)}, u32[]{:S(2)}, u32[]{:S(2)}) collective-permute-start(s16[192,128]{1,0:T(8,128)(2,1)S(1)} %get-tuple-element.13), channel_id=1, source_target_pairs={{0,2},{1,35},{2,64},{3,97},{4,6},{5,39},{6,68},{7,101},{8,10},{9,4... | collective-permute-start | bytes 147464 | tf_op jit(solution)/shard_map/ppermute | solution.py:388
  60.8 3.3 %collective-permute-start.2 = (s16[192,128]{1,0:T(8,128)(2,1)S(1)}, s16[192,128]{1,0:T(8,128)(2,1)S(1)}, u32[]{:S(2)}, u32[]{:S(2)}) collective-permute-start(s16[192,128]{1,0:T(8,128)(2,1)S(1)} %get-tuple-element.14), channel_id=1, source_target_pairs={{0,0},{1,33},{2,66},{3,99},{4,4},{5,37},{6,70},{7,103},{8,8},{9,41... | collective-permute-start | bytes 147464 | tf_op jit(solution)/shard_map/ppermute | solution.py:388
  64.1 0.1 collective-permute-start.3
  64.2 6.8 %collective-permute-start.4 = (s16[192,128]{1,0:T(8,128)(2,1)S(1)}, s16[192,128]{1,0:T(8,128)(2,1)S(1)}, u32[]{:S(2)}, u32[]{:S(2)}) collective-permute-start(s16[192,128]{1,0:T(8,128)(2,1)S(1)} %get-tuple-element.16), channel_id=1, source_target_pairs={{0,1},{1,32},{2,67},{3,98},{4,5},{5,36},{6,71},{7,102},{8,9},{9,40... | collective-permute-start | bytes 147464 | tf_op jit(solution)/shard_map/ppermute | solution.py:388
  71.1 0.0 collective-permute-done.1.refs_0_
  71.1 0.0 collective-permute-done.2.refs_1_
  71.1 0.0 collective-permute-done.3.refs_2_
  71.1 6.7 %collective-permute-done.4.refs_3_ = s16[192,128]{1,0:T(8,128)(2,1)S(1)} collective-permute-done((s16[192,128]{1,0:T(8,128)(2,1)S(1)}, s16[192,128]{1,0:T(8,128)(2,1)S(1)}, u32[]{:S(2)}, u32[]{:S(2)}) %collective-permute-start.4) | collective-permute-done | bytes 49184 | tf_op jit(solution)/shard_map/ppermute | solution.py:388
  77.8 0.8 finish.1
  (1 shorter events, 0.0 us)
Async XLA Ops:
  3.6 8.5 %copy-start = (f32[1,9,9,48]{3,0,2,1:T(1,128)S(1)}, f32[1,9,9,48]{3,0,2,1:T(1,128)}, u32[]{:S(2)}) copy-start(f32[1,9,9,48]{3,0,2,1:T(1,128)} %param.13) | copy-start | bytes 46660
  3.6 33.1 %all-to-all-start = ((bf16[32,2,30,4,128]{4,3,2,1,0:T(4,128)(2,1)}), bf16[32,2,30,4,128]{4,3,2,1,0:T(4,128)(2,1)S(1)}, u32[]{:S(2)}, u32[]{:S(2)}) async-start(bf16[32,2,30,4,128]{4,3,2,1,0:T(4,128)(2,1)} %pack.1), calls=%async_computation | async-start | bytes 3932160 | tf_op jit(solution)/shard_map/all_to_all | solution.py:372
  52.2 1.8 %collective-permute-start = (f32[4,192,128]{2,1,0:T(8,128)S(1)}, f32[4,192,128]{2,1,0:T(8,128)S(1)}, u32[]{:S(2)}, u32[]{:S(2)}) collective-permute-start(f32[4,192,128]{2,1,0:T(8,128)S(1)} %dynamic-slice_bitcast_fusion), channel_id=1, source_target_pairs={{0,128},{128,0},{1,129},{129,1},{2,130},{130,2},{3,131},{131,3},{4... | collective-permute-start | bytes 1179656 | tf_op jit(solution)/shard_map/ppermute | solution.py:378
  54.1 17.0 %collective-permute-start.1 = (s16[192,128]{1,0:T(8,128)(2,1)S(1)}, s16[192,128]{1,0:T(8,128)(2,1)S(1)}, u32[]{:S(2)}, u32[]{:S(2)}) collective-permute-start(s16[192,128]{1,0:T(8,128)(2,1)S(1)} %get-tuple-element.13), channel_id=1, source_target_pairs={{0,2},{1,35},{2,64},{3,97},{4,6},{5,39},{6,68},{7,101},{8,10},{9,4... | collective-permute-start | bytes 147464 | tf_op jit(solution)/shard_map/ppermute | solution.py:388
  60.8 10.3 %collective-permute-start.2 = (s16[192,128]{1,0:T(8,128)(2,1)S(1)}, s16[192,128]{1,0:T(8,128)(2,1)S(1)}, u32[]{:S(2)}, u32[]{:S(2)}) collective-permute-start(s16[192,128]{1,0:T(8,128)(2,1)S(1)} %get-tuple-element.14), channel_id=1, source_target_pairs={{0,0},{1,33},{2,66},{3,99},{4,4},{5,37},{6,70},{7,103},{8,8},{9,41... | collective-permute-start | bytes 147464 | tf_op jit(solution)/shard_map/ppermute | solution.py:388
  64.1 6.9 %collective-permute-start.3 = (s16[192,128]{1,0:T(8,128)(2,1)S(1)}, s16[192,128]{1,0:T(8,128)(2,1)S(1)}, u32[]{:S(2)}, u32[]{:S(2)}) collective-permute-start(s16[192,128]{1,0:T(8,128)(2,1)S(1)} %get-tuple-element.15), channel_id=1, source_target_pairs={{0,3},{1,34},{2,65},{3,96},{4,7},{5,38},{6,69},{7,100},{8,11},{9,4... | collective-permute-start | bytes 147464 | tf_op jit(solution)/shard_map/ppermute | solution.py:388
  64.2 13.6 %collective-permute-start.4 = (s16[192,128]{1,0:T(8,128)(2,1)S(1)}, s16[192,128]{1,0:T(8,128)(2,1)S(1)}, u32[]{:S(2)}, u32[]{:S(2)}) collective-permute-start(s16[192,128]{1,0:T(8,128)(2,1)S(1)} %get-tuple-element.16), channel_id=1, source_target_pairs={{0,1},{1,32},{2,67},{3,98},{4,5},{5,36},{6,71},{7,102},{8,9},{9,40... | collective-permute-start | bytes 147464 | tf_op jit(solution)/shard_map/ppermute | solution.py:388
